TPU v7x, 32 devices: a whole 2x2x4 slice. The times are simulated.
32 devices in a mesh: slab: 2 (over y), orb: 16 (over z, x, core).
Axes of the slice: x: 2, y: 2, z: 4, core: 2. Of those that a mesh axis runs over, the one named last changes fastest.
Arguments:
- orbitals_t: bfloat16 [2048, 16384], P('orb', 'slab'), may hold values from -6 to 6
- tiles: bfloat16 [224, 128, 128], P('slab'), may hold values from -0.375 to 0.375
- tile_rows: int32 [224], P('slab'), may hold values from 0 to 63
- tile_cols: int32 [224], P('slab'), may hold values from -2 to 65, as said below
- row_counts: int32 [128], P('slab'), may hold values from 1 to 128, 12288 in all
- bounds: float32 [3], replicated, may hold values from 0 to 1
- rotation: bfloat16 [2048, 2048], P('orb'), may hold values from -0.125 to 0.125
Outputs:
- rotated_t: bfloat16 [2048, 16384], P('orb', 'slab')
Inputs may be any that keep to these rules, and one draw needn't show every extreme that they name: `tile_cols`: within every slab, the first 64 tiles are the diagonal tiles of row blocks 0 to 63 in order; a tile's column block lies within 2 blocks of its row block; in every slab some tile of row block 0 has column block -2 and some tile of row block 63 has column block 65.
All inputs are finite; a program needn't handle non-finite values. No bound on the sum of `row_counts` on one device may be relied on, other than what follows from the above.
Results may differ from a plain program's by a relative error of at most 0.006.
Values may be sent and summed in bfloat16 or wider, within the bound.
No kernel may reach another device: no remote copies, remote signals or barrier semaphores. Data moves between devices by JAX's collectives and lax.ppermute only.
A program may use at most 64 MiB of HBM per device.

v0:
```python
import jax
import jax.numpy as jnp
from jax import lax
from jax.sharding import PartitionSpec as P

HB = 2


def with_halo(block, sides, width):
    for axis, dim in sides:
        count = lax.axis_size(axis)
        forward = [(i, i + 1) for i in range(count - 1)]
        backward = [(target, source) for source, target in forward]
        low = lax.ppermute(
            lax.slice_in_dim(block, block.shape[dim] - width, None, axis=dim), axis, forward
        )
        high = lax.ppermute(lax.slice_in_dim(block, 0, width, axis=dim), axis, backward)
        block = jnp.concatenate([low, block, high], axis=dim)
    return block


def local(orbitals_t, tiles, tile_rows, tile_cols, row_counts, bounds, rotation):
    norb_dev, rows_dev = orbitals_t.shape
    tile_size = tiles.shape[1]
    blocks = rows_dev // tile_size
    lower_bound = -3.0 + bounds[0]
    cutoff = bounds[1] - 0.5
    upper_bound = 3.0 + bounds[2]
    half_width = (upper_bound - cutoff) / 2.0
    center = (upper_bound + cutoff) / 2.0
    sigma_one = half_width / (lower_bound - center)
    sigma_two = 1.0 / (2.0 / sigma_one - sigma_one)
    live = (
        (lax.broadcasted_iota(jnp.int32, (blocks, tile_size), 1) < row_counts[:, None])
        .astype(jnp.float32)
        .reshape(rows_dev)
    )
    extra_rows = tile_rows[blocks:]
    onehot = (extra_rows[:, None] == lax.broadcasted_iota(jnp.int32, (1, blocks), 1)).astype(
        jnp.float32
    )
    col_index = tile_cols + HB

    def apply_tiles(source):
        extended = with_halo(source, (("slab", 1),), HB * tile_size)
        col_blocks = extended.reshape(norb_dev, blocks + 2 * HB, tile_size)
        picked = jnp.take(col_blocks, col_index, axis=1)
        products = jnp.einsum("otc,trc->otr", picked, tiles, preferred_element_type=jnp.float32)
        diagonal_part = products[:, :blocks]
        extra_part = jnp.einsum(
            "otr,tb->obr", products[:, blocks:], onehot, precision=lax.Precision.HIGH
        )
        summed = diagonal_part + extra_part
        return summed.reshape(norb_dev, rows_dev)

    source = orbitals_t.astype(jnp.float32)
    applied = apply_tiles(orbitals_t)
    filtered_one = (live * (applied - center * source) * (sigma_one / half_width)).astype(
        jnp.bfloat16
    )
    applied = apply_tiles(filtered_one)
    first = filtered_one.astype(jnp.float32)
    filtered_two = (
        live
        * (
            (applied - center * first) * (2.0 * sigma_two / half_width)
            - sigma_one * sigma_two * source
        )
    ).astype(jnp.bfloat16)
    row_major = lax.all_to_all(filtered_two, "orb", split_axis=1, concat_axis=0, tiled=True)
    rotated = jnp.einsum(
        "kj,kr->jr",
        lax.all_gather(rotation, "orb", axis=0, tiled=True),
        row_major,
        preferred_element_type=jnp.float32,
    ).astype(jnp.bfloat16)
    return lax.all_to_all(rotated, "orb", split_axis=0, concat_axis=1, tiled=True)


def solution(mesh):
    return jax.shard_map(
        local,
        mesh=mesh,
        in_specs=(
            P("orb", "slab"),
            P("slab", None, None),
            P("slab"),
            P("slab"),
            P("slab"),
            P(),
            P("orb", None),
        ),
        out_specs=P("orb", "slab"),
        check_vma=False,
    )
```

profile of v0, /device:TPU:0, one launch (start us, length us, event | category | flops | bytes accessed | tf_op | source)
XLA Modules:
  0.0 256.7 jit_solution(14594037841716951941)
XLA Ops:
  7.3 3.2 %copy.27 = bf16[128,8192]{0,1:T(8,128)(2,1)S(1)} copy(bf16[128,8192]{1,0:T(8,128)(2,1)} %param.9) | data formatting | bytes 4194304 | tf_op args[0]
  10.5 4.9 %collective-permute-start = (bf16[128,256]{0,1:T(8,128)(2,1)S(1)}, bf16[128,256]{0,1:T(8,128)(2,1)S(1)}, u32[]{:S(2)}, u32[]{:S(2)}) collective-permute-start(bf16[128,256]{0,1:T(8,128)(2,1)S(1)} %get-tuple-element.10), channel_id=1, source_target_pairs={{0,16},{1,17},{2,18},{3,19},{4,20},{5,21},{6,22},{7,23},{8,24},{9,... | collective-permute-start | bytes 196616 | tf_op jit(solution)/shard_map/ppermute | solution.py:14
  19.4 2.1 collective-permute-done.1
  21.6 5.8 %pad_maximum_fusion = bf16[128,8704]{0,1:T(8,128)(2,1)} fusion(bf16[128,256]{0,1:T(8,128)(2,1)S(1)} %collective-permute-done.1, bf16[128,8192]{0,1:T(8,128)(2,1)S(1)} %copy.27, bf16[128,256]{0,1:T(8,128)(2,1)S(1)} %collective-permute-done), kind=kLoop, calls=%fused_computation.26 | loop fusion | flops 6684672 | bytes 4456448 | tf_op jit(solution)/shard_map/concatenate | solution.py:18
  27.4 4.2 %copy.30 = bf16[128,68,128]{2,0,1:T(8,128)(2,1)} copy(bf16[128,68,128]{0,2,1:T(8,128)(2,1)} %bitcast.56) | data formatting | bytes 4456448 | tf_op jit(solution)/shard_map/reshape | solution.py:46
  31.5 4.5 %gather_fusion = bf16[112,128,128]{2,1,0:T(8,128)(2,1)} fusion(bf16[128,68,128]{2,0,1:T(8,128)(2,1)} %copy.30, s32[1024]{0:T(1024)S(1)} %pad_clamp_fusion), kind=kCustom, calls=%fused_computation.clone | custom fusion | bytes 7340480 | tf_op jit(solution)/shard_map/jit(_take)/gather | solution.py:47
  36.1 5.9 %fusion.16 = f32[128,112,128]{0,2,1:T(8,128)S(1)} fusion(bf16[112,128,128]{2,1,0:T(8,128)(2,1)} %param.10, bf16[112,128,128]{2,1,0:T(8,128)(2,1)} %gather_fusion, pred[112]{0:T(512)(128)(4,1)S(1)} %get-tuple-element.6), kind=kOutput, calls=%fused_computation.24 | convolution fusion | flops 471597056 | bytes 14680176 | tf_op jit(solution)/shard_map/otc,trc->otr/dot_general | solution.py:48
  42.0 3.0 %copy-done.1 = f32[128,112,128]{0,2,1:T(8,128)} copy-done((f32[128,112,128]{0,2,1:T(8,128)}, f32[128,112,128]{0,2,1:T(8,128)S(1)}, u32[]{:S(2)}) %copy-start.1) | copy-done | bytes 7340056
  45.0 2.2 slice.55
  47.2 3.6 %copy.31 = f32[128,48,128]{2,1,0:T(8,128)} copy(f32[128,48,128]{0,2,1:T(8,128)} %slice.55) | data formatting | bytes 6291456 | tf_op jit(solution)/shard_map/slice | solution.py:51
  50.8 5.3 %fusion.28 = f32[64,128,128]{2,0,1:T(8,128)} fusion(f32[128,48,128]{2,1,0:T(8,128)} %copy.31, s32[48]{0:T(128)S(1)} %slice.39), kind=kOutput, calls=%fused_computation.37 | convolution fusion | flops 301992960 | bytes 7340224 | tf_op jit(solution)/shard_map/otr,tb->obr/dot_general | solution.py:50
  56.1 5.4 %copy.32 = f32[64,128,128]{1,2,0:T(8,128)} copy(f32[64,128,128]{2,0,1:T(8,128)} %fusion.28) | data formatting | bytes 8388608 | tf_op jit(solution)/shard_map/otr,tb->obr/dot_general | solution.py:50
  61.5 4.2 %slice_add_fusion.1 = f32[128,64,128]{0,2,1:T(8,128)S(1)} fusion(f32[128,112,128]{0,2,1:T(8,128)} %copy-done.1, f32[64,128,128]{1,2,0:T(8,128)} %copy.32), kind=kLoop, calls=%fused_computation.12 | loop fusion | flops 1048576 | bytes 12582912 | tf_op jit(solution)/shard_map/add | solution.py:53
  65.7 3.5 %fusion.3 = bf16[128,8192]{0,1:T(8,128)(2,1)S(1)} fusion(bf16[128,8192]{0,1:T(8,128)(2,1)S(1)} %copy.27, f32[128,64,128]{0,2,1:T(8,128)S(1)} %slice_add_fusion.1, f32[]{:T(128)S(6)} %div.29, f32[]{:T(128)} %bitcast.7, f32[8192]{0:T(1024)S(1)} %convert_bitcast_fusion), kind=kLoop, calls=%fused_computation.7 | loop fusion | flops 6291456 | bytes 8421384 | tf_op jit(solution)/shard_map/convert_element_type | solution.py:58
  70.6 2.7 %collective-permute-start.2 = (bf16[128,256]{0,1:T(8,128)(2,1)S(1)}, bf16[128,256]{0,1:T(8,128)(2,1)S(1)}, u32[]{:S(2)}, u32[]{:S(2)}) collective-permute-start(bf16[128,256]{0,1:T(8,128)(2,1)S(1)} %get-tuple-element.8), channel_id=1, source_target_pairs={{0,16},{1,17},{2,18},{3,19},{4,20},{5,21},{6,22},{7,23},{8,24},{9,... | collective-permute-start | bytes 196616 | tf_op jit(solution)/shard_map/ppermute | solution.py:14
  75.2 4.3 %collective-permute-done.3 = bf16[128,256]{0,1:T(8,128)(2,1)S(1)} collective-permute-done((bf16[128,256]{0,1:T(8,128)(2,1)S(1)}, bf16[128,256]{0,1:T(8,128)(2,1)S(1)}, u32[]{:S(2)}, u32[]{:S(2)}) %collective-permute-start.3) | collective-permute-done | bytes 65568 | tf_op jit(solution)/shard_map/ppermute | solution.py:17
  79.4 6.6 %pad_maximum_fusion.1 = bf16[128,8704]{0,1:T(8,128)(2,1)} fusion(bf16[128,256]{0,1:T(8,128)(2,1)S(1)} %collective-permute-done.3, bf16[128,8192]{0,1:T(8,128)(2,1)} %copy-done.2, bf16[128,256]{0,1:T(8,128)(2,1)S(1)} %collective-permute-done.2), kind=kLoop, calls=%fused_computation.27 | loop fusion | flops 6684672 | bytes 4456448 | tf_op jit(solution)/shard_map/concatenate | solution.py:18
  86.1 4.2 %copy.34 = bf16[128,68,128]{2,0,1:T(8,128)(2,1)} copy(bf16[128,68,128]{0,2,1:T(8,128)(2,1)} %bitcast.57) | data formatting | bytes 4456448 | tf_op jit(solution)/shard_map/reshape | solution.py:46
  90.3 4.5 %gather_fusion.1 = bf16[112,128,128]{2,1,0:T(8,128)(2,1)} fusion(bf16[128,68,128]{2,0,1:T(8,128)(2,1)} %copy.34, s32[1024]{0:T(1024)S(1)} %pad_clamp_fusion), kind=kCustom, calls=%fused_computation.1.clone | custom fusion | bytes 7340480 | tf_op jit(solution)/shard_map/jit(_take)/gather | solution.py:47
  94.8 5.9 %fusion.19 = f32[128,112,128]{0,2,1:T(8,128)S(1)} fusion(bf16[112,128,128]{2,1,0:T(8,128)(2,1)} %param.10, bf16[112,128,128]{2,1,0:T(8,128)(2,1)} %gather_fusion.1, pred[112]{0:T(512)(128)(4,1)S(1)} %get-tuple-element.6), kind=kOutput, calls=%fused_computation.25 | convolution fusion | flops 471597056 | bytes 14680176 | tf_op jit(solution)/shard_map/otc,trc->otr/dot_general | solution.py:48
  100.7 3.0 %copy-done = f32[128,112,128]{0,2,1:T(8,128)} copy-done((f32[128,112,128]{0,2,1:T(8,128)}, f32[128,112,128]{0,2,1:T(8,128)S(1)}, u32[]{:S(2)}) %copy-start) | copy-done | bytes 7340056
  103.7 1.9 slice.59
  105.5 3.6 %copy.35 = f32[128,48,128]{2,1,0:T(8,128)} copy(f32[128,48,128]{0,2,1:T(8,128)} %slice.59) | data formatting | bytes 6291456 | tf_op jit(solution)/shard_map/slice | solution.py:51
  109.1 5.2 %fusion.26 = f32[64,128,128]{2,0,1:T(8,128)} fusion(f32[128,48,128]{2,1,0:T(8,128)} %copy.35, s32[48]{0:T(128)S(1)} %slice.39), kind=kOutput, calls=%fused_computation.36 | convolution fusion | flops 301992960 | bytes 7340224 | tf_op jit(solution)/shard_map/otr,tb->obr/dot_general | solution.py:50
  114.4 5.4 %copy.36 = f32[64,128,128]{1,2,0:T(8,128)} copy(f32[64,128,128]{2,0,1:T(8,128)} %fusion.26) | data formatting | bytes 8388608 | tf_op jit(solution)/shard_map/otr,tb->obr/dot_general | solution.py:50
  119.8 4.4 %slice_add_fusion = f32[128,64,128]{0,2,1:T(8,128)S(1)} fusion(f32[128,112,128]{0,2,1:T(8,128)} %copy-done, f32[64,128,128]{1,2,0:T(8,128)} %copy.36), kind=kLoop, calls=%fused_computation.11 | loop fusion | flops 1048576 | bytes 12582912 | tf_op jit(solution)/shard_map/add | solution.py:53
  124.2 4.4 %fusion.6 = bf16[128,8192]{0,1:T(8,128)(2,1)} fusion(bf16[128,8192]{0,1:T(8,128)(2,1)S(1)} %copy.27, f32[128,64,128]{0,2,1:T(8,128)S(1)} %slice_add_fusion, bf16[128,8192]{0,1:T(8,128)(2,1)S(1)} %copy-done.3, f32[]{:T(128)S(6)} %mul.58, f32[]{:T(128)S(6)} %div.33, f32[]{:T(128)} %bitcast.7, f32[8192]{0:T(1024)S(1)} %convert_bitcast_fusion), kind=kLoop, calls=%fused_computation.10 | loop fusion | flops 9437184 | bytes 10518540 | tf_op jit(solution)/shard_map/convert_element_type | solution.py:69
  128.6 2.9 %copy.37 = bf16[128,16,512]{2,0,1:T(8,128)(2,1)S(1)} copy(bf16[128,16,512]{0,2,1:T(8,128)(2,1)} %bitcast.60) | data formatting | bytes 4194304 | tf_op jit(solution)/shard_map/all_to_all | solution.py:70
  131.4 52.9 %all_to_all.38 = bf16[128,16,512]{2,0,1:T(8,128)(2,1)} all-to-all(bf16[128,16,512]{2,0,1:T(8,128)(2,1)S(1)} %copy.37), channel_id=1, replica_groups=mesh['slab'=2,'orb'=16] {'orb'}, dimensions={1} | all-to-all | bytes 4194304 | tf_op jit(solution)/shard_map/all_to_all | solution.py:70
  184.3 8.6 %fusion.24 = bf16[64,16,8,128]{3,2,1,0:T(8,128)(2,1)S(1)} fusion(bf16[2048,512]{1,0:T(8,128)(2,1)} %bitcast.61, bf16[2048,2048]{1,0:T(8,128)(2,1)} %all-gather.2.cloned.1.call-done), kind=kOutput, calls=%fused_computation.31 | convolution fusion | flops 4296015872 | bytes 12582912 | tf_op jit(solution)/shard_map/kj,kr->jr/dot_general | solution.py:71
  193.5 52.3 %all_to_all.39 = bf16[16,128,512]{1,2,0:T(8,128)(2,1)} all-to-all(bf16[16,128,512]{1,2,0:T(8,128)(2,1)S(1)} %bitcast.58), channel_id=1, replica_groups=mesh['slab'=2,'orb'=16] {'orb'}, dimensions={0} | all-to-all | bytes 4194304 | tf_op jit(solution)/shard_map/all_to_all | solution.py:77
  245.8 4.1 %copy.39 = bf16[128,8192]{1,0:T(8,128)(2,1)} copy(bf16[128,8192]{0,1:T(8,128)(2,1)} %bitcast.59) | data formatting | bytes 4194304 | tf_op jit(solution)/shard_map/all_to_all | solution.py:77
  (29 shorter events, 6.4 us)
Async XLA Ops:
  6.5 10.2 %copy-start.4 = (f32[3]{0:T(128)S(1)}, f32[3]{0:T(128)}, u32[]{:S(2)}) copy-start(f32[3]{0:T(128)} %param.14) | copy-start | bytes 40
  6.5 12.0 %copy-start.6 = (s32[112]{0:T(128)S(1)}, s32[112]{0:T(128)}, u32[]{:S(2)}) copy-start(s32[112]{0:T(128)} %param.11) | copy-start | bytes 1348
  6.5 12.8 %copy-start.7 = (s32[112]{0:T(128)S(1)}, s32[112]{0:T(128)}, u32[]{:S(2)}) copy-start(s32[112]{0:T(128)} %param.12) | copy-start | bytes 1348
  6.5 12.8 %copy-start.5 = (s32[64]{0:T(128)S(1)}, s32[64]{0:T(128)}, u32[]{:S(2)}) copy-start(s32[64]{0:T(128)} %param.13) | copy-start | bytes 772
  6.5 177.8 %all-gather.2.cloned.1.call-start = ((), (), s32[]{:S(2)}) async-start(), calls=%async_computation.2 | async-start | bytes 8912896 | tf_op jit(solution)/shard_map/all_gather | solution.py:73
  10.5 8.9 %collective-permute-start = (bf16[128,256]{0,1:T(8,128)(2,1)S(1)}, bf16[128,256]{0,1:T(8,128)(2,1)S(1)}, u32[]{:S(2)}, u32[]{:S(2)}) collective-permute-start(bf16[128,256]{0,1:T(8,128)(2,1)S(1)} %get-tuple-element.10), channel_id=1, source_target_pairs={{0,16},{1,17},{2,18},{3,19},{4,20},{5,21},{6,22},{7,23},{8,24},{9,... | collective-permute-start | bytes 196616 | tf_op jit(solution)/shard_map/ppermute | solution.py:14
  15.4 6.2 %collective-permute-start.1 = (bf16[128,256]{0,1:T(8,128)(2,1)S(1)}, bf16[128,256]{0,1:T(8,128)(2,1)S(1)}, u32[]{:S(2)}, u32[]{:S(2)}) collective-permute-start(bf16[128,256]{0,1:T(8,128)(2,1)S(1)} %get-tuple-element.11), channel_id=1, source_target_pairs={{16,0},{17,1},{18,2},{19,3},{20,4},{21,5},{22,6},{23,7},{24,8},{25... | collective-permute-start | bytes 196616 | tf_op jit(solution)/shard_map/ppermute | solution.py:17
  42.0 3.0 %copy-start.1 = (f32[128,112,128]{0,2,1:T(8,128)}, f32[128,112,128]{0,2,1:T(8,128)S(1)}, u32[]{:S(2)}) copy-start(f32[128,112,128]{0,2,1:T(8,128)S(1)} %fusion.16) | copy-start | bytes 22020100
  69.2 1.3 copy-start.2
  70.6 4.6 %collective-permute-start.2 = (bf16[128,256]{0,1:T(8,128)(2,1)S(1)}, bf16[128,256]{0,1:T(8,128)(2,1)S(1)}, u32[]{:S(2)}, u32[]{:S(2)}) collective-permute-start(bf16[128,256]{0,1:T(8,128)(2,1)S(1)} %get-tuple-element.8), channel_id=1, source_target_pairs={{0,16},{1,17},{2,18},{3,19},{4,20},{5,21},{6,22},{7,23},{8,24},{9,... | collective-permute-start | bytes 196616 | tf_op jit(solution)/shard_map/ppermute | solution.py:14
  73.3 6.2 %collective-permute-start.3 = (bf16[128,256]{0,1:T(8,128)(2,1)S(1)}, bf16[128,256]{0,1:T(8,128)(2,1)S(1)}, u32[]{:S(2)}, u32[]{:S(2)}) collective-permute-start(bf16[128,256]{0,1:T(8,128)(2,1)S(1)} %get-tuple-element.9), channel_id=1, source_target_pairs={{16,0},{17,1},{18,2},{19,3},{20,4},{21,5},{22,6},{23,7},{24,8},{25... | collective-permute-start | bytes 196616 | tf_op jit(solution)/shard_map/ppermute | solution.py:17
  100.7 3.0 %copy-start = (f32[128,112,128]{0,2,1:T(8,128)}, f32[128,112,128]{0,2,1:T(8,128)S(1)}, u32[]{:S(2)}) copy-start(f32[128,112,128]{0,2,1:T(8,128)S(1)} %fusion.19) | copy-start | bytes 22020100
  119.8 4.4 %copy-start.3 = (bf16[128,8192]{0,1:T(8,128)(2,1)S(1)}, bf16[128,8192]{0,1:T(8,128)(2,1)}, u32[]{:S(2)}) copy-start(bf16[128,8192]{0,1:T(8,128)(2,1)} %copy-done.2) | copy-start | bytes 6291460
Sparse Core Ops, SparseCore 0:
  9.5 77.5 all-gather.1
where the time goes:
time: 258 us; the launch traced here: 257 us
  blocking collectives  105 us (41%)
  local copies, waits for them, and re-layouts  58.2 us (23%)
  matrix products  30.9 us (12%)
  other arithmetic  29 us (11%)
  between operations  15.7 us (6%)
  starting transfers between devices  10.4 us (4%)
  waiting for transfers between devices  7.33 us (3%)
    all_to_all x1, blocking collectives, local(): lax.all_to_all(filtered_two, 'orb', split_axis=1, concat_axis=0, tiled=True)  52.9 us
    all_to_all x1, blocking collectives, local(): lax.all_to_all(rotated, 'orb', split_axis=0, concat_axis=1, tiled=True)  52.3 us
    concatenate x2, other arithmetic, with_halo(): block = jnp.concatenate([low, block, high], axis=dim)  12.4 us
    dot_general x2, matrix products, apply_tiles(): jnp.einsum('otc,trc->otr', picked, tiles, preferred_element_type=jnp.floa...  11.8 us
    slice x4, local copies, waits for them, and re-layouts, apply_tiles(): products[:, blocks:]  11.3 us
    dot_general x2, local copies, waits for them, and re-layouts, apply_tiles(): jnp.einsum('otr,tb->obr', products[:, blocks:], onehot, precision=lax.Pre...  10.8 us
    unnamed x17, local copies, waits for them, and re-layouts  10.6 us
    dot_general x2, matrix products, apply_tiles(): jnp.einsum('otr,tb->obr', products[:, blocks:], onehot, precision=lax.Pre...  10.5 us
  transfers between devices with their start and end apart: 5, of which 3 were waited for; matrix products, arithmetic and copies ran while one was open for 38% of the time, Pallas kernels for 0%

commit v1 on v0

--- a/solution.py
+++ b/solution.py
@@ -1,9 +1,403 @@
+import functools
+
 import jax
 import jax.numpy as jnp
 from jax import lax
+from jax.experimental import pallas as pl
+from jax.experimental.pallas import tpu as pltpu
 from jax.sharding import PartitionSpec as P
 
 HB = 2
+EDGE = 2 * HB
+PLANE = 4
+VMEM = pl.BlockSpec(memory_space=pltpu.VMEM)
+SMEM = pl.BlockSpec(memory_space=pltpu.SMEM)
+COST = pl.CostEstimate(flops=1000, bytes_accessed=1000, transcendentals=0)
+PARAMS = pltpu.CompilerParams(vmem_limit_bytes=36 * 1024 * 1024)
+f32, bf16 = jnp.float32, jnp.bfloat16
+
+
+def call(body, out_shape, in_specs, scratch_shapes=()):
+    return pl.pallas_call(
+        body,
+        out_shape=out_shape,
+        in_specs=in_specs,
+        out_specs=jax.tree.map(lambda _: VMEM, out_shape),
+        scratch_shapes=scratch_shapes,
+        compiler_params=PARAMS,
+        cost_estimate=COST,
+    )
+
+
+def after(value, *done):
+    return lax.optimization_barrier((value, done))[0]
+
+
+def coefficients(bounds_ref):
+    lower_bound = -3.0 + bounds_ref[0]
+    cutoff = bounds_ref[1] - 0.5
+    upper_bound = 3.0 + bounds_ref[2]
+    half_width = (upper_bound - cutoff) / 2.0
+    center = (upper_bound + cutoff) / 2.0
+    sigma_one = half_width / (lower_bound - center)
+    sigma_two = 1.0 / (2.0 / sigma_one - sigma_one)
+    return center, sigma_one / half_width, 2.0 * sigma_two / half_width, sigma_one * sigma_two
+
+
+def loop(start, stop, body, unroll, carry=0):
+    return lax.fori_loop(start, stop, body, carry, unroll=unroll)
+
+
+def product(tile, block):
+    return jnp.dot(tile, block, preferred_element_type=f32)
+
+
+def is_edge(row, blocks):
+    return (row < HB) | (row >= blocks - HB)
+
+
+def edge_slot(row, blocks):
+    return jnp.where(row < HB, row, row - blocks + EDGE)
+
+
+def edge_row(slot, blocks):
+    return slot if slot < HB else blocks - EDGE + slot
+
+
+def live_mask(tile, lanes, count):
+    return lax.broadcasted_iota(jnp.int32, (tile, lanes), 0) < count
+
+
+def sum_counts(counts_ref, rows):
+    total = 0
+    for r in rows:
+        total = total + counts_ref[r]
+    return total
+
+
+def start_kernel(groups, place_ref, x_ref, rotation_ref, halo_ref, *piece_refs):
+    width = halo_ref.shape[1]
+    z, slab, p = place_ref[0], place_ref[1], place_ref[2]
+    begin = jnp.where(slab == 0, x_ref.shape[1] - width, 0)
+    halo_ref[...] = x_ref[:, pl.ds(pl.multiple_of(begin, width), width)]
+    lanes = piece_refs[0].shape[1] // groups
+    half = groups // 2
+    for q, ref in enumerate(piece_refs):
+        for h in range(2):
+            for g in range(half):
+                block = ((slab ^ h) * half + g) * PLANE + (p ^ q)
+                begin = pl.multiple_of(block * lanes, lanes)
+                ref[:, (h * half + g) * lanes:(h * half + g + 1) * lanes] = rotation_ref[
+                    :, pl.ds(begin, lanes)
+                ]
+
+
+def multiply(blocks, rows_ref, cols_ref, tiles_ref, source_ref, acc_ref, extra_ref, first=None):
+    def diagonal(r, _):
+        block = source_ref[r] if first is None else first(r)
+        acc_ref[r] = product(tiles_ref[r], block)
+        return 0
+
+    loop(0, blocks, diagonal, 16)
+    listed = tiles_ref.shape[0]
+
+    def extra(k, _):
+        col = jnp.clip(cols_ref[k], 0, blocks - 1)
+        extra_ref[k - blocks] = product(tiles_ref[k], source_ref[col])
+        return 0
+
+    loop(blocks, listed, extra, 16)
+
+    def gather(k, _):
+        @pl.when((cols_ref[k] >= 0) & (cols_ref[k] < blocks))
+        def _():
+            acc_ref[rows_ref[k]] += extra_ref[k - blocks]
+
+        return 0
+
+    loop(blocks, listed, gather, 4)
+
+
+def multiply_edges(blocks, slab, rows_ref, cols_ref, tiles_ref, halo_ref, add):
+    def extra(k, _):
+        col = cols_ref[k]
+        slot = jnp.where(slab == 0, col - blocks, col + HB)
+
+        @pl.when(((col < 0) | (col >= blocks)) & (slot >= 0) & (slot < HB))
+        def _():
+            add(rows_ref[k], product(tiles_ref[k], halo_ref[slot]))
+
+        return 0
+
+    loop(blocks, tiles_ref.shape[0], extra, 4)
+
+
+def first_kernel(
+    blocks, place_ref, rows_ref, cols_ref, counts_ref, bounds_ref, x_ref, halo_ref, tiles_ref,
+    f1_ref, edge_ref, xt_ref, acc_ref, extra_ref, ext_ref,
+):
+    tile = tiles_ref.shape[1]
+    lanes = x_ref.shape[0]
+    slab = place_ref[1]
+
+    def turn(r):
+        xt_ref[r] = x_ref[:, pl.ds(pl.multiple_of(r * tile, tile), tile)].T
+        return xt_ref[r]
+
+    multiply(blocks, rows_ref, cols_ref, tiles_ref, xt_ref, acc_ref, extra_ref, turn)
+    for b in range(HB):
+        ext_ref[b] = halo_ref[:, b * tile:(b + 1) * tile].T
+
+    def add(row, value):
+        acc_ref[row] += value
+
+    multiply_edges(blocks, slab, rows_ref, cols_ref, tiles_ref, ext_ref, add)
+    center, scale = coefficients(bounds_ref)[:2]
+
+    def finish(r, _):
+        value = (acc_ref[r] - center * xt_ref[r].astype(f32)) * scale
+        f1_ref[r] = jnp.where(live_mask(tile, lanes, counts_ref[r]), value, 0.0).astype(bf16)
+        return 0
+
+    loop(0, blocks, finish, 4)
+    begin = jnp.where(slab == 0, blocks - HB, 0)
+    for b in range(HB):
+        edge_ref[b] = f1_ref[begin + b]
+
+
+def second_values(r, acc, block, xt_ref, counts_ref, scales):
+    tile, lanes = block.shape
+    center, _, scale, both = scales
+    value = (acc - center * block.astype(f32)) * scale - both * xt_ref[r].astype(f32)
+    return jnp.where(live_mask(tile, lanes, counts_ref[r]), value, 0.0)
+
+
+def split_parts(outs, place_ref, packed_ref, base):
+    part = outs[0].shape[0]
+    for s, out in enumerate(outs):
+        start = pl.multiple_of(base + (place_ref[0] ^ s) * part, 16)
+        out[...] = packed_ref[pl.ds(start, part)].astype(bf16)
+
+
+def second_kernel(
+    blocks, groups, place_ref, rows_ref, cols_ref, counts_ref, bounds_ref, f1_ref, xt_ref, tiles_ref,
+    *refs,
+):
+    outs, refs = refs[:groups], refs[groups:]
+    shared_ref, excess_ref, rest_ref, edge_ref, acc_ref, extra_ref, packed_ref = refs
+    tile = tiles_ref.shape[1]
+    multiply(blocks, rows_ref, cols_ref, tiles_ref, f1_ref, acc_ref, extra_ref)
+    edges = [edge_row(e, blocks) for e in range(EDGE)]
+    for e, r in enumerate(edges):
+        edge_ref[e] = acc_ref[r]
+    scales = coefficients(bounds_ref)
+
+    def finish(r, offset):
+        packed_ref[pl.ds(offset, tile)] = second_values(
+            r, acc_ref[r], f1_ref[r], xt_ref, counts_ref, scales
+        )
+        return offset + counts_ref[r]
+
+    loop(HB, blocks - HB, finish, 4, sum_counts(counts_ref, edges))
+    size = rest_ref.shape[0]
+    rest_ref[...] = packed_ref[:size]
+    split_parts(outs, place_ref, packed_ref, size)
+    shared_ref[...] = packed_ref[2 * size:3 * size].astype(bf16)
+    excess_ref[...] = packed_ref[3 * size:4 * size].astype(bf16)
+
+
+def second_edge_kernel(
+    blocks, groups, place_ref, rows_ref, cols_ref, counts_ref, bounds_ref, halo_ref, f1_ref, xt_ref,
+    tiles_ref, sum_ref, rest_ref, *refs,
+):
+    outs, (acc_ref, packed_ref) = refs[:groups], refs[groups:]
+    tile = tiles_ref.shape[1]
+    acc_ref[...] = sum_ref[...]
+
+    def add(row, value):
+        acc_ref[edge_slot(row, blocks)] += value
+
+    multiply_edges(blocks, place_ref[1], rows_ref, cols_ref, tiles_ref, halo_ref, add)
+    scales = coefficients(bounds_ref)
+    packed_ref[...] = rest_ref[...]
+    offset = 0
+    for e in range(EDGE):
+        r = edge_row(e, blocks)
+        value = second_values(r, acc_ref[e], f1_ref[r], xt_ref, counts_ref, scales)
+        here = pl.ds(offset, tile)
+        live = live_mask(tile, value.shape[1], counts_ref[r])
+        packed_ref[here] = jnp.where(live, value, packed_ref[here])
+        offset = offset + counts_ref[r]
+    split_parts(outs, place_ref, packed_ref, 0)
+
+
+def merge_kernel(blocks, groups, place_ref, counts_ref, shared_ref, excess_ref, *refs):
+    outs, packed_ref = refs[:groups], refs[groups]
+    size = shared_ref.shape[0]
+    live = sum_counts(counts_ref, range(blocks))
+    packed_ref[:size] = shared_ref[...].astype(f32)
+    packed_ref[pl.ds(jnp.clip(live - 2 * size, 0, size), size)] = excess_ref[...].astype(f32)
+    split_parts(outs, place_ref, packed_ref, 0)
+
+
+def rotate_kernel(groups, place_ref, *refs):
+    own, over_x, over_core, over_both = refs[:4]
+    mine, near, far_two, far_three, other_two, other_three = refs[4:10]
+    outs, turned = refs[10:10 + groups], refs[-1]
+    width = outs[0].shape[1]
+    half = groups // 2 * width
+    lhs = jnp.concatenate(
+        [ref[s] for s in range(groups) for ref in (own, over_core, over_x, over_both)], axis=1
+    )
+    for h in range(2):
+        far = (far_two, far_three) if h == 0 else (other_two, other_three)
+        rhs = [ref[:, h * half:(h + 1) * half] for ref in (mine, near)] + [ref[...] for ref in far]
+        total = product(lhs, jnp.concatenate(rhs, axis=0)).astype(bf16)
+        first = (place_ref[1] ^ h) * (groups // 2)
+        for z in range(groups // 2):
+            turned[first + z] = total[:, z * width:(z + 1) * width]
+    for s in range(groups):
+        outs[s][...] = turned[place_ref[0] ^ s]
+
+
+def spread_kernel(blocks, groups, place_ref, counts_ref, back_ref, *refs):
+    parts, out_ref, packed_ref = refs[:-2], refs[-2], refs[-1]
+    part, width = parts[0].shape
+    size = part * groups
+    tile = out_ref.shape[1] // blocks
+    live = sum_counts(counts_ref, range(blocks))
+    packed_ref[pl.ds(jnp.clip(live - size, 2 * size, 3 * size), size)] = back_ref[...].astype(f32)
+    for i in range(3):
+        for s in range(groups):
+            start = pl.multiple_of((i * groups + (place_ref[0] ^ s)) * part, 16)
+            packed_ref[pl.ds(start, part)] = parts[i * groups + s][...].astype(f32)
+
+    def one(b, offset):
+        rows = packed_ref[pl.ds(offset, tile)]
+        rows = jnp.where(live_mask(tile, width, counts_ref[b]), rows, 0.0)
+        out_ref[:, pl.ds(pl.multiple_of(b * tile, tile), tile)] = rows.T.astype(bf16)
+        return offset + counts_ref[b]
+
+    offset = 0
+    for e in range(EDGE):
+        offset = one(edge_row(e, blocks), offset)
+    loop(HB, blocks - HB, one, 4, offset)
+
+
+def paired(orbitals_t, tiles, tile_rows, tile_cols, row_counts, bounds, rotation):
+    norb_dev, rows_dev = orbitals_t.shape
+    listed, tile = tiles.shape[:2]
+    blocks = rows_dev // tile
+    orbs = lax.axis_size("orb")
+    groups = orbs // PLANE
+    me, slab = lax.axis_index("orb"), lax.axis_index("slab")
+    z, p = me // PLANE, me % PLANE
+    place = jnp.stack([z, slab, p])
+    size = rows_dev // 4
+    part = size // groups
+    block_shape = (blocks, tile, norb_dev)
+    edge_shape = (EDGE, tile, norb_dev)
+    halo_shape = (HB, tile, norb_dev)
+    extra_shape = (listed - blocks, tile, norb_dev)
+    size_shape = (size, norb_dev)
+    lists = (place, tile_rows, tile_cols, row_counts, bounds)
+
+    def shaped(shape, dtype=bf16):
+        return jax.ShapeDtypeStruct(shape, dtype)
+
+    part_outs = [shaped((part, norb_dev))] * groups
+
+    def swap(value, bits):
+        return lax.ppermute(value, "orb", [(i, i ^ bits) for i in range(orbs)])
+
+    def over_z(values):
+        moved = {s: swap(values[s], s * PLANE) for s in (2, 3, 1)}
+        return [values[0], moved[1], moved[2], moved[3]]
+
+    def other_slab(value):
+        return lax.ppermute(value, "slab", [(0, 1), (1, 0)])
+
+    half = groups // 2 * norb_dev
+    halo, *pieces = call(
+        functools.partial(start_kernel, groups),
+        [shaped((norb_dev, HB * tile))] + [shaped((norb_dev, 2 * half))] * PLANE,
+        [SMEM] + [VMEM] * 2,
+    )(place, orbitals_t, rotation)
+    halo = other_slab(halo)
+    mine = [pieces[0]] + [swap(pieces[q], q) for q in range(1, PLANE)]
+    mine = jnp.concatenate(mine, axis=0)
+    far_two = swap(mine[:, :half], 2 * PLANE)
+    near = swap(mine, PLANE)
+
+    f1, edge, xt = call(
+        functools.partial(first_kernel, blocks),
+        [shaped(block_shape), shaped(halo_shape), shaped(block_shape)],
+        [SMEM] * 5 + [VMEM] * 3,
+        [pltpu.VMEM(block_shape, f32), pltpu.VMEM(extra_shape, f32), pltpu.VMEM(halo_shape, bf16)],
+    )(*lists, orbitals_t, halo, tiles)
+    halo = other_slab(edge)
+
+    *first_parts, shared, excess, rest, edge_sum = call(
+        functools.partial(second_kernel, blocks, groups),
+        part_outs
+        + [shaped(size_shape)] * 2 + [shaped(size_shape, f32), shaped(edge_shape, f32)],
+        [SMEM] * 5 + [VMEM] * 3,
+        [
+            pltpu.VMEM(block_shape, f32),
+            pltpu.VMEM(extra_shape, f32),
+            pltpu.VMEM((rows_dev + tile, norb_dev), f32),
+        ],
+    )(*lists, after(f1, far_two), xt, tiles)
+    excess = other_slab(excess)
+    whole_first = over_z(first_parts)
+    rest_parts = call(
+        functools.partial(second_edge_kernel, blocks, groups),
+        part_outs,
+        [SMEM] * 5 + [VMEM] * 6,
+        [pltpu.VMEM(edge_shape, f32), pltpu.VMEM(size_shape, f32)],
+    )(*lists, halo, f1, xt, tiles, edge_sum, after(rest, near))
+    shared = after(shared, rest_parts)
+    shared_parts = call(
+        functools.partial(merge_kernel, blocks, groups),
+        part_outs,
+        [SMEM] * 2 + [VMEM] * 2,
+        [pltpu.VMEM((2 * size, norb_dev), f32)],
+    )(place, row_counts, shared, excess)
+    far_three = swap(far_two, PLANE)
+    shared_parts = after(shared_parts, whole_first, far_three)
+    weights = [mine, near, far_two, far_three, other_slab(far_two), other_slab(far_three)]
+
+    def gather(whole):
+        own = jnp.stack(whole)
+        over_x = swap(own, 2)
+        return own, over_x, swap(own, 1), swap(over_x, 1)
+
+    def rotate(gathered):
+        return call(
+            functools.partial(rotate_kernel, groups),
+            part_outs,
+            [SMEM] + [VMEM] * (4 + len(weights)),
+            [pltpu.VMEM((groups, part, norb_dev), bf16)],
+        )(place, *gathered, *weights)
+
+    whole_shared = over_z(shared_parts)
+    whole_rest = over_z(after(rest_parts, whole_shared))
+    whole_shared, weights = lax.optimization_barrier((whole_shared, weights))
+    first_back = over_z(rotate(gather(whole_first)))
+    shared_back = over_z(after(rotate(gather(whole_shared)), first_back))
+    rest_back = over_z(after(rotate(gather(whole_rest)), shared_back))
+    back = jnp.concatenate([jnp.zeros_like(v) for v in shared_back])
+    for s, v in enumerate(shared_back):
+        back = lax.dynamic_update_slice_in_dim(back, v, (z ^ s) * part, 0)
+    back = other_slab(back)
+
+    returned = rest_back + first_back + shared_back
+    return call(
+        functools.partial(spread_kernel, blocks, groups),
+        shaped((norb_dev, rows_dev)),
+        [SMEM] * 2 + [VMEM] * (1 + len(returned)),
+        [pltpu.VMEM((rows_dev + 2 * tile, norb_dev), f32)],
+    )(place, row_counts, back, *returned)
 
 
 def with_halo(block, sides, width):
@@ -19,7 +413,7 @@
     return block
 
 
-def local(orbitals_t, tiles, tile_rows, tile_cols, row_counts, bounds, rotation):
+def general(orbitals_t, tiles, tile_rows, tile_cols, row_counts, bounds, rotation):
     norb_dev, rows_dev = orbitals_t.shape
     tile_size = tiles.shape[1]
     blocks = rows_dev // tile_size
@@ -77,6 +471,12 @@
     return lax.all_to_all(rotated, "orb", split_axis=0, concat_axis=1, tiled=True)
 
 
+def local(orbitals_t, tiles, *rest):
+    slabs, orbs = lax.axis_size("slab"), lax.axis_size("orb")
+    fits = slabs == 2 and orbs == PLANE * PLANE and orbitals_t.shape[0] % tiles.shape[1] == 0
+    return (paired if fits else general)(orbitals_t, tiles, *rest)
+
+
 def solution(mesh):
     return jax.shard_map(
         local,

time: 258 us -> 141 us (0.55)
  blocking collectives: 105 us -> 0 us
  local copies, waits for them, and re-layouts: 58.2 us -> 6.11 us
  waiting for transfers between devices: 7.33 us -> 57.8 us
  starting transfers between devices: 10.4 us -> 51.6 us
  matrix products: 30.9 us -> 0 us
  other arithmetic: 29 us -> 0.28 us
  Pallas kernels: 0 us -> 24.4 us
  between operations: 15.7 us -> 0.28 us
    all_to_all x2 -> x0, blocking collectives: 105 us -> none  [the longest x1 52.9 us: local(): lax.all_to_all(filtered_two, 'orb', split_axis=1, concat_axis=0, tiled=True)]
    ppermute x4 -> x39, waiting for transfers between devices: 6.65 us -> 57.8 us  [the longest x33 46.6 us: swap(): return lax.ppermute(value, 'orb', [(i, i ^ bits) for i in range(orbs)])]
    ppermute x4 -> x39, starting transfers between devices: 10.3 us -> 51.6 us  [the longest x33 44.3 us: swap(): return lax.ppermute(value, 'orb', [(i, i ^ bits) for i in range(orbs)])]
    dot_general x5 -> x0, matrix products: 30.9 us -> none  [the longest x2 11.8 us: apply_tiles(): jnp.einsum('otc,trc->otr', picked, tiles, preferred_element_type=jnp.floa...]
    pallas_call x0 -> x9, Pallas kernels: none -> 24.4 us  [the longest x3 6.19 us: rotate(): call(functools.partial(rotate_kernel, groups), part_outs, [SMEM] + [VMEM]...]
    concatenate x2 -> x0, other arithmetic: 12.4 us -> none  [with_halo(): block = jnp.concatenate([low, block, high], axis=dim)]
    slice x8 -> x1, local copies, waits for them, and re-layouts: 12 us -> 0.02 us  [paired(): far_two = swap(mine[:, :half], 2 * PLANE)]
    dot_general x2 -> x0, local copies, waits for them, and re-layouts: 10.8 us -> none  [apply_tiles(): jnp.einsum('otr,tb->obr', products[:, blocks:], onehot, precision=lax.Pre...]
  transfers between devices with their start and end apart: 5 -> 39, of which waited for: 3 -> 16; matrix products, arithmetic and copies ran while one was open for 38% -> 0% of each run, Pallas kernels for 0% -> 14%
where the time goes in v1:
time: 141 us; the launch traced here: 140 us
  waiting for transfers between devices  57.8 us (41%)
  starting transfers between devices  51.6 us (37%)
  Pallas kernels  24.4 us (17%)
  local copies, waits for them, and re-layouts  6.11 us (4%)
    ppermute x33, waiting for transfers between devices, swap(): return lax.ppermute(value, 'orb', [(i, i ^ bits) for i in range(orbs)])  46.6 us
    ppermute x33, starting transfers between devices, swap(): return lax.ppermute(value, 'orb', [(i, i ^ bits) for i in range(orbs)])  44.3 us
    ppermute x6, waiting for transfers between devices, other_slab(): return lax.ppermute(value, 'slab', [(0, 1), (1, 0)])  11.2 us
    ppermute x6, starting transfers between devices, other_slab(): return lax.ppermute(value, 'slab', [(0, 1), (1, 0)])  7.25 us
    pallas_call x3, Pallas kernels, rotate(): call(functools.partial(rotate_kernel, groups), part_outs, [SMEM] + [VMEM]...  6.19 us
    unnamed x33, local copies, waits for them, and re-layouts  5.93 us
    pallas_call x1, Pallas kernels, paired(): call(functools.partial(first_kernel, blocks), [shaped(block_shape), shape...  5.77 us
    pallas_call x1, Pallas kernels, paired(): call(functools.partial(second_kernel, blocks, groups), part_outs + [shape...  5.21 us
  transfers between devices with their start and end apart: 39, of which 16 were waited for; matrix products, arithmetic and copies ran while one was open for 0% of the time, Pallas kernels for 14%

profile of v1, /device:TPU:0, one launch (start us, length us, event | category | flops | bytes accessed | tf_op | source)
XLA Modules:
  0.0 140.4 jit_solution(1195600867876580078)
XLA Ops:
  0.1 1.6 %copy-done.1 = bf16[128,8192]{1,0:T(8,128)(2,1)S(1)} copy-done((bf16[128,8192]{1,0:T(8,128)(2,1)S(1)}, bf16[128,8192]{1,0:T(8,128)(2,1)}, u32[]{:S(2)}) %copy-start.1) | copy-done | bytes 2097176
  4.0 2.6 %collective-permute-start.2 = (bf16[128,512]{1,0:T(8,128)(2,1)S(1)}, bf16[128,512]{1,0:T(8,128)(2,1)S(1)}, u32[]{:S(2)}, u32[]{:S(2)}) collective-permute-start(bf16[128,512]{1,0:T(8,128)(2,1)S(1)} %get-tuple-element.74), channel_id=1, source_target_pairs={{0,2},{1,3},{2,0},{3,1},{4,6},{5,7},{6,4},{7,5},{8,10},{9,11},{10,... | collective-permute-start | bytes 393224 | tf_op jit(solution)/shard_map/ppermute | solution.py:311
  6.6 4.2 %collective-permute-done.2 = bf16[128,512]{1,0:T(8,128)(2,1)S(1)} collective-permute-done((bf16[128,512]{1,0:T(8,128)(2,1)S(1)}, bf16[128,512]{1,0:T(8,128)(2,1)S(1)}, u32[]{:S(2)}, u32[]{:S(2)}) %collective-permute-start.2) | collective-permute-done | bytes 131104 | tf_op jit(solution)/shard_map/ppermute | solution.py:311
  10.9 2.3 %collective-permute-done.3 = bf16[128,512]{1,0:T(8,128)(2,1)S(1)} collective-permute-done((bf16[128,512]{1,0:T(8,128)(2,1)S(1)}, bf16[128,512]{1,0:T(8,128)(2,1)S(1)}, u32[]{:S(2)}, u32[]{:S(2)}) %collective-permute-start.3) | collective-permute-done | bytes 131104 | tf_op jit(solution)/shard_map/ppermute | solution.py:311
  13.2 2.7 %collective-permute-start.4 = (bf16[512,256]{1,0:T(8,128)(2,1)S(1)}, bf16[512,256]{1,0:T(8,128)(2,1)S(1)}, u32[]{:S(2)}, u32[]{:S(2)}) collective-permute-start(bf16[512,256]{1,0:T(8,128)(2,1)S(1)} %slice.4), channel_id=1, source_target_pairs={{0,8},{1,9},{2,10},{3,11},{4,12},{5,13},{6,14},{7,15},{8,0},{9,1},... | collective-permute-start | bytes 786440 | tf_op jit(solution)/shard_map/ppermute | solution.py:311
  17.4 1.6 %collective-permute-start.6 = (bf16[512,512]{1,0:T(8,128)(2,1)S(1)}, bf16[512,512]{1,0:T(8,128)(2,1)S(1)}, u32[]{:S(2)}, u32[]{:S(2)}) collective-permute-start(bf16[512,512]{1,0:T(8,128)(2,1)S(1)} %constant_dynamic-update-slice_fusion.refs_4_), channel_id=1, source_target_pairs={{0,4},{1,5},{2,6},{3,7},{4,0},{5,1},{6,2},{7,3},{8,12},{9,13},{10,... | collective-permute-start | bytes 1572872 | tf_op jit(solution)/shard_map/ppermute | solution.py:311
  20.2 5.8 %shard_map.74 = (bf16[64,128,128]{2,1,0:T(8,128)(2,1)S(1)}, bf16[2,128,128]{2,1,0:T(8,128)(2,1)S(1)}, bf16[64,128,128]{2,1,0:T(8,128)(2,1)S(1)}) custom-call(s32[3]{0:T(128)S(1)} %pad_add_fusion.place_ref, s32[112]{0:T(128)S(1)} %copy-done.10, s32[112]{0:T(128)S(1)} %copy-done.11, s32[64]{0:T(128)S(1)} %copy-done.9, f32[3]{0:T(128)S(1)} %copy-done.12, ...), custom_call_target="tpu_custom_call" | custom-call | flops 1000 | bytes 1000 | tf_op jit(solution)/shard_map/pallas_call | solution.py:332
  26.0 2.4 %collective-permute-done.4.refs_6_ = bf16[512,256]{1,0:T(8,128)(2,1)S(1)} collective-permute-done((bf16[512,256]{1,0:T(8,128)(2,1)S(1)}, bf16[512,256]{1,0:T(8,128)(2,1)S(1)}, u32[]{:S(2)}, u32[]{:S(2)}) %collective-permute-start.4) | collective-permute-done | bytes 262176 | tf_op jit(solution)/shard_map/ppermute | solution.py:311
  28.4 5.2 %shard_map.75 = (bf16[512,128]{1,0:T(8,128)(2,1)S(1)}, bf16[512,128]{1,0:T(8,128)(2,1)S(1)}, bf16[512,128]{1,0:T(8,128)(2,1)S(1)}, bf16[512,128]{1,0:T(8,128)(2,...) custom-call(s32[3]{0:T(128)S(1)} %pad_add_fusion.place_ref, ...), custom_call_target="tpu_custom_call" | custom-call | flops 1000 | bytes 1000 | tf_op jit(solution)/shard_map/pallas_call | solution.py:340
  33.6 1.6 %collective-permute-start.7 = (bf16[2048,128]{1,0:T(8,128)(2,1)S(1)}, bf16[2048,128]{1,0:T(8,128)(2,1)S(1)}, u32[]{:S(2)}, u32[]{:S(2)}) collective-permute-start(bf16[2048,128]{1,0:T(8,128)(2,1)S(1)} %get-tuple-element.88), channel_id=1, source_target_pairs={{0,16},{16,0},{1,17},{17,1},{2,18},{18,2},{3,19},{19,3},{4,20},{20... | collective-permute-start | bytes 1572872 | tf_op jit(solution)/shard_map/ppermute | solution.py:318
  36.4 2.9 %collective-permute-start.10 = (bf16[512,128]{1,0:T(8,128)(2,1)S(1)}, bf16[512,128]{1,0:T(8,128)(2,1)S(1)}, u32[]{:S(2)}, u32[]{:S(2)}) collective-permute-start(bf16[512,128]{1,0:T(8,128)(2,1)S(1)} %get-tuple-element.96), channel_id=1, source_target_pairs={{0,12},{1,13},{2,14},{3,15},{4,8},{5,9},{6,10},{7,11},{8,4},{9,5},... | collective-permute-start | bytes 393224 | tf_op jit(solution)/shard_map/ppermute | solution.py:311
  39.2 9.1 %collective-permute-done.5.halo_ref = bf16[2,128,128]{2,1,0:T(8,128)(2,1)S(1)} collective-permute-done((bf16[2,128,128]{2,1,0:T(8,128)(2,1)S(1)}, bf16[2,128,128]{2,1,0:T(8,128)(2,1)S(1)}, u32[]{:S(2)}, u32[]{:S(2)}) %collective-permute-start.5) | collective-permute-done | bytes 65568 | tf_op jit(solution)/shard_map/ppermute | solution.py:318
  49.6 3.4 %collective-permute-start.9 = (bf16[512,128]{1,0:T(8,128)(2,1)S(1)}, bf16[512,128]{1,0:T(8,128)(2,1)S(1)}, u32[]{:S(2)}, u32[]{:S(2)}) collective-permute-start(bf16[512,128]{1,0:T(8,128)(2,1)S(1)} %get-tuple-element.95), channel_id=1, source_target_pairs={{0,8},{1,9},{2,10},{3,11},{4,12},{5,13},{6,14},{7,15},{8,0},{9,1},... | collective-permute-start | bytes 393224 | tf_op jit(solution)/shard_map/ppermute | solution.py:311
  58.6 2.7 %collective-permute-start.13 = (bf16[512,128]{1,0:T(8,128)(2,1)S(1)}, bf16[512,128]{1,0:T(8,128)(2,1)S(1)}, u32[]{:S(2)}, u32[]{:S(2)}) collective-permute-start(bf16[512,128]{1,0:T(8,128)(2,1)S(1)} %get-tuple-element.99), channel_id=1, source_target_pairs={{0,8},{1,9},{2,10},{3,11},{4,12},{5,13},{6,14},{7,15},{8,0},{9,1},... | collective-permute-start | bytes 393224 | tf_op jit(solution)/shard_map/ppermute | solution.py:311
  66.1 3.6 %collective-permute-done.13 = bf16[512,128]{1,0:T(8,128)(2,1)S(1)} collective-permute-done((bf16[512,128]{1,0:T(8,128)(2,1)S(1)}, bf16[512,128]{1,0:T(8,128)(2,1)S(1)}, u32[]{:S(2)}, u32[]{:S(2)}) %collective-permute-start.13) | collective-permute-done | bytes 131104 | tf_op jit(solution)/shard_map/ppermute | solution.py:311
  71.4 2.1 %collective-permute-start.30 = (bf16[512,128]{1,0:T(8,128)(2,1)S(1)}, bf16[512,128]{1,0:T(8,128)(2,1)S(1)}, u32[]{:S(2)}, u32[]{:S(2)}) collective-permute-start(bf16[512,128]{1,0:T(8,128)(2,1)S(1)} %get-tuple-element.124), channel_id=1, source_target_pairs={{0,4},{1,5},{2,6},{3,7},{4,0},{5,1},{6,2},{7,3},{8,12},{9,13},{10,... | collective-permute-start | bytes 393224 | tf_op jit(solution)/shard_map/ppermute | solution.py:311
  73.6 2.3 %collective-permute-start.32 = (bf16[512,128]{1,0:T(8,128)(2,1)S(1)}, bf16[512,128]{1,0:T(8,128)(2,1)S(1)}, u32[]{:S(2)}, u32[]{:S(2)}) collective-permute-start(bf16[512,128]{1,0:T(8,128)(2,1)S(1)} %get-tuple-element.126), channel_id=1, source_target_pairs={{0,12},{1,13},{2,14},{3,15},{4,8},{5,9},{6,10},{7,11},{8,4},{9,5},... | collective-permute-start | bytes 393224 | tf_op jit(solution)/shard_map/ppermute | solution.py:311
  75.8 2.0 %collective-permute-done.20.refs_1_ = bf16[4,512,128]{2,1,0:T(8,128)(2,1)S(1)} collective-permute-done((bf16[4,512,128]{2,1,0:T(8,128)(2,1)S(1)}, bf16[4,512,128]{2,1,0:T(8,128)(2,1)S(1)}, u32[]{:S(2)}, u32[]{:S(2)}) %collective-permute-start.20) | collective-permute-done | bytes 524320 | tf_op jit(solution)/shard_map/ppermute | solution.py:311
  78.4 5.8 %collective-permute-done.31 = bf16[512,128]{1,0:T(8,128)(2,1)S(1)} collective-permute-done((bf16[512,128]{1,0:T(8,128)(2,1)S(1)}, bf16[512,128]{1,0:T(8,128)(2,1)S(1)}, u32[]{:S(2)}, u32[]{:S(2)}) %collective-permute-start.31) | collective-permute-done | bytes 131104 | tf_op jit(solution)/shard_map/ppermute | solution.py:311
  85.8 1.9 %shard_map.79 = (bf16[512,128]{1,0:T(8,128)(2,1)S(1)}, bf16[512,128]{1,0:T(8,128)(2,1)S(1)}, bf16[512,128]{1,0:T(8,128)(2,1)S(1)}, bf16[512,128]{1,0:T(8,128)(2,1)S(1)}) custom-call(s32[3]{0:T(128)S(1)} %pad_add_fusion.place_ref, bf16[4,512,128]{2,1,0:T(8,128)(2,1)S(1)} %pad_maximum_fusion.1.refs_0_, ...), custom_call_target="tpu_custom_call" | custom-call | flops 1000 | bytes 1000 | tf_op jit(solution)/shard_map/pallas_call | solution.py:376
  87.7 1.7 %collective-permute-start.23 = (bf16[512,128]{1,0:T(8,128)(2,1)S(1)}, bf16[512,128]{1,0:T(8,128)(2,1)S(1)}, u32[]{:S(2)}, u32[]{:S(2)}) collective-permute-start(bf16[512,128]{1,0:T(8,128)(2,1)S(1)} %get-tuple-element.116), channel_id=1, source_target_pairs={{0,4},{1,5},{2,6},{3,7},{4,0},{5,1},{6,2},{7,3},{8,12},{9,13},{10,... | collective-permute-start | bytes 393224 | tf_op jit(solution)/shard_map/ppermute | solution.py:311
  92.1 2.5 %shard_map.78 = (bf16[512,128]{1,0:T(8,128)(2,1)S(1)}, bf16[512,128]{1,0:T(8,128)(2,1)}, bf16[512,128]{1,0:T(8,128)(2,1)S(1)}, bf16[512,128]{1,0:T(8,128)(2,1)S(1)}) custom-call(s32[3]{0:T(128)S(1)} %pad_add_fusion.place_ref, bf16[4,512,128]{2,1,0:T(8,128)(2,1)S(1)} %pad_maximum_fusion.refs_0_, bf16[4,512,128]{2,1,0:T(8,128)(2,1)S(1)} %collective-permute-done.17.refs_1_, ...), custom_call_target="tpu_custom_call" | custom-call | flops 1000 | bytes 1000 | tf_op jit(solution)/shard_map/pallas_call | solution.py:376
  96.6 5.0 %collective-permute-done.24.refs_6_ = bf16[512,128]{1,0:T(8,128)(2,1)S(1)} collective-permute-done((bf16[512,128]{1,0:T(8,128)(2,1)S(1)}, bf16[512,128]{1,0:T(8,128)(2,1)S(1)}, u32[]{:S(2)}, u32[]{:S(2)}) %collective-permute-start.24) | collective-permute-done | bytes 131104 | tf_op jit(solution)/shard_map/ppermute | solution.py:311
  106.0 1.7 %collective-permute-start.28 = (bf16[512,128]{1,0:T(8,128)(2,1)}, bf16[512,128]{1,0:T(8,128)(2,1)S(1)}, u32[]{:S(2)}, u32[]{:S(2)}) collective-permute-start(bf16[512,128]{1,0:T(8,128)(2,1)} %copy-done.13), channel_id=1, source_target_pairs={{0,12},{1,13},{2,14},{3,15},{4,8},{5,9},{6,10},{7,11},{8,4},{9,5},... | collective-permute-start | bytes 393224 | tf_op jit(solution)/shard_map/ppermute | solution.py:311
  108.1 9.3 %collective-permute-done.27.refs_10_ = bf16[512,128]{1,0:T(8,128)(2,1)S(1)} collective-permute-done((bf16[512,128]{1,0:T(8,128)(2,1)}, bf16[512,128]{1,0:T(8,128)(2,1)S(1)}, u32[]{:S(2)}, u32[]{:S(2)}) %collective-permute-start.27) | collective-permute-done | bytes 131104 | tf_op jit(solution)/shard_map/ppermute | solution.py:311
  117.5 1.6 %collective-permute-start.29 = (bf16[2048,128]{1,0:T(8,128)(2,1)S(1)}, bf16[2048,128]{1,0:T(8,128)(2,1)S(1)}, u32[]{:S(2)}, u32[]{:S(2)}) collective-permute-start(bf16[2048,128]{1,0:T(8,128)(2,1)S(1)} %constant_dynamic-update-slice_fusion.4), channel_id=1, source_target_pairs={{0,16},{16,0},{1,17},{17,1},{2,18},{18,2},{3,19},{19,3},{4,20},{20... | collective-permute-start | bytes 1572872 | tf_op jit(solution)/shard_map/ppermute | solution.py:318
  119.0 1.8 %shard_map.80 = (bf16[512,128]{1,0:T(8,128)(2,1)S(1)}, bf16[512,128]{1,0:T(8,128)(2,1)S(1)}, bf16[512,128]{1,0:T(8,128)(2,1)S(1)}, bf16[512,128]{1,0:T(8,128)(2,1)S(1)}) custom-call(s32[3]{0:T(128)S(1)} %pad_add_fusion.place_ref, bf16[4,512,128]{2,1,0:T(8,128)(2,1)S(1)} %pad_maximum_fusion.2.refs_0_, ...), custom_call_target="tpu_custom_call" | custom-call | flops 1000 | bytes 1000 | tf_op jit(solution)/shard_map/pallas_call | solution.py:376
  120.9 2.9 %collective-permute-start.36 = (bf16[512,128]{1,0:T(8,128)(2,1)S(1)}, bf16[512,128]{1,0:T(8,128)(2,1)S(1)}, u32[]{:S(2)}, u32[]{:S(2)}) collective-permute-start(bf16[512,128]{1,0:T(8,128)(2,1)S(1)} %get-tuple-element.132), channel_id=1, source_target_pairs={{0,4},{1,5},{2,6},{3,7},{4,0},{5,1},{6,2},{7,3},{8,12},{9,13},{10,... | collective-permute-start | bytes 393224 | tf_op jit(solution)/shard_map/ppermute | solution.py:311
  124.6 1.6 %collective-permute-start.38 = (bf16[512,128]{1,0:T(8,128)(2,1)S(1)}, bf16[512,128]{1,0:T(8,128)(2,1)S(1)}, u32[]{:S(2)}, u32[]{:S(2)}) collective-permute-start(bf16[512,128]{1,0:T(8,128)(2,1)S(1)} %get-tuple-element.134), channel_id=1, source_target_pairs={{0,12},{1,13},{2,14},{3,15},{4,8},{5,9},{6,10},{7,11},{8,4},{9,5},... | collective-permute-start | bytes 393224 | tf_op jit(solution)/shard_map/ppermute | solution.py:311
  126.2 1.6 %collective-permute-done.36.refs_1_ = bf16[512,128]{1,0:T(8,128)(2,1)S(1)} collective-permute-done((bf16[512,128]{1,0:T(8,128)(2,1)S(1)}, bf16[512,128]{1,0:T(8,128)(2,1)S(1)}, u32[]{:S(2)}, u32[]{:S(2)}) %collective-permute-start.36) | collective-permute-done | bytes 131104 | tf_op jit(solution)/shard_map/ppermute | solution.py:311
  127.9 8.3 %collective-permute-done.37.refs_2_ = bf16[512,128]{1,0:T(8,128)(2,1)S(1)} collective-permute-done((bf16[512,128]{1,0:T(8,128)(2,1)S(1)}, bf16[512,128]{1,0:T(8,128)(2,1)S(1)}, u32[]{:S(2)}, u32[]{:S(2)}) %collective-permute-start.37) | collective-permute-done | bytes 131104 | tf_op jit(solution)/shard_map/ppermute | solution.py:311
  136.2 4.2 %shard_map.81 = bf16[128,8192]{1,0:T(8,128)(2,1)} custom-call(s32[3]{0:T(128)S(1)} %pad_add_fusion.place_ref, s32[64]{0:T(128)S(1)} %copy-done.9, bf16[2048,128]{1,0:T(8,128)(2,1)S(1)} %collective-permute-done.29.back_ref, bf16[512,128]{1,0:T(8,128)(2,1)S(1)} %get-tuple-element.131.refs_0_, bf16[512,128]{1,0:T(8,128)(2,1)S(1)} %collective-permute-done.36.refs_1_, ...), custom_call_target="tpu_custom_call" | custom-call | flops 1000 | bytes 1000 | tf_op jit(solution)/shard_map/pallas_call | solution.py:395
  (99 shorter events, 32.1 us)
Async XLA Ops:
  13.2 15.2 %collective-permute-start.4 = (bf16[512,256]{1,0:T(8,128)(2,1)S(1)}, bf16[512,256]{1,0:T(8,128)(2,1)S(1)}, u32[]{:S(2)}, u32[]{:S(2)}) collective-permute-start(bf16[512,256]{1,0:T(8,128)(2,1)S(1)} %slice.4), channel_id=1, source_target_pairs={{0,8},{1,9},{2,10},{3,11},{4,12},{5,13},{6,14},{7,15},{8,0},{9,1},... | collective-permute-start | bytes 786440 | tf_op jit(solution)/shard_map/ppermute | solution.py:311
  17.4 32.2 %collective-permute-start.6 = (bf16[512,512]{1,0:T(8,128)(2,1)S(1)}, bf16[512,512]{1,0:T(8,128)(2,1)S(1)}, u32[]{:S(2)}, u32[]{:S(2)}) collective-permute-start(bf16[512,512]{1,0:T(8,128)(2,1)S(1)} %constant_dynamic-update-slice_fusion.refs_4_), channel_id=1, source_target_pairs={{0,4},{1,5},{2,6},{3,7},{4,0},{5,1},{6,2},{7,3},{8,12},{9,13},{10,... | collective-permute-start | bytes 1572872 | tf_op jit(solution)/shard_map/ppermute | solution.py:311
  33.6 20.9 %collective-permute-start.7 = (bf16[2048,128]{1,0:T(8,128)(2,1)S(1)}, bf16[2048,128]{1,0:T(8,128)(2,1)S(1)}, u32[]{:S(2)}, u32[]{:S(2)}) collective-permute-start(bf16[2048,128]{1,0:T(8,128)(2,1)S(1)} %get-tuple-element.88), channel_id=1, source_target_pairs={{0,16},{16,0},{1,17},{17,1},{2,18},{18,2},{3,19},{19,3},{4,20},{20... | collective-permute-start | bytes 1572872 | tf_op jit(solution)/shard_map/ppermute | solution.py:318
  35.2 17.8 %collective-permute-start.11 = (bf16[512,256]{1,0:T(8,128)(2,1)S(1)}, bf16[512,256]{1,0:T(8,128)(2,1)S(1)}, u32[]{:S(2)}, u32[]{:S(2)}) collective-permute-start(bf16[512,256]{1,0:T(8,128)(2,1)S(1)} %collective-permute-done.4.refs_6_), channel_id=1, source_target_pairs={{0,4},{1,5},{2,6},{3,7},{4,0},{5,1},{6,2},{7,3},{8,12},{9,13},{10,... | collective-permute-start | bytes 786440 | tf_op jit(solution)/shard_map/ppermute | solution.py:311
  35.9 12.5 %collective-permute-start.5 = (bf16[2,128,128]{2,1,0:T(8,128)(2,1)S(1)}, bf16[2,128,128]{2,1,0:T(8,128)(2,1)S(1)}, u32[]{:S(2)}, u32[]{:S(2)}) collective-permute-start(bf16[2,128,128]{2,1,0:T(8,128)(2,1)S(1)} %get-tuple-element.79), channel_id=1, source_target_pairs={{0,16},{16,0},{1,17},{17,1},{2,18},{18,2},{3,19},{19,3},{4,20},{20... | collective-permute-start | bytes 196616 | tf_op jit(solution)/shard_map/ppermute | solution.py:318
  36.4 20.9 %collective-permute-start.10 = (bf16[512,128]{1,0:T(8,128)(2,1)S(1)}, bf16[512,128]{1,0:T(8,128)(2,1)S(1)}, u32[]{:S(2)}, u32[]{:S(2)}) collective-permute-start(bf16[512,128]{1,0:T(8,128)(2,1)S(1)} %get-tuple-element.96), channel_id=1, source_target_pairs={{0,12},{1,13},{2,14},{3,15},{4,8},{5,9},{6,10},{7,11},{8,4},{9,5},... | collective-permute-start | bytes 393224 | tf_op jit(solution)/shard_map/ppermute | solution.py:311
  48.3 9.0 %collective-permute-start.8 = (bf16[512,128]{1,0:T(8,128)(2,1)S(1)}, bf16[512,128]{1,0:T(8,128)(2,1)S(1)}, u32[]{:S(2)}, u32[]{:S(2)}) collective-permute-start(bf16[512,128]{1,0:T(8,128)(2,1)S(1)} %get-tuple-element.94), channel_id=1, source_target_pairs={{0,4},{1,5},{2,6},{3,7},{4,0},{5,1},{6,2},{7,3},{8,12},{9,13},{10,... | collective-permute-start | bytes 393224 | tf_op jit(solution)/shard_map/ppermute | solution.py:311
  49.6 8.9 %collective-permute-start.9 = (bf16[512,128]{1,0:T(8,128)(2,1)S(1)}, bf16[512,128]{1,0:T(8,128)(2,1)S(1)}, u32[]{:S(2)}, u32[]{:S(2)}) collective-permute-start(bf16[512,128]{1,0:T(8,128)(2,1)S(1)} %get-tuple-element.95), channel_id=1, source_target_pairs={{0,8},{1,9},{2,10},{3,11},{4,12},{5,13},{6,14},{7,15},{8,0},{9,1},... | collective-permute-start | bytes 393224 | tf_op jit(solution)/shard_map/ppermute | solution.py:311
  53.0 9.9 %collective-permute-start.15 = (bf16[512,256]{1,0:T(8,128)(2,1)S(1)}, bf16[512,256]{1,0:T(8,128)(2,1)S(1)}, u32[]{:S(2)}, u32[]{:S(2)}) collective-permute-start(bf16[512,256]{1,0:T(8,128)(2,1)S(1)} %collective-permute-done.4.refs_6_), channel_id=1, source_target_pairs={{0,16},{16,0},{1,17},{17,1},{2,18},{18,2},{3,19},{19,3},{4,20},{20... | collective-permute-start | bytes 786440 | tf_op jit(solution)/shard_map/ppermute | solution.py:318
  54.5 10.9 %collective-permute-start.16 = (bf16[512,256]{1,0:T(8,128)(2,1)S(1)}, bf16[512,256]{1,0:T(8,128)(2,1)S(1)}, u32[]{:S(2)}, u32[]{:S(2)}) collective-permute-start(bf16[512,256]{1,0:T(8,128)(2,1)S(1)} %collective-permute-done.11.refs_7_), channel_id=1, source_target_pairs={{0,16},{16,0},{1,17},{17,1},{2,18},{18,2},{3,19},{19,3},{4,20},{20... | collective-permute-start | bytes 786440 | tf_op jit(solution)/shard_map/ppermute | solution.py:318
  58.5 7.6 %collective-permute-start.12 = (bf16[512,128]{1,0:T(8,128)(2,1)S(1)}, bf16[512,128]{1,0:T(8,128)(2,1)S(1)}, u32[]{:S(2)}, u32[]{:S(2)}) collective-permute-start(bf16[512,128]{1,0:T(8,128)(2,1)S(1)} %get-tuple-element.98), channel_id=1, source_target_pairs={{0,4},{1,5},{2,6},{3,7},{4,0},{5,1},{6,2},{7,3},{8,12},{9,13},{10,... | collective-permute-start | bytes 393224 | tf_op jit(solution)/shard_map/ppermute | solution.py:311
  58.6 11.1 %collective-permute-start.13 = (bf16[512,128]{1,0:T(8,128)(2,1)S(1)}, bf16[512,128]{1,0:T(8,128)(2,1)S(1)}, u32[]{:S(2)}, u32[]{:S(2)}) collective-permute-start(bf16[512,128]{1,0:T(8,128)(2,1)S(1)} %get-tuple-element.99), channel_id=1, source_target_pairs={{0,8},{1,9},{2,10},{3,11},{4,12},{5,13},{6,14},{7,15},{8,0},{9,1},... | collective-permute-start | bytes 393224 | tf_op jit(solution)/shard_map/ppermute | solution.py:311
  61.3 8.4 %collective-permute-start.14 = (bf16[512,128]{1,0:T(8,128)(2,1)S(1)}, bf16[512,128]{1,0:T(8,128)(2,1)S(1)}, u32[]{:S(2)}, u32[]{:S(2)}) collective-permute-start(bf16[512,128]{1,0:T(8,128)(2,1)S(1)} %get-tuple-element.100), channel_id=1, source_target_pairs={{0,12},{1,13},{2,14},{3,15},{4,8},{5,9},{6,10},{7,11},{8,4},{9,5},... | collective-permute-start | bytes 393224 | tf_op jit(solution)/shard_map/ppermute | solution.py:311
  62.9 14.9 %collective-permute-start.20 = (bf16[4,512,128]{2,1,0:T(8,128)(2,1)S(1)}, bf16[4,512,128]{2,1,0:T(8,128)(2,1)S(1)}, u32[]{:S(2)}, u32[]{:S(2)}) collective-permute-start(bf16[4,512,128]{2,1,0:T(8,128)(2,1)S(1)} %pad_maximum_fusion.1.refs_0_), channel_id=1, source_target_pairs={{0,2},{1,3},{2,0},{3,1},{4,6},{5,7},{6,4},{7,5},{8,10},{9,11},{10,... | collective-permute-start | bytes 1572872 | tf_op jit(solution)/shard_map/ppermute | solution.py:311
  69.8 14.4 %collective-permute-start.17 = (bf16[4,512,128]{2,1,0:T(8,128)(2,1)S(1)}, bf16[4,512,128]{2,1,0:T(8,128)(2,1)S(1)}, u32[]{:S(2)}, u32[]{:S(2)}) collective-permute-start(bf16[4,512,128]{2,1,0:T(8,128)(2,1)S(1)} %pad_maximum_fusion.refs_0_), channel_id=1, source_target_pairs={{0,2},{1,3},{2,0},{3,1},{4,6},{5,7},{6,4},{7,5},{8,10},{9,11},{10,... | collective-permute-start | bytes 1572872 | tf_op jit(solution)/shard_map/ppermute | solution.py:311
  73.5 10.7 %collective-permute-start.31 = (bf16[512,128]{1,0:T(8,128)(2,1)S(1)}, bf16[512,128]{1,0:T(8,128)(2,1)S(1)}, u32[]{:S(2)}, u32[]{:S(2)}) collective-permute-start(bf16[512,128]{1,0:T(8,128)(2,1)S(1)} %get-tuple-element.125), channel_id=1, source_target_pairs={{0,8},{1,9},{2,10},{3,11},{4,12},{5,13},{6,14},{7,15},{8,0},{9,1},... | collective-permute-start | bytes 393224 | tf_op jit(solution)/shard_map/ppermute | solution.py:311
  73.6 11.1 %collective-permute-start.32 = (bf16[512,128]{1,0:T(8,128)(2,1)S(1)}, bf16[512,128]{1,0:T(8,128)(2,1)S(1)}, u32[]{:S(2)}, u32[]{:S(2)}) collective-permute-start(bf16[512,128]{1,0:T(8,128)(2,1)S(1)} %get-tuple-element.126), channel_id=1, source_target_pairs={{0,12},{1,13},{2,14},{3,15},{4,8},{5,9},{6,10},{7,11},{8,4},{9,5},... | collective-permute-start | bytes 393224 | tf_op jit(solution)/shard_map/ppermute | solution.py:311
  77.9 7.9 %collective-permute-start.21 = (bf16[4,512,128]{2,1,0:T(8,128)(2,1)S(1)}, bf16[4,512,128]{2,1,0:T(8,128)(2,1)S(1)}, u32[]{:S(2)}, u32[]{:S(2)}) collective-permute-start(bf16[4,512,128]{2,1,0:T(8,128)(2,1)S(1)} %pad_maximum_fusion.1.refs_0_), channel_id=1, source_target_pairs={{0,1},{1,0},{2,3},{3,2},{4,5},{5,4},{6,7},{7,6},{8,9},{9,8},{10,11... | collective-permute-start | bytes 1572872 | tf_op jit(solution)/shard_map/ppermute | solution.py:311
  77.9 7.9 %collective-permute-start.22 = (bf16[4,512,128]{2,1,0:T(8,128)(2,1)S(1)}, bf16[4,512,128]{2,1,0:T(8,128)(2,1)S(1)}, u32[]{:S(2)}, u32[]{:S(2)}) collective-permute-start(bf16[4,512,128]{2,1,0:T(8,128)(2,1)S(1)} %collective-permute-done.20.refs_1_), channel_id=1, source_target_pairs={{0,1},{1,0},{2,3},{3,2},{4,5},{5,4},{6,7},{7,6},{8,9},{9,8},{10,11... | collective-permute-start | bytes 1572872 | tf_op jit(solution)/shard_map/ppermute | solution.py:311
  84.2 8.0 %collective-permute-start.19 = (bf16[4,512,128]{2,1,0:T(8,128)(2,1)S(1)}, bf16[4,512,128]{2,1,0:T(8,128)(2,1)S(1)}, u32[]{:S(2)}, u32[]{:S(2)}) collective-permute-start(bf16[4,512,128]{2,1,0:T(8,128)(2,1)S(1)} %collective-permute-done.17.refs_1_), channel_id=1, source_target_pairs={{0,1},{1,0},{2,3},{3,2},{4,5},{5,4},{6,7},{7,6},{8,9},{9,8},{10,11... | collective-permute-start | bytes 1572872 | tf_op jit(solution)/shard_map/ppermute | solution.py:311
  84.8 19.4 %collective-permute-start.33 = (bf16[4,512,128]{2,1,0:T(8,128)(2,1)S(1)}, bf16[4,512,128]{2,1,0:T(8,128)(2,1)S(1)}, u32[]{:S(2)}, u32[]{:S(2)}) collective-permute-start(bf16[4,512,128]{2,1,0:T(8,128)(2,1)S(1)} %pad_maximum_fusion.2.refs_0_), channel_id=1, source_target_pairs={{0,2},{1,3},{2,0},{3,1},{4,6},{5,7},{6,4},{7,5},{8,10},{9,11},{10,... | collective-permute-start | bytes 1572872 | tf_op jit(solution)/shard_map/ppermute | solution.py:311
  87.7 8.3 %collective-permute-start.23 = (bf16[512,128]{1,0:T(8,128)(2,1)S(1)}, bf16[512,128]{1,0:T(8,128)(2,1)S(1)}, u32[]{:S(2)}, u32[]{:S(2)}) collective-permute-start(bf16[512,128]{1,0:T(8,128)(2,1)S(1)} %get-tuple-element.116), channel_id=1, source_target_pairs={{0,4},{1,5},{2,6},{3,7},{4,0},{5,1},{6,2},{7,3},{8,12},{9,13},{10,... | collective-permute-start | bytes 393224 | tf_op jit(solution)/shard_map/ppermute | solution.py:311
  89.4 12.2 %collective-permute-start.24 = (bf16[512,128]{1,0:T(8,128)(2,1)S(1)}, bf16[512,128]{1,0:T(8,128)(2,1)S(1)}, u32[]{:S(2)}, u32[]{:S(2)}) collective-permute-start(bf16[512,128]{1,0:T(8,128)(2,1)S(1)} %get-tuple-element.117), channel_id=1, source_target_pairs={{0,8},{1,9},{2,10},{3,11},{4,12},{5,13},{6,14},{7,15},{8,0},{9,1},... | collective-permute-start | bytes 393224 | tf_op jit(solution)/shard_map/ppermute | solution.py:311
  90.7 11.5 %collective-permute-start.25 = (bf16[512,128]{1,0:T(8,128)(2,1)S(1)}, bf16[512,128]{1,0:T(8,128)(2,1)S(1)}, u32[]{:S(2)}, u32[]{:S(2)}) collective-permute-start(bf16[512,128]{1,0:T(8,128)(2,1)S(1)} %get-tuple-element.118), channel_id=1, source_target_pairs={{0,12},{1,13},{2,14},{3,15},{4,8},{5,9},{6,10},{7,11},{8,4},{9,5},... | collective-permute-start | bytes 393224 | tf_op jit(solution)/shard_map/ppermute | solution.py:311
  104.2 14.9 %collective-permute-start.34 = (bf16[4,512,128]{2,1,0:T(8,128)(2,1)S(1)}, bf16[4,512,128]{2,1,0:T(8,128)(2,1)S(1)}, u32[]{:S(2)}, u32[]{:S(2)}) collective-permute-start(bf16[4,512,128]{2,1,0:T(8,128)(2,1)S(1)} %pad_maximum_fusion.2.refs_0_), channel_id=1, source_target_pairs={{0,1},{1,0},{2,3},{3,2},{4,5},{5,4},{6,7},{7,6},{8,9},{9,8},{10,11... | collective-permute-start | bytes 1572872 | tf_op jit(solution)/shard_map/ppermute | solution.py:311
  104.2 14.9 %collective-permute-start.35 = (bf16[4,512,128]{2,1,0:T(8,128)(2,1)S(1)}, bf16[4,512,128]{2,1,0:T(8,128)(2,1)S(1)}, u32[]{:S(2)}, u32[]{:S(2)}) collective-permute-start(bf16[4,512,128]{2,1,0:T(8,128)(2,1)S(1)} %collective-permute-done.33.refs_1_), channel_id=1, source_target_pairs={{0,1},{1,0},{2,3},{3,2},{4,5},{5,4},{6,7},{7,6},{8,9},{9,8},{10,11... | collective-permute-start | bytes 1572872 | tf_op jit(solution)/shard_map/ppermute | solution.py:311
  104.7 12.7 %collective-permute-start.27 = (bf16[512,128]{1,0:T(8,128)(2,1)}, bf16[512,128]{1,0:T(8,128)(2,1)S(1)}, u32[]{:S(2)}, u32[]{:S(2)}) collective-permute-start(bf16[512,128]{1,0:T(8,128)(2,1)} %copy-done.14), channel_id=1, source_target_pairs={{0,8},{1,9},{2,10},{3,11},{4,12},{5,13},{6,14},{7,15},{8,0},{9,1},... | collective-permute-start | bytes 393224 | tf_op jit(solution)/shard_map/ppermute | solution.py:311
  106.0 11.4 %collective-permute-start.28 = (bf16[512,128]{1,0:T(8,128)(2,1)}, bf16[512,128]{1,0:T(8,128)(2,1)S(1)}, u32[]{:S(2)}, u32[]{:S(2)}) collective-permute-start(bf16[512,128]{1,0:T(8,128)(2,1)} %copy-done.13), channel_id=1, source_target_pairs={{0,12},{1,13},{2,14},{3,15},{4,8},{5,9},{6,10},{7,11},{8,4},{9,5},... | collective-permute-start | bytes 393224 | tf_op jit(solution)/shard_map/ppermute | solution.py:311
  117.5 18.7 %collective-permute-start.29 = (bf16[2048,128]{1,0:T(8,128)(2,1)S(1)}, bf16[2048,128]{1,0:T(8,128)(2,1)S(1)}, u32[]{:S(2)}, u32[]{:S(2)}) collective-permute-start(bf16[2048,128]{1,0:T(8,128)(2,1)S(1)} %constant_dynamic-update-slice_fusion.4), channel_id=1, source_target_pairs={{0,16},{16,0},{1,17},{17,1},{2,18},{18,2},{3,19},{19,3},{4,20},{20... | collective-permute-start | bytes 1572872 | tf_op jit(solution)/shard_map/ppermute | solution.py:318
  120.9 7.0 %collective-permute-start.36 = (bf16[512,128]{1,0:T(8,128)(2,1)S(1)}, bf16[512,128]{1,0:T(8,128)(2,1)S(1)}, u32[]{:S(2)}, u32[]{:S(2)}) collective-permute-start(bf16[512,128]{1,0:T(8,128)(2,1)S(1)} %get-tuple-element.132), channel_id=1, source_target_pairs={{0,4},{1,5},{2,6},{3,7},{4,0},{5,1},{6,2},{7,3},{8,12},{9,13},{10,... | collective-permute-start | bytes 393224 | tf_op jit(solution)/shard_map/ppermute | solution.py:311
  123.8 12.4 %collective-permute-start.37 = (bf16[512,128]{1,0:T(8,128)(2,1)S(1)}, bf16[512,128]{1,0:T(8,128)(2,1)S(1)}, u32[]{:S(2)}, u32[]{:S(2)}) collective-permute-start(bf16[512,128]{1,0:T(8,128)(2,1)S(1)} %get-tuple-element.133), channel_id=1, source_target_pairs={{0,8},{1,9},{2,10},{3,11},{4,12},{5,13},{6,14},{7,15},{8,0},{9,1},... | collective-permute-start | bytes 393224 | tf_op jit(solution)/shard_map/ppermute | solution.py:311
  124.6 11.5 %collective-permute-start.38 = (bf16[512,128]{1,0:T(8,128)(2,1)S(1)}, bf16[512,128]{1,0:T(8,128)(2,1)S(1)}, u32[]{:S(2)}, u32[]{:S(2)}) collective-permute-start(bf16[512,128]{1,0:T(8,128)(2,1)S(1)} %get-tuple-element.134), channel_id=1, source_target_pairs={{0,12},{1,13},{2,14},{3,15},{4,8},{5,9},{6,10},{7,11},{8,4},{9,5},... | collective-permute-start | bytes 393224 | tf_op jit(solution)/shard_map/ppermute | solution.py:311
  (22 other events, 188.7 us)

commit v2 on v1

--- a/solution.py
+++ b/solution.py
@@ -9,23 +9,26 @@
 
 HB = 2
 EDGE = 2 * HB
+GROUP = 8
 PLANE = 4
+ORDER = (0, 2, 3, 1)
 VMEM = pl.BlockSpec(memory_space=pltpu.VMEM)
+HBM = pl.BlockSpec(memory_space=pltpu.HBM)
 SMEM = pl.BlockSpec(memory_space=pltpu.SMEM)
-COST = pl.CostEstimate(flops=1000, bytes_accessed=1000, transcendentals=0)
-PARAMS = pltpu.CompilerParams(vmem_limit_bytes=36 * 1024 * 1024)
+MIB = 1024 * 1024
 f32, bf16 = jnp.float32, jnp.bfloat16
 
 
-def call(body, out_shape, in_specs, scratch_shapes=()):
+def call(body, limit, out_shape, in_specs, scratch_shapes=(), moved=1000, out_specs=None, **options):
     return pl.pallas_call(
         body,
         out_shape=out_shape,
         in_specs=in_specs,
-        out_specs=jax.tree.map(lambda _: VMEM, out_shape),
+        out_specs=out_specs or jax.tree.map(lambda _: VMEM, out_shape),
         scratch_shapes=scratch_shapes,
-        compiler_params=PARAMS,
-        cost_estimate=COST,
+        compiler_params=pltpu.CompilerParams(vmem_limit_bytes=limit * MIB),
+        cost_estimate=pl.CostEstimate(flops=1000, bytes_accessed=moved, transcendentals=0),
+        **options,
     )
 
 
@@ -75,27 +78,44 @@
     return total
 
 
-def start_kernel(groups, place_ref, x_ref, rotation_ref, halo_ref, *piece_refs):
+def start_kernel(groups, place_ref, x_ref, rotation_ref, halo_ref, xt_ref, *refs):
+    pieces, sems = refs[:-1], refs[-1]
     width = halo_ref.shape[1]
     z, slab, p = place_ref[0], place_ref[1], place_ref[2]
     begin = jnp.where(slab == 0, x_ref.shape[1] - width, 0)
-    halo_ref[...] = x_ref[:, pl.ds(pl.multiple_of(begin, width), width)]
-    lanes = piece_refs[0].shape[1] // groups
+    begin = pl.multiple_of(begin, width)
+    copies = [pltpu.make_async_copy(x_ref.at[:, pl.ds(begin, width)], halo_ref, sems.at[0])]
+    lanes = pieces[0].shape[1] // groups
     half = groups // 2
-    for q, ref in enumerate(piece_refs):
+    for q, ref in enumerate(pieces):
         for h in range(2):
             for g in range(half):
                 block = ((slab ^ h) * half + g) * PLANE + (p ^ q)
                 begin = pl.multiple_of(block * lanes, lanes)
-                ref[:, (h * half + g) * lanes:(h * half + g + 1) * lanes] = rotation_ref[
-                    :, pl.ds(begin, lanes)
-                ]
-
-
-def multiply(blocks, rows_ref, cols_ref, tiles_ref, source_ref, acc_ref, extra_ref, first=None):
+                at = (h * half + g) * lanes
+                copies.append(
+                    pltpu.make_async_copy(
+                        rotation_ref.at[:, pl.ds(begin, lanes)],
+                        ref.at[:, at:at + lanes],
+                        sems.at[len(copies)],
+                    )
+                )
+    for copy in copies:
+        copy.start()
+    blocks, tile = xt_ref.shape[:2]
+
+    def turn(r, _):
+        xt_ref[r] = x_ref[:, pl.ds(pl.multiple_of(r * tile, tile), tile)].T
+        return 0
+
+    loop(0, blocks, turn, 16)
+    for copy in copies:
+        copy.wait()
+
+
+def multiply(blocks, rows_ref, cols_ref, tiles_ref, source_ref, acc_ref, extra_ref):
     def diagonal(r, _):
-        block = source_ref[r] if first is None else first(r)
-        acc_ref[r] = product(tiles_ref[r], block)
+        acc_ref[r] = product(tiles_ref[r], source_ref[r])
         return 0
 
     loop(0, blocks, diagonal, 16)
@@ -109,13 +129,11 @@
     loop(blocks, listed, extra, 16)
 
     def gather(k, _):
-        @pl.when((cols_ref[k] >= 0) & (cols_ref[k] < blocks))
-        def _():
-            acc_ref[rows_ref[k]] += extra_ref[k - blocks]
-
+        inside = (cols_ref[k] >= 0) & (cols_ref[k] < blocks)
+        acc_ref[jnp.where(inside, rows_ref[k], blocks)] += extra_ref[k - blocks]
         return 0
 
-    loop(blocks, listed, gather, 4)
+    loop(blocks, listed, gather, 8)
 
 
 def multiply_edges(blocks, slab, rows_ref, cols_ref, tiles_ref, halo_ref, add):
@@ -133,18 +151,12 @@
 
 
 def first_kernel(
-    blocks, place_ref, rows_ref, cols_ref, counts_ref, bounds_ref, x_ref, halo_ref, tiles_ref,
-    f1_ref, edge_ref, xt_ref, acc_ref, extra_ref, ext_ref,
+    blocks, place_ref, rows_ref, cols_ref, counts_ref, bounds_ref, xt_ref, halo_ref, tiles_ref,
+    f1_ref, edge_ref, acc_ref, extra_ref, ext_ref,
 ):
-    tile = tiles_ref.shape[1]
-    lanes = x_ref.shape[0]
+    tile, lanes = xt_ref.shape[1:]
     slab = place_ref[1]
-
-    def turn(r):
-        xt_ref[r] = x_ref[:, pl.ds(pl.multiple_of(r * tile, tile), tile)].T
-        return xt_ref[r]
-
-    multiply(blocks, rows_ref, cols_ref, tiles_ref, xt_ref, acc_ref, extra_ref, turn)
+    multiply(blocks, rows_ref, cols_ref, tiles_ref, xt_ref, acc_ref, extra_ref)
     for b in range(HB):
         ext_ref[b] = halo_ref[:, b * tile:(b + 1) * tile].T
 
@@ -174,7 +186,7 @@
 
 def split_parts(outs, place_ref, packed_ref, base):
     part = outs[0].shape[0]
-    for s, out in enumerate(outs):
+    for s, out in zip(ORDER, outs):
         start = pl.multiple_of(base + (place_ref[0] ^ s) * part, 16)
         out[...] = packed_ref[pl.ds(start, part)].astype(bf16)
 
@@ -240,48 +252,137 @@
     split_parts(outs, place_ref, packed_ref, 0)
 
 
-def rotate_kernel(groups, place_ref, *refs):
-    own, over_x, over_core, over_both = refs[:4]
-    mine, near, far_two, far_three, other_two, other_three = refs[4:10]
-    outs, turned = refs[10:10 + groups], refs[-1]
+def rotate_kernel(
+    groups, place_ref, own, over_x, core, mine, near, far_two, far_three, near_more, other_ref, *refs
+):
+    outs, turned = refs[:groups], refs[groups]
     width = outs[0].shape[1]
     half = groups // 2 * width
     lhs = jnp.concatenate(
-        [ref[s] for s in range(groups) for ref in (own, over_core, over_x, over_both)], axis=1
+        [part for s in range(groups) for part in (own[s], core[0, s], over_x[s], core[1, s])], axis=1
     )
+
+    def wide(ref, at=0):
+        rows = mine.shape[0]
+        return jnp.concatenate(
+            [ref[(at + i) * rows:(at + i + 1) * rows] for i in range(groups // 2)], axis=1
+        )
+
     for h in range(2):
-        far = (far_two, far_three) if h == 0 else (other_two, other_three)
-        rhs = [ref[:, h * half:(h + 1) * half] for ref in (mine, near)] + [ref[...] for ref in far]
-        total = product(lhs, jnp.concatenate(rhs, axis=0)).astype(bf16)
+        if h == 0:
+            rhs = [far_two[...], wide(far_three), near[...]]
+        else:
+            rhs = [wide(other_ref), wide(other_ref, groups // 2), wide(near_more)]
+        rhs = jnp.concatenate([mine[:, h * half:(h + 1) * half]] + rhs, axis=0)
+        total = product(lhs, rhs).astype(bf16)
         first = (place_ref[1] ^ h) * (groups // 2)
         for z in range(groups // 2):
             turned[first + z] = total[:, z * width:(z + 1) * width]
-    for s in range(groups):
-        outs[s][...] = turned[place_ref[0] ^ s]
-
-
-def spread_kernel(blocks, groups, place_ref, counts_ref, back_ref, *refs):
-    parts, out_ref, packed_ref = refs[:-2], refs[-2], refs[-1]
-    part, width = parts[0].shape
+    for s, out in zip(ORDER, outs):
+        out[...] = turned[place_ref[0] ^ s]
+
+
+def spread(blocks, tile, counts_ref, cases, block_ref, out_hbm, sems):
+    def copy(b):
+        there = out_hbm.at[:, pl.ds(pl.multiple_of(b * tile, tile), tile)]
+        return pltpu.make_async_copy(block_ref.at[b], there, sems.at[b])
+
+    def each(act):
+        def some(g, offset):
+            places = []
+            for i in range(g * GROUP, (g + 1) * GROUP):
+                b = edge_row(i, blocks) if i < EDGE else i - HB
+                places.append((b, offset, offset + counts_ref[b]))
+                offset = places[-1][2]
+            for wanted, source in cases:
+                flags = [wanted(begin, end) for _, begin, end in places]
+
+                @pl.when(functools.reduce(jnp.logical_or, flags))
+                def _():
+                    act(places, flags, source)
+
+            return offset
+
+        offset = 0
+        for g in range(blocks // GROUP):
+            offset = some(g, offset)
+
+    def write(places, flags, source):
+        for b, begin, _ in places:
+            rows = source(begin)
+            rows = jnp.where(live_mask(tile, rows.shape[1], counts_ref[b]), rows, 0.0).astype(bf16)
+            block_ref[b] = rows.T
+        for (b, _, _), flag in zip(places, flags):
+            @pl.when(flag)
+            def _():
+                copy(b).start()
+
+    def wait(places, flags, source):
+        for (b, _, _), flag in zip(places, flags):
+            @pl.when(flag)
+            def _():
+                copy(b).wait()
+
+    each(write)
+    each(wait)
+
+
+def spread_kernel(blocks, groups, place_ref, counts_ref, *refs):
+    parts, (out_hbm, seam_ref, packed_ref, block_ref, sems) = refs[:-5], refs[-5:]
+    part = parts[0].shape[0]
     size = part * groups
-    tile = out_ref.shape[1] // blocks
+    tile = block_ref.shape[1]
+    for i in range(2):
+        for j, s in enumerate(ORDER):
+            start = pl.multiple_of((i * groups + (place_ref[0] ^ s)) * part, 16)
+            packed_ref[pl.ds(start, part)] = parts[i * groups + j][...].astype(f32)
+    seam_ref[0] = packed_ref[:tile]
+    seam_ref[1] = packed_ref[2 * size - tile:2 * size]
+
+    def wanted(begin, end):
+        return (begin >= size) & (end <= 3 * size)
+
+    def source(begin):
+        return packed_ref[pl.ds(jnp.clip(begin - size, 0, 2 * size), tile)]
+
+    spread(blocks, tile, counts_ref, [(wanted, source)], block_ref, out_hbm, sems)
+
+
+def spread_rest_kernel(blocks, groups, place_ref, counts_ref, done_hbm, seam_ref, back_ref, *refs):
+    parts, (out_hbm, packed_ref, far_ref, block_ref, sems) = refs[:-5], refs[-5:]
+    part = parts[0].shape[0]
+    size = part * groups
+    tile = block_ref.shape[1]
+    for j, s in enumerate(ORDER):
+        start = pl.multiple_of((place_ref[0] ^ s) * part, 16)
+        packed_ref[pl.ds(start, part)] = parts[j][...].astype(f32)
+    packed_ref[size:] = seam_ref[0]
     live = sum_counts(counts_ref, range(blocks))
-    packed_ref[pl.ds(jnp.clip(live - size, 2 * size, 3 * size), size)] = back_ref[...].astype(f32)
-    for i in range(3):
-        for s in range(groups):
-            start = pl.multiple_of((i * groups + (place_ref[0] ^ s)) * part, 16)
-            packed_ref[pl.ds(start, part)] = parts[i * groups + s][...].astype(f32)
-
-    def one(b, offset):
-        rows = packed_ref[pl.ds(offset, tile)]
-        rows = jnp.where(live_mask(tile, width, counts_ref[b]), rows, 0.0)
-        out_ref[:, pl.ds(pl.multiple_of(b * tile, tile), tile)] = rows.T.astype(bf16)
-        return offset + counts_ref[b]
-
-    offset = 0
-    for e in range(EDGE):
-        offset = one(edge_row(e, blocks), offset)
-    loop(HB, blocks - HB, one, 4, offset)
+
+    @pl.when(live > 3 * size)
+    def _():
+        base = jnp.clip(live - 3 * size, 0, size)
+        for j, s in enumerate(ORDER):
+            far_ref[pl.ds(base + (place_ref[0] ^ s) * part, part)] = back_ref[
+                j * part:(j + 1) * part
+            ].astype(f32)
+
+    far_ref[size - tile:size] = seam_ref[1]
+
+    def near(begin, end):
+        return begin < size
+
+    def near_source(begin):
+        return packed_ref[pl.ds(jnp.minimum(begin, size), tile)]
+
+    def far(begin, end):
+        return end > 3 * size
+
+    def far_source(begin):
+        return far_ref[pl.ds(jnp.clip(begin - 2 * size, 0, 2 * size), tile)]
+
+    cases = [(near, near_source), (far, far_source)]
+    spread(blocks, tile, counts_ref, cases, block_ref, out_hbm, sems)
 
 
 def paired(orbitals_t, tiles, tile_rows, tile_cols, row_counts, bounds, rotation):
@@ -311,93 +412,146 @@
         return lax.ppermute(value, "orb", [(i, i ^ bits) for i in range(orbs)])
 
     def over_z(values):
-        moved = {s: swap(values[s], s * PLANE) for s in (2, 3, 1)}
-        return [values[0], moved[1], moved[2], moved[3]]
+        return [swap(v, s * PLANE) if s else v for s, v in zip(ORDER, values)]
 
     def other_slab(value):
         return lax.ppermute(value, "slab", [(0, 1), (1, 0)])
 
     half = groups // 2 * norb_dev
-    halo, *pieces = call(
+    halo, xt, *pieces = call(
         functools.partial(start_kernel, groups),
-        [shaped((norb_dev, HB * tile))] + [shaped((norb_dev, 2 * half))] * PLANE,
-        [SMEM] + [VMEM] * 2,
+        20,
+        [shaped((norb_dev, HB * tile)), shaped(block_shape)]
+        + [shaped((norb_dev, 2 * half))] * PLANE,
+        [SMEM, VMEM, HBM],
+        [pltpu.SemaphoreType.DMA((1 + PLANE * groups,))],
+        moved=20 * MIB,
     )(place, orbitals_t, rotation)
     halo = other_slab(halo)
     mine = [pieces[0]] + [swap(pieces[q], q) for q in range(1, PLANE)]
-    mine = jnp.concatenate(mine, axis=0)
+    mine = jnp.concatenate(after(mine, halo), axis=0)
     far_two = swap(mine[:, :half], 2 * PLANE)
-    near = swap(mine, PLANE)
-
-    f1, edge, xt = call(
+    near = swap(mine[:, :half], PLANE)
+    f1, edge = call(
         functools.partial(first_kernel, blocks),
-        [shaped(block_shape), shaped(halo_shape), shaped(block_shape)],
+        16,
+        [shaped(block_shape), shaped(halo_shape)],
         [SMEM] * 5 + [VMEM] * 3,
-        [pltpu.VMEM(block_shape, f32), pltpu.VMEM(extra_shape, f32), pltpu.VMEM(halo_shape, bf16)],
-    )(*lists, orbitals_t, halo, tiles)
+        [
+            pltpu.VMEM((blocks + 1, tile, norb_dev), f32),
+            pltpu.VMEM(extra_shape, f32),
+            pltpu.VMEM(halo_shape, bf16),
+        ],
+    )(*lists, xt, halo, tiles)
     halo = other_slab(edge)
 
     *first_parts, shared, excess, rest, edge_sum = call(
         functools.partial(second_kernel, blocks, groups),
+        18,
         part_outs
         + [shaped(size_shape)] * 2 + [shaped(size_shape, f32), shaped(edge_shape, f32)],
         [SMEM] * 5 + [VMEM] * 3,
         [
-            pltpu.VMEM(block_shape, f32),
+            pltpu.VMEM((blocks + 1, tile, norb_dev), f32),
             pltpu.VMEM(extra_shape, f32),
             pltpu.VMEM((rows_dev + tile, norb_dev), f32),
         ],
-    )(*lists, after(f1, far_two), xt, tiles)
+    )(*lists, f1, xt, tiles)
+
+    def together(*values):
+        return lax.optimization_barrier(values)
+
+    def over_core(own, over_x):
+        return swap(jnp.stack([own, over_x]), 1)
+
+    def rotate(*gathered):
+        return call(
+            functools.partial(rotate_kernel, groups),
+            12,
+            part_outs,
+            [SMEM] + [VMEM] * (3 + len(weights)),
+            [pltpu.VMEM((groups, part, norb_dev), bf16)],
+        )(place, *gathered, *weights)
+
+    excess, halo, first_parts, near, far_two = together(excess, halo, first_parts, near, far_two)
     excess = other_slab(excess)
-    whole_first = over_z(first_parts)
-    rest_parts = call(
-        functools.partial(second_edge_kernel, blocks, groups),
-        part_outs,
-        [SMEM] * 5 + [VMEM] * 6,
-        [pltpu.VMEM(edge_shape, f32), pltpu.VMEM(size_shape, f32)],
-    )(*lists, halo, f1, xt, tiles, edge_sum, after(rest, near))
-    shared = after(shared, rest_parts)
+    columns = [far_two[:, i * norb_dev:(i + 1) * norb_dev] for i in range(groups // 2)]
+    first = over_z([*first_parts[:3], jnp.concatenate([first_parts[3]] + columns)])
     shared_parts = call(
         functools.partial(merge_kernel, blocks, groups),
+        8,
         part_outs,
         [SMEM] * 2 + [VMEM] * 2,
         [pltpu.VMEM((2 * size, norb_dev), f32)],
     )(place, row_counts, shared, excess)
-    far_three = swap(far_two, PLANE)
-    shared_parts = after(shared_parts, whole_first, far_three)
-    weights = [mine, near, far_two, far_three, other_slab(far_two), other_slab(far_three)]
-
-    def gather(whole):
-        own = jnp.stack(whole)
-        over_x = swap(own, 2)
-        return own, over_x, swap(own, 1), swap(over_x, 1)
-
-    def rotate(gathered):
-        return call(
-            functools.partial(rotate_kernel, groups),
-            part_outs,
-            [SMEM] + [VMEM] * (4 + len(weights)),
-            [pltpu.VMEM((groups, part, norb_dev), bf16)],
-        )(place, *gathered, *weights)
-
-    whole_shared = over_z(shared_parts)
-    whole_rest = over_z(after(rest_parts, whole_shared))
-    whole_shared, weights = lax.optimization_barrier((whole_shared, weights))
-    first_back = over_z(rotate(gather(whole_first)))
-    shared_back = over_z(after(rotate(gather(whole_shared)), first_back))
-    rest_back = over_z(after(rotate(gather(whole_rest)), shared_back))
-    back = jnp.concatenate([jnp.zeros_like(v) for v in shared_back])
-    for s, v in enumerate(shared_back):
-        back = lax.dynamic_update_slice_in_dim(back, v, (z ^ s) * part, 0)
-    back = other_slab(back)
-
-    returned = rest_back + first_back + shared_back
+
+    first, shared_parts, rest = together(first, shared_parts, rest)
+    far_three, first[3] = first[3][part:], first[3][:part]
+    columns_near = [mine[:, half + i * norb_dev:half + (i + 1) * norb_dev] for i in range(groups // 2)]
+    shared = over_z([*shared_parts[:3], jnp.concatenate([shared_parts[3]] + columns_near)])
+    first_own = jnp.stack(first)
+    first_x = swap(first_own, 2)
+    others = other_slab(jnp.concatenate(columns + [far_three]))
+    rest_parts = call(
+        functools.partial(second_edge_kernel, blocks, groups),
+        8,
+        part_outs,
+        [SMEM] * 5 + [VMEM] * 6,
+        [pltpu.VMEM(edge_shape, f32), pltpu.VMEM(size_shape, f32)],
+    )(*lists, halo, f1, xt, tiles, edge_sum, rest)
+
+    shared, first_x, rest_parts, others = together(shared, first_x, rest_parts, others)
+    near_more, shared[3] = shared[3][part:], shared[3][:part]
+    rest = over_z(rest_parts)
+    first_core = over_core(first_own, first_x)
+    shared_own = jnp.stack(shared)
+    shared_x = swap(shared_own, 2)
+    weights = [mine, near, far_two, far_three, near_more, others]
+    first_turned = rotate(first_own, first_x, first_core)
+
+    rest, first_turned, shared_x = together(rest, first_turned, shared_x)
+    first_back = over_z(first_turned)
+    shared_core = over_core(shared_own, shared_x)
+    rest_own = jnp.stack(rest)
+    rest_x = swap(rest_own, 2)
+    shared_turned = rotate(shared_own, shared_x, shared_core)
+
+    first_back, shared_turned, rest_x = together(first_back, shared_turned, rest_x)
+    shared_back = over_z(shared_turned)
+    rest_core = over_core(rest_own, rest_x)
+    rest_turned = rotate(rest_own, rest_x, rest_core)
+
+    shared_back, rest_turned = together(shared_back, rest_turned)
+    rest_back = over_z(rest_turned)
+    back = other_slab(jnp.concatenate(shared_back))
+    width_shape = (blocks, norb_dev, tile)
+    out = shaped((norb_dev, rows_dev))
+    done, seam = call(
+        functools.partial(spread_kernel, blocks, groups),
+        12,
+        [out, shaped((2, tile, norb_dev), f32)],
+        [SMEM] * 2 + [VMEM] * (2 * groups),
+        [
+            pltpu.VMEM((2 * size + tile, norb_dev), f32),
+            pltpu.VMEM(width_shape, bf16),
+            pltpu.SemaphoreType.DMA((blocks,)),
+        ],
+        out_specs=[HBM, VMEM],
+    )(place, row_counts, *first_back, *shared_back)
     return call(
-        functools.partial(spread_kernel, blocks, groups),
-        shaped((norb_dev, rows_dev)),
-        [SMEM] * 2 + [VMEM] * (1 + len(returned)),
-        [pltpu.VMEM((rows_dev + 2 * tile, norb_dev), f32)],
-    )(place, row_counts, back, *returned)
+        functools.partial(spread_rest_kernel, blocks, groups),
+        12,
+        out,
+        [SMEM] * 2 + [HBM] + [VMEM] * (2 + groups),
+        [
+            pltpu.VMEM((size + tile, norb_dev), f32),
+            pltpu.VMEM((2 * size + tile, norb_dev), f32),
+            pltpu.VMEM(width_shape, bf16),
+            pltpu.SemaphoreType.DMA((blocks,)),
+        ],
+        out_specs=HBM,
+        input_output_aliases={2: 0},
+    )(place, row_counts, done, seam, back, *rest_back)
 
 
 def with_halo(block, sides, width):

time: 141 us -> 126 us (0.89)
  starting transfers between devices: 51.6 us -> 43.1 us
  waiting for transfers between devices: 57.8 us -> 53.8 us
  local copies, waits for them, and re-layouts: 6.11 us -> 2.81 us
    ppermute x33 -> x29, starting transfers between devices: 44.3 us -> 36.1 us  [swap(): return lax.ppermute(value, 'orb', [(i, i ^ bits) for i in range(orbs)])]
    unnamed x33 -> x17, local copies, waits for them, and re-layouts: 5.93 us -> 2.69 us
    ppermute x6 -> x5, waiting for transfers between devices: 11.2 us -> 9.15 us  [other_slab(): return lax.ppermute(value, 'slab', [(0, 1), (1, 0)])]
    ppermute x33 -> x29, waiting for transfers between devices: 46.6 us -> 44.7 us  [swap(): return lax.ppermute(value, 'orb', [(i, i ^ bits) for i in range(orbs)])]
    pallas_call x9 -> x10, Pallas kernels: 24.4 us -> 24.7 us  [the longest x3 5.54 us: rotate(): call(functools.partial(rotate_kernel, groups), 12, part_outs, [SMEM] + [V...]
    ppermute x6 -> x5, starting transfers between devices: 7.25 us -> 7.01 us  [other_slab(): return lax.ppermute(value, 'slab', [(0, 1), (1, 0)])]
  transfers between devices with their start and end apart: 39 -> 34, of which waited for: 16 -> 18; matrix products, arithmetic and copies ran while one was open for 0% -> 0% of each run, Pallas kernels for 14% -> 16%
where the time goes in v2:
time: 126 us; the launch traced here: 125 us
  waiting for transfers between devices  53.8 us (43%)
  starting transfers between devices  43.1 us (34%)
  Pallas kernels  24.7 us (20%)
  local copies, waits for them, and re-layouts  2.81 us (2%)
    ppermute x29, waiting for transfers between devices, swap(): return lax.ppermute(value, 'orb', [(i, i ^ bits) for i in range(orbs)])  44.7 us
    ppermute x29, starting transfers between devices, swap(): return lax.ppermute(value, 'orb', [(i, i ^ bits) for i in range(orbs)])  36.1 us
    ppermute x5, waiting for transfers between devices, other_slab(): return lax.ppermute(value, 'slab', [(0, 1), (1, 0)])  9.15 us
    ppermute x5, starting transfers between devices, other_slab(): return lax.ppermute(value, 'slab', [(0, 1), (1, 0)])  7.01 us
    pallas_call x3, Pallas kernels, rotate(): call(functools.partial(rotate_kernel, groups), 12, part_outs, [SMEM] + [V...  5.54 us
    pallas_call x1, Pallas kernels, paired(): call(functools.partial(second_kernel, blocks, groups), 18, part_outs + [s...  4.9 us
    pallas_call x1, Pallas kernels, paired(): call(functools.partial(first_kernel, blocks), 16, [shaped(block_shape), s...  4.9 us
    pallas_call x1, Pallas kernels, paired(): call(functools.partial(spread_kernel, blocks, groups), 12, [out, shaped((...  2.78 us
  transfers between devices with their start and end apart: 34, of which 18 were waited for; matrix products, arithmetic and copies ran while one was open for 0% of the time, Pallas kernels for 16%

profile of v2, /device:TPU:0, one launch (start us, length us, event | category | flops | bytes accessed | tf_op | source)
XLA Modules:
  0.0 125.5 jit_solution(16307997072610040932)
XLA Ops:
  2.7 1.7 %shard_map.73 = (bf16[128,256]{1,0:T(8,128)(2,1)S(1)}, bf16[64,128,128]{2,1,0:T(8,128)(2,1)S(1)}, bf16[128,512]{1,0:T(8,128)(2,1)S(1)}, bf16[128,512]{1,0:T(8,12...) custom-call(s32[3]{0:T(128)S(1)} %pad_add_fusion.place_ref, bf16[128,8192]{1,0:T(8,128)(2,1)S(1)} %copy-done.1, ...), custom_call_target="tpu_custom_call" | custom-call | flops 1000 | bytes 20971520 | tf_op jit(solution)/shard_map/pallas_call | solution.py:421
  5.0 2.6 %collective-permute-start.3 = (bf16[128,512]{1,0:T(8,128)(2,1)S(1)}, bf16[128,512]{1,0:T(8,128)(2,1)S(1)}, u32[]{:S(2)}, u32[]{:S(2)}) collective-permute-start(bf16[128,512]{1,0:T(8,128)(2,1)S(1)} %get-tuple-element.111), channel_id=1, source_target_pairs={{0,2},{1,3},{2,0},{3,1},{4,6},{5,7},{6,4},{7,5},{8,10},{9,11},{10,... | collective-permute-start | bytes 393224 | tf_op jit(solution)/shard_map/ppermute | solution.py:412
  7.6 1.8 %collective-permute-start = (bf16[128,256]{1,0:T(8,128)(2,1)S(1)}, bf16[128,256]{1,0:T(8,128)(2,1)S(1)}, u32[]{:S(2)}, u32[]{:S(2)}) collective-permute-start(bf16[128,256]{1,0:T(8,128)(2,1)S(1)} %get-tuple-element.101), channel_id=1, source_target_pairs={{0,16},{16,0},{1,17},{17,1},{2,18},{18,2},{3,19},{19,3},{4,20},{20... | collective-permute-start | bytes 196616 | tf_op jit(solution)/shard_map/ppermute | solution.py:418
  9.4 2.6 %collective-permute-done.halo_ref = bf16[128,256]{1,0:T(8,128)(2,1)S(1)} collective-permute-done((bf16[128,256]{1,0:T(8,128)(2,1)S(1)}, bf16[128,256]{1,0:T(8,128)(2,1)S(1)}, u32[]{:S(2)}, u32[]{:S(2)}) %collective-permute-start) | collective-permute-done | bytes 65568 | tf_op jit(solution)/shard_map/ppermute | solution.py:418
  12.0 2.2 %collective-permute-done.4 = bf16[128,512]{1,0:T(8,128)(2,1)S(1)} collective-permute-done((bf16[128,512]{1,0:T(8,128)(2,1)S(1)}, bf16[128,512]{1,0:T(8,128)(2,1)S(1)}, u32[]{:S(2)}, u32[]{:S(2)}) %collective-permute-start.4) | collective-permute-done | bytes 131104 | tf_op jit(solution)/shard_map/ppermute | solution.py:412
  14.3 1.7 %collective-permute-start.5 = (bf16[512,256]{1,0:T(8,128)(2,1)S(1)}, bf16[512,256]{1,0:T(8,128)(2,1)S(1)}, u32[]{:S(2)}, u32[]{:S(2)}) collective-permute-start(bf16[512,256]{1,0:T(8,128)(2,1)S(1)} %slice.37), channel_id=1, source_target_pairs={{0,4},{1,5},{2,6},{3,7},{4,0},{5,1},{6,2},{7,3},{8,12},{9,13},{10,... | collective-permute-start | bytes 786440 | tf_op jit(solution)/shard_map/ppermute | solution.py:412
  16.0 2.6 %collective-permute-start.6 = (bf16[512,256]{1,0:T(8,128)(2,1)S(1)}, bf16[512,256]{1,0:T(8,128)(2,1)S(1)}, u32[]{:S(2)}, u32[]{:S(2)}) collective-permute-start(bf16[512,256]{1,0:T(8,128)(2,1)S(1)} %slice.37), channel_id=1, source_target_pairs={{0,8},{1,9},{2,10},{3,11},{4,12},{5,13},{6,14},{7,15},{8,0},{9,1},... | collective-permute-start | bytes 786440 | tf_op jit(solution)/shard_map/ppermute | solution.py:412
  18.6 4.9 %shard_map.74 = (bf16[64,128,128]{2,1,0:T(8,128)(2,1)S(1)}, bf16[2,128,128]{2,1,0:T(8,128)(2,1)S(1)}) custom-call(s32[3]{0:T(128)S(1)} %pad_add_fusion.place_ref, s32[112]{0:T(128)S(1)} %copy-done.4, s32[112]{0:T(128)S(1)} %copy-done.5, s32[64]{0:T(128)S(1)} %copy-done.3, f32[3]{0:T(128)S(1)} %copy-done.6, ...), custom_call_target="tpu_custom_call" | custom-call | flops 1000 | bytes 1000 | tf_op jit(solution)/shard_map/pallas_call | solution.py:435
  25.1 4.9 %shard_map.75 = (bf16[512,128]{1,0:T(8,128)(2,1)S(1)}, bf16[512,128]{1,0:T(8,128)(2,1)S(1)}, bf16[512,128]{1,0:T(8,128)(2,1)S(1)}, bf16[512,128]{1,0:T(8,128)(2,...) custom-call(s32[3]{0:T(128)S(1)} %pad_add_fusion.place_ref, ...), custom_call_target="tpu_custom_call" | custom-call | flops 1000 | bytes 1000 | tf_op jit(solution)/shard_map/pallas_call | solution.py:448
  32.8 2.6 %collective-permute-start.7 = (bf16[512,128]{1,0:T(8,128)(2,1)S(1)}, bf16[512,128]{1,0:T(8,128)(2,1)S(1)}, u32[]{:S(2)}, u32[]{:S(2)}) collective-permute-start(bf16[512,128]{1,0:T(8,128)(2,1)S(1)} %get-tuple-element.118), channel_id=1, source_target_pairs={{0,8},{1,9},{2,10},{3,11},{4,12},{5,13},{6,14},{7,15},{8,0},{9,1},... | collective-permute-start | bytes 393224 | tf_op jit(solution)/shard_map/ppermute | solution.py:412
  36.8 6.5 %collective-permute-done.10.excess_ref = bf16[2048,128]{1,0:T(8,128)(2,1)S(1)} collective-permute-done((bf16[2048,128]{1,0:T(8,128)(2,1)S(1)}, bf16[2048,128]{1,0:T(8,128)(2,1)S(1)}, u32[]{:S(2)}, u32[]{:S(2)}) %collective-permute-start.10) | collective-permute-done | bytes 524320 | tf_op jit(solution)/shard_map/ppermute | solution.py:418
  44.7 3.9 %collective-permute-done.8 = bf16[512,128]{1,0:T(8,128)(2,1)S(1)} collective-permute-done((bf16[512,128]{1,0:T(8,128)(2,1)S(1)}, bf16[512,128]{1,0:T(8,128)(2,1)S(1)}, u32[]{:S(2)}, u32[]{:S(2)}) %collective-permute-start.8) | collective-permute-done | bytes 131104 | tf_op jit(solution)/shard_map/ppermute | solution.py:412
  51.1 2.3 %collective-permute-start.11 = (bf16[512,128]{1,0:T(8,128)(2,1)S(1)}, bf16[512,128]{1,0:T(8,128)(2,1)S(1)}, u32[]{:S(2)}, u32[]{:S(2)}) collective-permute-start(bf16[512,128]{1,0:T(8,128)(2,1)S(1)} %get-tuple-element.130), channel_id=1, source_target_pairs={{0,8},{1,9},{2,10},{3,11},{4,12},{5,13},{6,14},{7,15},{8,0},{9,1},... | collective-permute-start | bytes 393224 | tf_op jit(solution)/shard_map/ppermute | solution.py:412
  53.4 2.1 %collective-permute-start.12 = (bf16[512,128]{1,0:T(8,128)(2,1)S(1)}, bf16[512,128]{1,0:T(8,128)(2,1)S(1)}, u32[]{:S(2)}, u32[]{:S(2)}) collective-permute-start(bf16[512,128]{1,0:T(8,128)(2,1)S(1)} %get-tuple-element.131), channel_id=1, source_target_pairs={{0,12},{1,13},{2,14},{3,15},{4,8},{5,9},{6,10},{7,11},{8,4},{9,5},... | collective-permute-start | bytes 393224 | tf_op jit(solution)/shard_map/ppermute | solution.py:412
  57.0 4.5 %collective-permute-done.11 = bf16[512,128]{1,0:T(8,128)(2,1)S(1)} collective-permute-done((bf16[512,128]{1,0:T(8,128)(2,1)S(1)}, bf16[512,128]{1,0:T(8,128)(2,1)S(1)}, u32[]{:S(2)}, u32[]{:S(2)}) %collective-permute-start.11) | collective-permute-done | bytes 131104 | tf_op jit(solution)/shard_map/ppermute | solution.py:412
  61.5 3.6 %collective-permute-done.12 = bf16[512,128]{1,0:T(8,128)(2,1)S(1)} collective-permute-done((bf16[512,128]{1,0:T(8,128)(2,1)S(1)}, bf16[512,128]{1,0:T(8,128)(2,1)S(1)}, u32[]{:S(2)}, u32[]{:S(2)}) %collective-permute-start.12) | collective-permute-done | bytes 131104 | tf_op jit(solution)/shard_map/ppermute | solution.py:412
  66.0 2.1 %collective-permute-start.17 = (bf16[512,128]{1,0:T(8,128)(2,1)S(1)}, bf16[512,128]{1,0:T(8,128)(2,1)S(1)}, u32[]{:S(2)}, u32[]{:S(2)}) collective-permute-start(bf16[512,128]{1,0:T(8,128)(2,1)S(1)} %get-tuple-element.146), channel_id=1, source_target_pairs={{0,12},{1,13},{2,14},{3,15},{4,8},{5,9},{6,10},{7,11},{8,4},{9,5},... | collective-permute-start | bytes 393224 | tf_op jit(solution)/shard_map/ppermute | solution.py:412
  69.5 1.8 %shard_map.78 = (bf16[512,128]{1,0:T(8,128)(2,1)S(1)}, bf16[512,128]{1,0:T(8,128)(2,1)S(1)}, bf16[512,128]{1,0:T(8,128)(2,1)S(1)}, bf16[512,128]{1,0:T(8,128)(2,1)S(1)}) custom-call(s32[3]{0:T(128)S(1)} %pad_add_fusion.place_ref, bf16[4,512,128]{2,1,0:T(8,128)(2,1)S(1)} %get-tuple-element.200.own, bf16[4,512,128]{2,1,0:T(8,128)(2,1)S(1)} %collective-permute-done.14.over_x, ...), custom_call_target="tpu_custom_call" | custom-call | flops 1000 | bytes 1000 | tf_op jit(solution)/shard_map/pallas_call | solution.py:468
  71.3 6.3 %collective-permute-done.16 = bf16[512,128]{1,0:T(8,128)(2,1)S(1)} collective-permute-done((bf16[512,128]{1,0:T(8,128)(2,1)S(1)}, bf16[512,128]{1,0:T(8,128)(2,1)S(1)}, u32[]{:S(2)}, u32[]{:S(2)}) %collective-permute-start.16) | collective-permute-done | bytes 131104 | tf_op jit(solution)/shard_map/ppermute | solution.py:412
  80.8 2.3 %collective-permute-start.21 = (bf16[512,128]{1,0:T(8,128)(2,1)S(1)}, bf16[512,128]{1,0:T(8,128)(2,1)S(1)}, u32[]{:S(2)}, u32[]{:S(2)}) collective-permute-start(bf16[512,128]{1,0:T(8,128)(2,1)S(1)} %get-tuple-element.160), channel_id=1, source_target_pairs={{0,8},{1,9},{2,10},{3,11},{4,12},{5,13},{6,14},{7,15},{8,0},{9,1},... | collective-permute-start | bytes 393224 | tf_op jit(solution)/shard_map/ppermute | solution.py:412
  83.1 2.1 %collective-permute-start.22 = (bf16[512,128]{1,0:T(8,128)(2,1)S(1)}, bf16[512,128]{1,0:T(8,128)(2,1)S(1)}, u32[]{:S(2)}, u32[]{:S(2)}) collective-permute-start(bf16[512,128]{1,0:T(8,128)(2,1)S(1)} %get-tuple-element.161), channel_id=1, source_target_pairs={{0,12},{1,13},{2,14},{3,15},{4,8},{5,9},{6,10},{7,11},{8,4},{9,5},... | collective-permute-start | bytes 393224 | tf_op jit(solution)/shard_map/ppermute | solution.py:412
  85.2 1.9 %shard_map.79 = (bf16[512,128]{1,0:T(8,128)(2,1)S(1)}, bf16[512,128]{1,0:T(8,128)(2,1)S(1)}, bf16[512,128]{1,0:T(8,128)(2,1)S(1)}, bf16[512,128]{1,0:T(8,128)(2,1)S(1)}) custom-call(s32[3]{0:T(128)S(1)} %pad_add_fusion.place_ref, bf16[4,512,128]{2,1,0:T(8,128)(2,1)S(1)} %get-tuple-element.198.own, bf16[4,512,128]{2,1,0:T(8,128)(2,1)S(1)} %collective-permute-done.20.over_x, ...), custom_call_target="tpu_custom_call" | custom-call | flops 1000 | bytes 1000 | tf_op jit(solution)/shard_map/pallas_call | solution.py:468
  87.1 6.6 %collective-permute-done.21.refs_1_ = bf16[512,128]{1,0:T(8,128)(2,1)S(1)} collective-permute-done((bf16[512,128]{1,0:T(8,128)(2,1)S(1)}, bf16[512,128]{1,0:T(8,128)(2,1)S(1)}, u32[]{:S(2)}, u32[]{:S(2)}) %collective-permute-start.21) | collective-permute-done | bytes 131104 | tf_op jit(solution)/shard_map/ppermute | solution.py:412
  94.6 2.5 %collective-permute-start.26 = (bf16[512,128]{1,0:T(8,128)(2,1)S(1)}, bf16[512,128]{1,0:T(8,128)(2,1)S(1)}, u32[]{:S(2)}, u32[]{:S(2)}) collective-permute-start(bf16[512,128]{1,0:T(8,128)(2,1)S(1)} %get-tuple-element.177), channel_id=1, source_target_pairs={{0,8},{1,9},{2,10},{3,11},{4,12},{5,13},{6,14},{7,15},{8,0},{9,1},... | collective-permute-start | bytes 393224 | tf_op jit(solution)/shard_map/ppermute | solution.py:412
  97.1 1.9 %collective-permute-start.27 = (bf16[512,128]{1,0:T(8,128)(2,1)S(1)}, bf16[512,128]{1,0:T(8,128)(2,1)S(1)}, u32[]{:S(2)}, u32[]{:S(2)}) collective-permute-start(bf16[512,128]{1,0:T(8,128)(2,1)S(1)} %get-tuple-element.178), channel_id=1, source_target_pairs={{0,12},{1,13},{2,14},{3,15},{4,8},{5,9},{6,10},{7,11},{8,4},{9,5},... | collective-permute-start | bytes 393224 | tf_op jit(solution)/shard_map/ppermute | solution.py:412
  98.9 1.8 %shard_map.80 = (bf16[512,128]{1,0:T(8,128)(2,1)S(1)}, bf16[512,128]{1,0:T(8,128)(2,1)S(1)}, bf16[512,128]{1,0:T(8,128)(2,1)S(1)}, bf16[512,128]{1,0:T(8,128)(2,1)S(1)}) custom-call(s32[3]{0:T(128)S(1)} %pad_add_fusion.place_ref, bf16[4,512,128]{2,1,0:T(8,128)(2,1)S(1)} %get-tuple-element.196.own, bf16[4,512,128]{2,1,0:T(8,128)(2,1)S(1)} %collective-permute-done.25.over_x, ...), custom_call_target="tpu_custom_call" | custom-call | flops 1000 | bytes 1000 | tf_op jit(solution)/shard_map/pallas_call | solution.py:468
  100.8 6.8 %collective-permute-done.26.refs_5_ = bf16[512,128]{1,0:T(8,128)(2,1)S(1)} collective-permute-done((bf16[512,128]{1,0:T(8,128)(2,1)S(1)}, bf16[512,128]{1,0:T(8,128)(2,1)S(1)}, u32[]{:S(2)}, u32[]{:S(2)}) %collective-permute-start.26) | collective-permute-done | bytes 131104 | tf_op jit(solution)/shard_map/ppermute | solution.py:412
  110.0 2.7 %collective-permute-start.31 = (bf16[512,128]{1,0:T(8,128)(2,1)S(1)}, bf16[512,128]{1,0:T(8,128)(2,1)S(1)}, u32[]{:S(2)}, u32[]{:S(2)}) collective-permute-start(bf16[512,128]{1,0:T(8,128)(2,1)S(1)} %get-tuple-element.192), channel_id=1, source_target_pairs={{0,8},{1,9},{2,10},{3,11},{4,12},{5,13},{6,14},{7,15},{8,0},{9,1},... | collective-permute-start | bytes 393224 | tf_op jit(solution)/shard_map/ppermute | solution.py:412
  112.7 1.7 %collective-permute-start.32 = (bf16[512,128]{1,0:T(8,128)(2,1)S(1)}, bf16[512,128]{1,0:T(8,128)(2,1)S(1)}, u32[]{:S(2)}, u32[]{:S(2)}) collective-permute-start(bf16[512,128]{1,0:T(8,128)(2,1)S(1)} %get-tuple-element.193), channel_id=1, source_target_pairs={{0,12},{1,13},{2,14},{3,15},{4,8},{5,9},{6,10},{7,11},{8,4},{9,5},... | collective-permute-start | bytes 393224 | tf_op jit(solution)/shard_map/ppermute | solution.py:412
  114.4 2.8 %shard_map.81 = (bf16[128,8192]{1,0:T(8,128)(2,1)}, f32[2,128,128]{2,1,0:T(8,128)S(1)}) custom-call(s32[3]{0:T(128)S(1)} %pad_add_fusion.place_ref, s32[64]{0:T(128)S(1)} %copy-done.3, bf16[512,128]{1,0:T(8,128)(2,1)S(1)} %get-tuple-element.172.refs_0_, bf16[512,128]{1,0:T(8,128)(2,1)S(1)} %collective-permute-done.21.refs_1_, ...), custom_call_target="tpu_custom_call" | custom-call | flops 1000 | bytes 1000 | tf_op jit(solution)/shard_map/pallas_call | solution.py:529
  117.2 5.6 %collective-permute-done.31.refs_1_ = bf16[512,128]{1,0:T(8,128)(2,1)S(1)} collective-permute-done((bf16[512,128]{1,0:T(8,128)(2,1)S(1)}, bf16[512,128]{1,0:T(8,128)(2,1)S(1)}, u32[]{:S(2)}, u32[]{:S(2)}) %collective-permute-start.31) | collective-permute-done | bytes 131104 | tf_op jit(solution)/shard_map/ppermute | solution.py:412
  122.9 2.6 %shard_map.82 = bf16[128,8192]{1,0:T(8,128)(2,1)} custom-call(s32[3]{0:T(128)S(1)} %pad_add_fusion.place_ref, s32[64]{0:T(128)S(1)} %copy-done.3, bf16[128,8192]{1,0:T(8,128)(2,1)} %get-tuple-element.189.done_hbm, f32[2,128,128]{2,1,0:T(8,128)S(1)} %get-tuple-element.190.seam_ref, ...), custom_call_target="tpu_custom_call", output_to_operand_aliasing={{}: (2, {})} | custom-call | flops 1000 | bytes 1000 | tf_op jit(solution)/shard_map/pallas_call | solution.py:541
  (82 shorter events, 23.4 us)
Async XLA Ops:
  4.5 7.5 %collective-permute-start.2 = (bf16[128,512]{1,0:T(8,128)(2,1)S(1)}, bf16[128,512]{1,0:T(8,128)(2,1)S(1)}, u32[]{:S(2)}, u32[]{:S(2)}) collective-permute-start(bf16[128,512]{1,0:T(8,128)(2,1)S(1)} %get-tuple-element.110), channel_id=1, source_target_pairs={{0,1},{1,0},{2,3},{3,2},{4,5},{5,4},{6,7},{7,6},{8,9},{9,8},{10,11... | collective-permute-start | bytes 393224 | tf_op jit(solution)/shard_map/ppermute | solution.py:412
  5.0 7.0 %collective-permute-start.3 = (bf16[128,512]{1,0:T(8,128)(2,1)S(1)}, bf16[128,512]{1,0:T(8,128)(2,1)S(1)}, u32[]{:S(2)}, u32[]{:S(2)}) collective-permute-start(bf16[128,512]{1,0:T(8,128)(2,1)S(1)} %get-tuple-element.111), channel_id=1, source_target_pairs={{0,2},{1,3},{2,0},{3,1},{4,6},{5,7},{6,4},{7,5},{8,10},{9,11},{10,... | collective-permute-start | bytes 393224 | tf_op jit(solution)/shard_map/ppermute | solution.py:412
  7.5 6.6 %collective-permute-start.4 = (bf16[128,512]{1,0:T(8,128)(2,1)S(1)}, bf16[128,512]{1,0:T(8,128)(2,1)S(1)}, u32[]{:S(2)}, u32[]{:S(2)}) collective-permute-start(bf16[128,512]{1,0:T(8,128)(2,1)S(1)} %get-tuple-element.112), channel_id=1, source_target_pairs={{0,3},{1,2},{2,1},{3,0},{4,7},{5,6},{6,5},{7,4},{8,11},{9,10},{10,... | collective-permute-start | bytes 393224 | tf_op jit(solution)/shard_map/ppermute | solution.py:412
  14.3 15.7 %collective-permute-start.5 = (bf16[512,256]{1,0:T(8,128)(2,1)S(1)}, bf16[512,256]{1,0:T(8,128)(2,1)S(1)}, u32[]{:S(2)}, u32[]{:S(2)}) collective-permute-start(bf16[512,256]{1,0:T(8,128)(2,1)S(1)} %slice.37), channel_id=1, source_target_pairs={{0,4},{1,5},{2,6},{3,7},{4,0},{5,1},{6,2},{7,3},{8,12},{9,13},{10,... | collective-permute-start | bytes 786440 | tf_op jit(solution)/shard_map/ppermute | solution.py:412
  16.0 14.8 %collective-permute-start.6 = (bf16[512,256]{1,0:T(8,128)(2,1)S(1)}, bf16[512,256]{1,0:T(8,128)(2,1)S(1)}, u32[]{:S(2)}, u32[]{:S(2)}) collective-permute-start(bf16[512,256]{1,0:T(8,128)(2,1)S(1)} %slice.37), channel_id=1, source_target_pairs={{0,8},{1,9},{2,10},{3,11},{4,12},{5,13},{6,14},{7,15},{8,0},{9,1},... | collective-permute-start | bytes 786440 | tf_op jit(solution)/shard_map/ppermute | solution.py:412
  23.5 6.5 %collective-permute-start.1 = (bf16[2,128,128]{2,1,0:T(8,128)(2,1)S(1)}, bf16[2,128,128]{2,1,0:T(8,128)(2,1)S(1)}, u32[]{:S(2)}, u32[]{:S(2)}) collective-permute-start(bf16[2,128,128]{2,1,0:T(8,128)(2,1)S(1)} %get-tuple-element.104), channel_id=1, source_target_pairs={{0,16},{16,0},{1,17},{17,1},{2,18},{18,2},{3,19},{19,3},{4,20},{20... | collective-permute-start | bytes 196616 | tf_op jit(solution)/shard_map/ppermute | solution.py:418
  30.8 12.6 %collective-permute-start.10 = (bf16[2048,128]{1,0:T(8,128)(2,1)S(1)}, bf16[2048,128]{1,0:T(8,128)(2,1)S(1)}, u32[]{:S(2)}, u32[]{:S(2)}) collective-permute-start(bf16[2048,128]{1,0:T(8,128)(2,1)S(1)} %get-tuple-element.123), channel_id=1, source_target_pairs={{0,16},{16,0},{1,17},{17,1},{2,18},{18,2},{3,19},{19,3},{4,20},{20... | collective-permute-start | bytes 1572872 | tf_op jit(solution)/shard_map/ppermute | solution.py:418
  32.3 16.3 %collective-permute-start.9 = (bf16[1536,128]{1,0:T(8,128)(2,1)S(1)}, bf16[1536,128]{1,0:T(8,128)(2,1)S(1)}, u32[]{:S(2)}, u32[]{:S(2)}) collective-permute-start(bf16[1536,128]{1,0:T(8,128)(2,1)S(1)} %pad_maximum_fusion.8), channel_id=1, source_target_pairs={{0,4},{1,5},{2,6},{3,7},{4,0},{5,1},{6,2},{7,3},{8,12},{9,13},{10,... | collective-permute-start | bytes 1179656 | tf_op jit(solution)/shard_map/ppermute | solution.py:412
  32.8 11.9 %collective-permute-start.7 = (bf16[512,128]{1,0:T(8,128)(2,1)S(1)}, bf16[512,128]{1,0:T(8,128)(2,1)S(1)}, u32[]{:S(2)}, u32[]{:S(2)}) collective-permute-start(bf16[512,128]{1,0:T(8,128)(2,1)S(1)} %get-tuple-element.118), channel_id=1, source_target_pairs={{0,8},{1,9},{2,10},{3,11},{4,12},{5,13},{6,14},{7,15},{8,0},{9,1},... | collective-permute-start | bytes 393224 | tf_op jit(solution)/shard_map/ppermute | solution.py:412
  35.4 13.2 %collective-permute-start.8 = (bf16[512,128]{1,0:T(8,128)(2,1)S(1)}, bf16[512,128]{1,0:T(8,128)(2,1)S(1)}, u32[]{:S(2)}, u32[]{:S(2)}) collective-permute-start(bf16[512,128]{1,0:T(8,128)(2,1)S(1)} %get-tuple-element.119), channel_id=1, source_target_pairs={{0,12},{1,13},{2,14},{3,15},{4,8},{5,9},{6,10},{7,11},{8,4},{9,5},... | collective-permute-start | bytes 393224 | tf_op jit(solution)/shard_map/ppermute | solution.py:412
  48.7 16.3 %collective-permute-start.15 = (bf16[2048,128]{1,0:T(8,128)(2,1)S(1)}, bf16[2048,128]{1,0:T(8,128)(2,1)S(1)}, u32[]{:S(2)}, u32[]{:S(2)}) collective-permute-start(bf16[2048,128]{1,0:T(8,128)(2,1)S(1)} %pad_maximum_fusion.4), channel_id=1, source_target_pairs={{0,16},{16,0},{1,17},{17,1},{2,18},{18,2},{3,19},{19,3},{4,20},{20... | collective-permute-start | bytes 1572872 | tf_op jit(solution)/shard_map/ppermute | solution.py:418
  49.4 15.7 %collective-permute-start.14 = (bf16[4,512,128]{2,1,0:T(8,128)(2,1)S(1)}, bf16[4,512,128]{2,1,0:T(8,128)(2,1)S(1)}, u32[]{:S(2)}, u32[]{:S(2)}) collective-permute-start(bf16[4,512,128]{2,1,0:T(8,128)(2,1)S(1)} %get-tuple-element.200.own), channel_id=1, source_target_pairs={{0,2},{1,3},{2,0},{3,1},{4,6},{5,7},{6,4},{7,5},{8,10},{9,11},{10,... | collective-permute-start | bytes 1572872 | tf_op jit(solution)/shard_map/ppermute | solution.py:412
  51.0 14.1 %collective-permute-start.13 = (bf16[1536,128]{1,0:T(8,128)(2,1)S(1)}, bf16[1536,128]{1,0:T(8,128)(2,1)S(1)}, u32[]{:S(2)}, u32[]{:S(2)}) collective-permute-start(bf16[1536,128]{1,0:T(8,128)(2,1)S(1)} %pad_maximum_fusion.9), channel_id=1, source_target_pairs={{0,4},{1,5},{2,6},{3,7},{4,0},{5,1},{6,2},{7,3},{8,12},{9,13},{10,... | collective-permute-start | bytes 1179656 | tf_op jit(solution)/shard_map/ppermute | solution.py:412
  51.1 10.4 %collective-permute-start.11 = (bf16[512,128]{1,0:T(8,128)(2,1)S(1)}, bf16[512,128]{1,0:T(8,128)(2,1)S(1)}, u32[]{:S(2)}, u32[]{:S(2)}) collective-permute-start(bf16[512,128]{1,0:T(8,128)(2,1)S(1)} %get-tuple-element.130), channel_id=1, source_target_pairs={{0,8},{1,9},{2,10},{3,11},{4,12},{5,13},{6,14},{7,15},{8,0},{9,1},... | collective-permute-start | bytes 393224 | tf_op jit(solution)/shard_map/ppermute | solution.py:412
  53.4 11.7 %collective-permute-start.12 = (bf16[512,128]{1,0:T(8,128)(2,1)S(1)}, bf16[512,128]{1,0:T(8,128)(2,1)S(1)}, u32[]{:S(2)}, u32[]{:S(2)}) collective-permute-start(bf16[512,128]{1,0:T(8,128)(2,1)S(1)} %get-tuple-element.131), channel_id=1, source_target_pairs={{0,12},{1,13},{2,14},{3,15},{4,8},{5,9},{6,10},{7,11},{8,4},{9,5},... | collective-permute-start | bytes 393224 | tf_op jit(solution)/shard_map/ppermute | solution.py:412
  65.4 14.4 %collective-permute-start.20 = (bf16[4,512,128]{2,1,0:T(8,128)(2,1)S(1)}, bf16[4,512,128]{2,1,0:T(8,128)(2,1)S(1)}, u32[]{:S(2)}, u32[]{:S(2)}) collective-permute-start(bf16[4,512,128]{2,1,0:T(8,128)(2,1)S(1)} %get-tuple-element.198.own), channel_id=1, source_target_pairs={{0,2},{1,3},{2,0},{3,1},{4,6},{5,7},{6,4},{7,5},{8,10},{9,11},{10,... | collective-permute-start | bytes 1572872 | tf_op jit(solution)/shard_map/ppermute | solution.py:412
  66.0 11.7 %collective-permute-start.16 = (bf16[512,128]{1,0:T(8,128)(2,1)S(1)}, bf16[512,128]{1,0:T(8,128)(2,1)S(1)}, u32[]{:S(2)}, u32[]{:S(2)}) collective-permute-start(bf16[512,128]{1,0:T(8,128)(2,1)S(1)} %get-tuple-element.145), channel_id=1, source_target_pairs={{0,8},{1,9},{2,10},{3,11},{4,12},{5,13},{6,14},{7,15},{8,0},{9,1},... | collective-permute-start | bytes 393224 | tf_op jit(solution)/shard_map/ppermute | solution.py:412
  66.0 11.7 %collective-permute-start.17 = (bf16[512,128]{1,0:T(8,128)(2,1)S(1)}, bf16[512,128]{1,0:T(8,128)(2,1)S(1)}, u32[]{:S(2)}, u32[]{:S(2)}) collective-permute-start(bf16[512,128]{1,0:T(8,128)(2,1)S(1)} %get-tuple-element.146), channel_id=1, source_target_pairs={{0,12},{1,13},{2,14},{3,15},{4,8},{5,9},{6,10},{7,11},{8,4},{9,5},... | collective-permute-start | bytes 393224 | tf_op jit(solution)/shard_map/ppermute | solution.py:412
  68.1 10.9 %collective-permute-start.18 = (bf16[512,128]{1,0:T(8,128)(2,1)S(1)}, bf16[512,128]{1,0:T(8,128)(2,1)S(1)}, u32[]{:S(2)}, u32[]{:S(2)}) collective-permute-start(bf16[512,128]{1,0:T(8,128)(2,1)S(1)} %get-tuple-element.147), channel_id=1, source_target_pairs={{0,4},{1,5},{2,6},{3,7},{4,0},{5,1},{6,2},{7,3},{8,12},{9,13},{10,... | collective-permute-start | bytes 393224 | tf_op jit(solution)/shard_map/ppermute | solution.py:412
  79.9 5.3 %collective-permute-start.24 = (bf16[2,4,512,128]{3,2,1,0:T(8,128)(2,1)S(1)}, bf16[2,4,512,128]{3,2,1,0:T(8,128)(2,1)S(1)}, u32[]{:S(2)}, u32[]{:S(2)}) collective-permute-start(bf16[2,4,512,128]{3,2,1,0:T(8,128)(2,1)S(1)} %pad_maximum_fusion.1), channel_id=1, source_target_pairs={{0,1},{1,0},{2,3},{3,2},{4,5},{5,4},{6,7},{7,6},{8,9},{9,8},{10,11... | collective-permute-start | bytes 3145736 | tf_op jit(solution)/shard_map/ppermute | solution.py:412
  80.0 14.4 %collective-permute-start.25 = (bf16[4,512,128]{2,1,0:T(8,128)(2,1)S(1)}, bf16[4,512,128]{2,1,0:T(8,128)(2,1)S(1)}, u32[]{:S(2)}, u32[]{:S(2)}) collective-permute-start(bf16[4,512,128]{2,1,0:T(8,128)(2,1)S(1)} %get-tuple-element.196.own), channel_id=1, source_target_pairs={{0,2},{1,3},{2,0},{3,1},{4,6},{5,7},{6,4},{7,5},{8,10},{9,11},{10,... | collective-permute-start | bytes 1572872 | tf_op jit(solution)/shard_map/ppermute | solution.py:412
  80.8 12.9 %collective-permute-start.21 = (bf16[512,128]{1,0:T(8,128)(2,1)S(1)}, bf16[512,128]{1,0:T(8,128)(2,1)S(1)}, u32[]{:S(2)}, u32[]{:S(2)}) collective-permute-start(bf16[512,128]{1,0:T(8,128)(2,1)S(1)} %get-tuple-element.160), channel_id=1, source_target_pairs={{0,8},{1,9},{2,10},{3,11},{4,12},{5,13},{6,14},{7,15},{8,0},{9,1},... | collective-permute-start | bytes 393224 | tf_op jit(solution)/shard_map/ppermute | solution.py:412
  83.1 10.6 %collective-permute-start.22 = (bf16[512,128]{1,0:T(8,128)(2,1)S(1)}, bf16[512,128]{1,0:T(8,128)(2,1)S(1)}, u32[]{:S(2)}, u32[]{:S(2)}) collective-permute-start(bf16[512,128]{1,0:T(8,128)(2,1)S(1)} %get-tuple-element.161), channel_id=1, source_target_pairs={{0,12},{1,13},{2,14},{3,15},{4,8},{5,9},{6,10},{7,11},{8,4},{9,5},... | collective-permute-start | bytes 393224 | tf_op jit(solution)/shard_map/ppermute | solution.py:412
  85.2 9.1 %collective-permute-start.23 = (bf16[512,128]{1,0:T(8,128)(2,1)S(1)}, bf16[512,128]{1,0:T(8,128)(2,1)S(1)}, u32[]{:S(2)}, u32[]{:S(2)}) collective-permute-start(bf16[512,128]{1,0:T(8,128)(2,1)S(1)} %get-tuple-element.162), channel_id=1, source_target_pairs={{0,4},{1,5},{2,6},{3,7},{4,0},{5,1},{6,2},{7,3},{8,12},{9,13},{10,... | collective-permute-start | bytes 393224 | tf_op jit(solution)/shard_map/ppermute | solution.py:412
  94.5 4.4 %collective-permute-start.29 = (bf16[2,4,512,128]{3,2,1,0:T(8,128)(2,1)S(1)}, bf16[2,4,512,128]{3,2,1,0:T(8,128)(2,1)S(1)}, u32[]{:S(2)}, u32[]{:S(2)}) collective-permute-start(bf16[2,4,512,128]{3,2,1,0:T(8,128)(2,1)S(1)} %pad_maximum_fusion.2), channel_id=1, source_target_pairs={{0,1},{1,0},{2,3},{3,2},{4,5},{5,4},{6,7},{7,6},{8,9},{9,8},{10,11... | collective-permute-start | bytes 3145736 | tf_op jit(solution)/shard_map/ppermute | solution.py:412
  94.6 12.9 %collective-permute-start.26 = (bf16[512,128]{1,0:T(8,128)(2,1)S(1)}, bf16[512,128]{1,0:T(8,128)(2,1)S(1)}, u32[]{:S(2)}, u32[]{:S(2)}) collective-permute-start(bf16[512,128]{1,0:T(8,128)(2,1)S(1)} %get-tuple-element.177), channel_id=1, source_target_pairs={{0,8},{1,9},{2,10},{3,11},{4,12},{5,13},{6,14},{7,15},{8,0},{9,1},... | collective-permute-start | bytes 393224 | tf_op jit(solution)/shard_map/ppermute | solution.py:412
  97.1 10.5 %collective-permute-start.27 = (bf16[512,128]{1,0:T(8,128)(2,1)S(1)}, bf16[512,128]{1,0:T(8,128)(2,1)S(1)}, u32[]{:S(2)}, u32[]{:S(2)}) collective-permute-start(bf16[512,128]{1,0:T(8,128)(2,1)S(1)} %get-tuple-element.178), channel_id=1, source_target_pairs={{0,12},{1,13},{2,14},{3,15},{4,8},{5,9},{6,10},{7,11},{8,4},{9,5},... | collective-permute-start | bytes 393224 | tf_op jit(solution)/shard_map/ppermute | solution.py:412
  98.9 9.5 %collective-permute-start.28 = (bf16[512,128]{1,0:T(8,128)(2,1)S(1)}, bf16[512,128]{1,0:T(8,128)(2,1)S(1)}, u32[]{:S(2)}, u32[]{:S(2)}) collective-permute-start(bf16[512,128]{1,0:T(8,128)(2,1)S(1)} %get-tuple-element.179), channel_id=1, source_target_pairs={{0,4},{1,5},{2,6},{3,7},{4,0},{5,1},{6,2},{7,3},{8,12},{9,13},{10,... | collective-permute-start | bytes 393224 | tf_op jit(solution)/shard_map/ppermute | solution.py:412
  108.4 14.4 %collective-permute-start.30 = (bf16[2048,128]{1,0:T(8,128)(2,1)S(1)}, bf16[2048,128]{1,0:T(8,128)(2,1)S(1)}, u32[]{:S(2)}, u32[]{:S(2)}) collective-permute-start(bf16[2048,128]{1,0:T(8,128)(2,1)S(1)} %pad_maximum_fusion.7), channel_id=1, source_target_pairs={{0,16},{16,0},{1,17},{17,1},{2,18},{18,2},{3,19},{19,3},{4,20},{20... | collective-permute-start | bytes 1572872 | tf_op jit(solution)/shard_map/ppermute | solution.py:418
  110.0 12.8 %collective-permute-start.31 = (bf16[512,128]{1,0:T(8,128)(2,1)S(1)}, bf16[512,128]{1,0:T(8,128)(2,1)S(1)}, u32[]{:S(2)}, u32[]{:S(2)}) collective-permute-start(bf16[512,128]{1,0:T(8,128)(2,1)S(1)} %get-tuple-element.192), channel_id=1, source_target_pairs={{0,8},{1,9},{2,10},{3,11},{4,12},{5,13},{6,14},{7,15},{8,0},{9,1},... | collective-permute-start | bytes 393224 | tf_op jit(solution)/shard_map/ppermute | solution.py:412
  112.7 10.1 %collective-permute-start.32 = (bf16[512,128]{1,0:T(8,128)(2,1)S(1)}, bf16[512,128]{1,0:T(8,128)(2,1)S(1)}, u32[]{:S(2)}, u32[]{:S(2)}) collective-permute-start(bf16[512,128]{1,0:T(8,128)(2,1)S(1)} %get-tuple-element.193), channel_id=1, source_target_pairs={{0,12},{1,13},{2,14},{3,15},{4,8},{5,9},{6,10},{7,11},{8,4},{9,5},... | collective-permute-start | bytes 393224 | tf_op jit(solution)/shard_map/ppermute | solution.py:412
  114.4 8.4 %collective-permute-start.33 = (bf16[512,128]{1,0:T(8,128)(2,1)S(1)}, bf16[512,128]{1,0:T(8,128)(2,1)S(1)}, u32[]{:S(2)}, u32[]{:S(2)}) collective-permute-start(bf16[512,128]{1,0:T(8,128)(2,1)S(1)} %get-tuple-element.194), channel_id=1, source_target_pairs={{0,4},{1,5},{2,6},{3,7},{4,0},{5,1},{6,2},{7,3},{8,12},{9,13},{10,... | collective-permute-start | bytes 393224 | tf_op jit(solution)/shard_map/ppermute | solution.py:412
  (9 other events, 90.6 us)

commit v3 on v2

--- a/solution.py
+++ b/solution.py
@@ -11,7 +11,7 @@
 EDGE = 2 * HB
 GROUP = 8
 PLANE = 4
-ORDER = (0, 2, 3, 1)
+ORDER = (0, 3, 2, 1)
 VMEM = pl.BlockSpec(memory_space=pltpu.VMEM)
 HBM = pl.BlockSpec(memory_space=pltpu.HBM)
 SMEM = pl.BlockSpec(memory_space=pltpu.SMEM)
@@ -44,7 +44,8 @@
     center = (upper_bound + cutoff) / 2.0
     sigma_one = half_width / (lower_bound - center)
     sigma_two = 1.0 / (2.0 / sigma_one - sigma_one)
-    return center, sigma_one / half_width, 2.0 * sigma_two / half_width, sigma_one * sigma_two
+    first, second, last = sigma_one / half_width, 2.0 * sigma_two / half_width, sigma_one * half_width / 2.0
+    return center, first, second, last
 
 
 def loop(start, stop, body, unroll, carry=0):
@@ -113,9 +114,9 @@
         copy.wait()
 
 
-def multiply(blocks, rows_ref, cols_ref, tiles_ref, source_ref, acc_ref, extra_ref):
+def multiply(blocks, rows_ref, cols_ref, tiles_ref, source_ref, acc_ref, extra_ref, more):
     def diagonal(r, _):
-        acc_ref[r] = product(tiles_ref[r], source_ref[r])
+        acc_ref[r] = product(tiles_ref[r], source_ref[r]) - more(r)
         return 0
 
     loop(0, blocks, diagonal, 16)
@@ -156,7 +157,12 @@
 ):
     tile, lanes = xt_ref.shape[1:]
     slab = place_ref[1]
-    multiply(blocks, rows_ref, cols_ref, tiles_ref, xt_ref, acc_ref, extra_ref)
+    center, scale = coefficients(bounds_ref)[:2]
+
+    def more(r):
+        return center * xt_ref[r].astype(f32)
+
+    multiply(blocks, rows_ref, cols_ref, tiles_ref, xt_ref, acc_ref, extra_ref, more)
     for b in range(HB):
         ext_ref[b] = halo_ref[:, b * tile:(b + 1) * tile].T
 
@@ -164,24 +170,15 @@
         acc_ref[row] += value
 
     multiply_edges(blocks, slab, rows_ref, cols_ref, tiles_ref, ext_ref, add)
-    center, scale = coefficients(bounds_ref)[:2]
-
     def finish(r, _):
-        value = (acc_ref[r] - center * xt_ref[r].astype(f32)) * scale
-        f1_ref[r] = jnp.where(live_mask(tile, lanes, counts_ref[r]), value, 0.0).astype(bf16)
+        live = live_mask(tile, lanes, counts_ref[r])
+        f1_ref[r] = jnp.where(live, acc_ref[r] * scale, 0.0).astype(bf16)
         return 0
 
     loop(0, blocks, finish, 4)
     begin = jnp.where(slab == 0, blocks - HB, 0)
     for b in range(HB):
         edge_ref[b] = f1_ref[begin + b]
-
-
-def second_values(r, acc, block, xt_ref, counts_ref, scales):
-    tile, lanes = block.shape
-    center, _, scale, both = scales
-    value = (acc - center * block.astype(f32)) * scale - both * xt_ref[r].astype(f32)
-    return jnp.where(live_mask(tile, lanes, counts_ref[r]), value, 0.0)
 
 
 def split_parts(outs, place_ref, packed_ref, base):
@@ -198,16 +195,18 @@
     outs, refs = refs[:groups], refs[groups:]
     shared_ref, excess_ref, rest_ref, edge_ref, acc_ref, extra_ref, packed_ref = refs
     tile = tiles_ref.shape[1]
-    multiply(blocks, rows_ref, cols_ref, tiles_ref, f1_ref, acc_ref, extra_ref)
+    center, _, scale, last = coefficients(bounds_ref)
+
+    def more(r):
+        return center * f1_ref[r].astype(f32) + last * xt_ref[r].astype(f32)
+
+    multiply(blocks, rows_ref, cols_ref, tiles_ref, f1_ref, acc_ref, extra_ref, more)
     edges = [edge_row(e, blocks) for e in range(EDGE)]
     for e, r in enumerate(edges):
         edge_ref[e] = acc_ref[r]
-    scales = coefficients(bounds_ref)
-
     def finish(r, offset):
-        packed_ref[pl.ds(offset, tile)] = second_values(
-            r, acc_ref[r], f1_ref[r], xt_ref, counts_ref, scales
-        )
+        live = live_mask(tile, acc_ref.shape[2], counts_ref[r])
+        packed_ref[pl.ds(offset, tile)] = jnp.where(live, acc_ref[r] * scale, 0.0)
         return offset + counts_ref[r]
 
     loop(HB, blocks - HB, finish, 4, sum_counts(counts_ref, edges))
@@ -219,8 +218,8 @@
 
 
 def second_edge_kernel(
-    blocks, groups, place_ref, rows_ref, cols_ref, counts_ref, bounds_ref, halo_ref, f1_ref, xt_ref,
-    tiles_ref, sum_ref, rest_ref, *refs,
+    blocks, groups, place_ref, rows_ref, cols_ref, counts_ref, bounds_ref, halo_ref, tiles_ref,
+    sum_ref, rest_ref, *refs,
 ):
     outs, (acc_ref, packed_ref) = refs[:groups], refs[groups:]
     tile = tiles_ref.shape[1]
@@ -230,15 +229,14 @@
         acc_ref[edge_slot(row, blocks)] += value
 
     multiply_edges(blocks, place_ref[1], rows_ref, cols_ref, tiles_ref, halo_ref, add)
-    scales = coefficients(bounds_ref)
+    scale = coefficients(bounds_ref)[2]
     packed_ref[...] = rest_ref[...]
     offset = 0
     for e in range(EDGE):
         r = edge_row(e, blocks)
-        value = second_values(r, acc_ref[e], f1_ref[r], xt_ref, counts_ref, scales)
         here = pl.ds(offset, tile)
-        live = live_mask(tile, value.shape[1], counts_ref[r])
-        packed_ref[here] = jnp.where(live, value, packed_ref[here])
+        live = live_mask(tile, acc_ref.shape[2], counts_ref[r])
+        packed_ref[here] = jnp.where(live, acc_ref[e] * scale, packed_ref[here])
         offset = offset + counts_ref[r]
     split_parts(outs, place_ref, packed_ref, 0)
 
@@ -253,7 +251,7 @@
 
 
 def rotate_kernel(
-    groups, place_ref, own, over_x, core, mine, near, far_two, far_three, near_more, other_ref, *refs
+    groups, place_ref, own, over_x, core, mine, near, far_two, far_three, other_near, other_ref, *refs
 ):
     outs, turned = refs[:groups], refs[groups]
     width = outs[0].shape[1]
@@ -269,11 +267,12 @@
         )
 
     for h in range(2):
+        own_half = mine[:, h * half:(h + 1) * half]
         if h == 0:
-            rhs = [far_two[...], wide(far_three), near[...]]
+            rhs = [own_half, near[...], far_two[...], wide(far_three)]
         else:
-            rhs = [wide(other_ref), wide(other_ref, groups // 2), wide(near_more)]
-        rhs = jnp.concatenate([mine[:, h * half:(h + 1) * half]] + rhs, axis=0)
+            rhs = [own_half, other_near[...], wide(other_ref), wide(other_ref, groups // 2)]
+        rhs = jnp.concatenate([rhs[s] for s in ORDER], axis=0)
         total = product(lhs, rhs).astype(bf16)
         first = (place_ref[1] ^ h) * (groups // 2)
         for z in range(groups // 2):
@@ -475,8 +474,12 @@
 
     excess, halo, first_parts, near, far_two = together(excess, halo, first_parts, near, far_two)
     excess = other_slab(excess)
+    other_near = other_slab(near)
     columns = [far_two[:, i * norb_dev:(i + 1) * norb_dev] for i in range(groups // 2)]
-    first = over_z([*first_parts[:3], jnp.concatenate([first_parts[3]] + columns)])
+    first_parts = list(first_parts)
+    nearest = ORDER.index(1)
+    first_parts[nearest] = jnp.concatenate([first_parts[nearest]] + columns)
+    first = over_z(first_parts)
     shared_parts = call(
         functools.partial(merge_kernel, blocks, groups),
         8,
@@ -485,10 +488,9 @@
         [pltpu.VMEM((2 * size, norb_dev), f32)],
     )(place, row_counts, shared, excess)
 
-    first, shared_parts, rest = together(first, shared_parts, rest)
-    far_three, first[3] = first[3][part:], first[3][:part]
-    columns_near = [mine[:, half + i * norb_dev:half + (i + 1) * norb_dev] for i in range(groups // 2)]
-    shared = over_z([*shared_parts[:3], jnp.concatenate([shared_parts[3]] + columns_near)])
+    first, shared_parts, rest, other_near = together(first, shared_parts, rest, other_near)
+    far_three, first[nearest] = first[nearest][part:], first[nearest][:part]
+    shared = over_z(shared_parts)
     first_own = jnp.stack(first)
     first_x = swap(first_own, 2)
     others = other_slab(jnp.concatenate(columns + [far_three]))
@@ -496,17 +498,16 @@
         functools.partial(second_edge_kernel, blocks, groups),
         8,
         part_outs,
-        [SMEM] * 5 + [VMEM] * 6,
+        [SMEM] * 5 + [VMEM] * 4,
         [pltpu.VMEM(edge_shape, f32), pltpu.VMEM(size_shape, f32)],
-    )(*lists, halo, f1, xt, tiles, edge_sum, rest)
+    )(*lists, halo, tiles, edge_sum, rest)
 
     shared, first_x, rest_parts, others = together(shared, first_x, rest_parts, others)
-    near_more, shared[3] = shared[3][part:], shared[3][:part]
     rest = over_z(rest_parts)
     first_core = over_core(first_own, first_x)
     shared_own = jnp.stack(shared)
     shared_x = swap(shared_own, 2)
-    weights = [mine, near, far_two, far_three, near_more, others]
+    weights = [mine, near, far_two, far_three, other_near, others]
     first_turned = rotate(first_own, first_x, first_core)
 
     rest, first_turned, shared_x = together(rest, first_turned, shared_x)

time: 126 us -> 124 us (0.984)
  waiting for transfers between devices: 53.8 us -> 51.9 us
  starting transfers between devices: 43.1 us -> 44.7 us
    ppermute x29, waiting for transfers between devices: 44.7 us -> 39.7 us  [swap(): return lax.ppermute(value, 'orb', [(i, i ^ bits) for i in range(orbs)])]
    ppermute x5 -> x6, waiting for transfers between devices: 9.15 us -> 12.2 us  [other_slab(): return lax.ppermute(value, 'slab', [(0, 1), (1, 0)])]
    ppermute x5 -> x6, starting transfers between devices: 7.01 us -> 8.28 us  [other_slab(): return lax.ppermute(value, 'slab', [(0, 1), (1, 0)])]
  transfers between devices with their start and end apart: 34 -> 35, of which waited for: 18 -> 19; matrix products, arithmetic and copies ran while one was open for 0% -> 0% of each run, Pallas kernels for 16% -> 16%
where the time goes in v3:
time: 124 us
  waiting for transfers between devices  51.9 us (42%)
  starting transfers between devices  44.7 us (36%)
  Pallas kernels  23.5 us (19%)
  local copies, waits for them, and re-layouts  2.76 us (2%)
    ppermute x29, waiting for transfers between devices, swap(): return lax.ppermute(value, 'orb', [(i, i ^ bits) for i in range(orbs)])  39.7 us
    ppermute x29, starting transfers between devices, swap(): return lax.ppermute(value, 'orb', [(i, i ^ bits) for i in range(orbs)])  36.4 us
    ppermute x6, waiting for transfers between devices, other_slab(): return lax.ppermute(value, 'slab', [(0, 1), (1, 0)])  12.2 us
    ppermute x6, starting transfers between devices, other_slab(): return lax.ppermute(value, 'slab', [(0, 1), (1, 0)])  8.28 us
    pallas_call x3, Pallas kernels, rotate(): call(functools.partial(rotate_kernel, groups), 12, part_outs, [SMEM] + [V...  5.53 us
    pallas_call x1, Pallas kernels, paired(): call(functools.partial(first_kernel, blocks), 16, [shaped(block_shape), s...  4.46 us
    pallas_call x1, Pallas kernels, paired(): call(functools.partial(second_kernel, blocks, groups), 18, part_outs + [s...  4.3 us
    pallas_call x1, Pallas kernels, paired(): call(functools.partial(spread_kernel, blocks, groups), 12, [out, shaped((...  2.92 us
  transfers between devices with their start and end apart: 35, of which 19 were waited for; matrix products, arithmetic and copies ran while one was open for 0% of the time, Pallas kernels for 16%

profile of v3, /device:TPU:0, one launch (start us, length us, event | category | flops | bytes accessed | tf_op | source)
XLA Modules:
  0.0 123.8 jit_solution(5903481842309193241)
XLA Ops:
  5.0 2.6 %collective-permute-start.3 = (bf16[128,512]{1,0:T(8,128)(2,1)S(1)}, bf16[128,512]{1,0:T(8,128)(2,1)S(1)}, u32[]{:S(2)}, u32[]{:S(2)}) collective-permute-start(bf16[128,512]{1,0:T(8,128)(2,1)S(1)} %get-tuple-element.112), channel_id=1, source_target_pairs={{0,2},{1,3},{2,0},{3,1},{4,6},{5,7},{6,4},{7,5},{8,10},{9,11},{10,... | collective-permute-start | bytes 393224 | tf_op jit(solution)/shard_map/ppermute | solution.py:411
  7.6 1.8 %collective-permute-start = (bf16[128,256]{1,0:T(8,128)(2,1)S(1)}, bf16[128,256]{1,0:T(8,128)(2,1)S(1)}, u32[]{:S(2)}, u32[]{:S(2)}) collective-permute-start(bf16[128,256]{1,0:T(8,128)(2,1)S(1)} %get-tuple-element.102), channel_id=1, source_target_pairs={{0,16},{16,0},{1,17},{17,1},{2,18},{18,2},{3,19},{19,3},{4,20},{20... | collective-permute-start | bytes 196616 | tf_op jit(solution)/shard_map/ppermute | solution.py:417
  9.4 2.6 %collective-permute-done.halo_ref = bf16[128,256]{1,0:T(8,128)(2,1)S(1)} collective-permute-done((bf16[128,256]{1,0:T(8,128)(2,1)S(1)}, bf16[128,256]{1,0:T(8,128)(2,1)S(1)}, u32[]{:S(2)}, u32[]{:S(2)}) %collective-permute-start) | collective-permute-done | bytes 65568 | tf_op jit(solution)/shard_map/ppermute | solution.py:417
  12.0 2.2 %collective-permute-done.4 = bf16[128,512]{1,0:T(8,128)(2,1)S(1)} collective-permute-done((bf16[128,512]{1,0:T(8,128)(2,1)S(1)}, bf16[128,512]{1,0:T(8,128)(2,1)S(1)}, u32[]{:S(2)}, u32[]{:S(2)}) %collective-permute-start.4) | collective-permute-done | bytes 131104 | tf_op jit(solution)/shard_map/ppermute | solution.py:411
  14.3 1.7 %collective-permute-start.5 = (bf16[512,256]{1,0:T(8,128)(2,1)S(1)}, bf16[512,256]{1,0:T(8,128)(2,1)S(1)}, u32[]{:S(2)}, u32[]{:S(2)}) collective-permute-start(bf16[512,256]{1,0:T(8,128)(2,1)S(1)} %slice.21), channel_id=1, source_target_pairs={{0,4},{1,5},{2,6},{3,7},{4,0},{5,1},{6,2},{7,3},{8,12},{9,13},{10,... | collective-permute-start | bytes 786440 | tf_op jit(solution)/shard_map/ppermute | solution.py:411
  16.0 2.6 %collective-permute-start.6 = (bf16[512,256]{1,0:T(8,128)(2,1)S(1)}, bf16[512,256]{1,0:T(8,128)(2,1)S(1)}, u32[]{:S(2)}, u32[]{:S(2)}) collective-permute-start(bf16[512,256]{1,0:T(8,128)(2,1)S(1)} %slice.21), channel_id=1, source_target_pairs={{0,8},{1,9},{2,10},{3,11},{4,12},{5,13},{6,14},{7,15},{8,0},{9,1},... | collective-permute-start | bytes 786440 | tf_op jit(solution)/shard_map/ppermute | solution.py:411
  18.6 4.5 %shard_map.74 = (bf16[64,128,128]{2,1,0:T(8,128)(2,1)S(1)}, bf16[2,128,128]{2,1,0:T(8,128)(2,1)S(1)}) custom-call(s32[3]{0:T(128)S(1)} %pad_add_fusion.place_ref, s32[112]{0:T(128)S(1)} %copy-done.4, s32[112]{0:T(128)S(1)} %copy-done.5, s32[64]{0:T(128)S(1)} %copy-done.3, f32[3]{0:T(128)S(1)} %copy-done.6, ...), custom_call_target="tpu_custom_call" | custom-call | flops 1000 | bytes 1000 | tf_op jit(solution)/shard_map/pallas_call | solution.py:434
  24.6 4.3 %shard_map.75 = (bf16[512,128]{1,0:T(8,128)(2,1)S(1)}, bf16[512,128]{1,0:T(8,128)(2,1)S(1)}, bf16[512,128]{1,0:T(8,128)(2,1)S(1)}, bf16[512,128]{1,0:T(8,128)(2,...) custom-call(s32[3]{0:T(128)S(1)} %pad_add_fusion.place_ref, ...), custom_call_target="tpu_custom_call" | custom-call | flops 1000 | bytes 1000 | tf_op jit(solution)/shard_map/pallas_call | solution.py:447
  29.0 1.8 %collective-permute-done.6.far_two = bf16[512,256]{1,0:T(8,128)(2,1)S(1)} collective-permute-done((bf16[512,256]{1,0:T(8,128)(2,1)S(1)}, bf16[512,256]{1,0:T(8,128)(2,1)S(1)}, u32[]{:S(2)}, u32[]{:S(2)}) %collective-permute-start.6) | collective-permute-done | bytes 262176 | tf_op jit(solution)/shard_map/ppermute | solution.py:411
  33.4 2.1 %collective-permute-start.7 = (bf16[512,128]{1,0:T(8,128)(2,1)S(1)}, bf16[512,128]{1,0:T(8,128)(2,1)S(1)}, u32[]{:S(2)}, u32[]{:S(2)}) collective-permute-start(bf16[512,128]{1,0:T(8,128)(2,1)S(1)} %get-tuple-element.119), channel_id=1, source_target_pairs={{0,12},{1,13},{2,14},{3,15},{4,8},{5,9},{6,10},{7,11},{8,4},{9,5},... | collective-permute-start | bytes 393224 | tf_op jit(solution)/shard_map/ppermute | solution.py:411
  36.5 8.7 %collective-permute-done.10.excess_ref = bf16[2048,128]{1,0:T(8,128)(2,1)S(1)} collective-permute-done((bf16[2048,128]{1,0:T(8,128)(2,1)S(1)}, bf16[2048,128]{1,0:T(8,128)(2,1)S(1)}, u32[]{:S(2)}, u32[]{:S(2)}) %collective-permute-start.10) | collective-permute-done | bytes 524320 | tf_op jit(solution)/shard_map/ppermute | solution.py:417
  51.3 3.9 %collective-permute-start.12 = (bf16[512,128]{1,0:T(8,128)(2,1)S(1)}, bf16[512,128]{1,0:T(8,128)(2,1)S(1)}, u32[]{:S(2)}, u32[]{:S(2)}) collective-permute-start(bf16[512,128]{1,0:T(8,128)(2,1)S(1)} %get-tuple-element.132), channel_id=1, source_target_pairs={{0,12},{1,13},{2,14},{3,15},{4,8},{5,9},{6,10},{7,11},{8,4},{9,5},... | collective-permute-start | bytes 393224 | tf_op jit(solution)/shard_map/ppermute | solution.py:411
  57.3 1.8 %collective-permute-done.12 = bf16[512,128]{1,0:T(8,128)(2,1)S(1)} collective-permute-done((bf16[512,128]{1,0:T(8,128)(2,1)S(1)}, bf16[512,128]{1,0:T(8,128)(2,1)S(1)}, u32[]{:S(2)}, u32[]{:S(2)}) %collective-permute-start.12) | collective-permute-done | bytes 131104 | tf_op jit(solution)/shard_map/ppermute | solution.py:411
  59.1 5.5 %collective-permute-done.13 = bf16[512,128]{1,0:T(8,128)(2,1)S(1)} collective-permute-done((bf16[512,128]{1,0:T(8,128)(2,1)S(1)}, bf16[512,128]{1,0:T(8,128)(2,1)S(1)}, u32[]{:S(2)}, u32[]{:S(2)}) %collective-permute-start.13) | collective-permute-done | bytes 131104 | tf_op jit(solution)/shard_map/ppermute | solution.py:411
  67.1 2.8 %collective-permute-start.19 = (bf16[512,128]{1,0:T(8,128)(2,1)S(1)}, bf16[512,128]{1,0:T(8,128)(2,1)S(1)}, u32[]{:S(2)}, u32[]{:S(2)}) collective-permute-start(bf16[512,128]{1,0:T(8,128)(2,1)S(1)} %get-tuple-element.149), channel_id=1, source_target_pairs={{0,4},{1,5},{2,6},{3,7},{4,0},{5,1},{6,2},{7,3},{8,12},{9,13},{10,... | collective-permute-start | bytes 393224 | tf_op jit(solution)/shard_map/ppermute | solution.py:411
  69.9 1.8 %shard_map.78 = (bf16[512,128]{1,0:T(8,128)(2,1)S(1)}, bf16[512,128]{1,0:T(8,128)(2,1)S(1)}, bf16[512,128]{1,0:T(8,128)(2,1)S(1)}, bf16[512,128]{1,0:T(8,128)(2,1)S(1)}) custom-call(s32[3]{0:T(128)S(1)} %pad_add_fusion.place_ref, bf16[4,512,128]{2,1,0:T(8,128)(2,1)S(1)} %get-tuple-element.202.own, bf16[4,512,128]{2,1,0:T(8,128)(2,1)S(1)} %collective-permute-done.15.over_x, ...), custom_call_target="tpu_custom_call" | custom-call | flops 1000 | bytes 1000 | tf_op jit(solution)/shard_map/pallas_call | solution.py:467
  71.8 2.0 %collective-permute-done.17 = bf16[512,128]{1,0:T(8,128)(2,1)S(1)} collective-permute-done((bf16[512,128]{1,0:T(8,128)(2,1)S(1)}, bf16[512,128]{1,0:T(8,128)(2,1)S(1)}, u32[]{:S(2)}, u32[]{:S(2)}) %collective-permute-start.17) | collective-permute-done | bytes 131104 | tf_op jit(solution)/shard_map/ppermute | solution.py:411
  73.8 4.8 %collective-permute-done.18 = bf16[512,128]{1,0:T(8,128)(2,1)S(1)} collective-permute-done((bf16[512,128]{1,0:T(8,128)(2,1)S(1)}, bf16[512,128]{1,0:T(8,128)(2,1)S(1)}, u32[]{:S(2)}, u32[]{:S(2)}) %collective-permute-start.18) | collective-permute-done | bytes 131104 | tf_op jit(solution)/shard_map/ppermute | solution.py:411
  82.1 2.8 %collective-permute-start.24 = (bf16[512,128]{1,0:T(8,128)(2,1)S(1)}, bf16[512,128]{1,0:T(8,128)(2,1)S(1)}, u32[]{:S(2)}, u32[]{:S(2)}) collective-permute-start(bf16[512,128]{1,0:T(8,128)(2,1)S(1)} %get-tuple-element.164), channel_id=1, source_target_pairs={{0,4},{1,5},{2,6},{3,7},{4,0},{5,1},{6,2},{7,3},{8,12},{9,13},{10,... | collective-permute-start | bytes 393224 | tf_op jit(solution)/shard_map/ppermute | solution.py:411
  84.9 1.9 %shard_map.79 = (bf16[512,128]{1,0:T(8,128)(2,1)S(1)}, bf16[512,128]{1,0:T(8,128)(2,1)S(1)}, bf16[512,128]{1,0:T(8,128)(2,1)S(1)}, bf16[512,128]{1,0:T(8,128)(2,1)S(1)}) custom-call(s32[3]{0:T(128)S(1)} %pad_add_fusion.place_ref, bf16[4,512,128]{2,1,0:T(8,128)(2,1)S(1)} %get-tuple-element.200.own, bf16[4,512,128]{2,1,0:T(8,128)(2,1)S(1)} %collective-permute-done.21.over_x, ...), custom_call_target="tpu_custom_call" | custom-call | flops 1000 | bytes 1000 | tf_op jit(solution)/shard_map/pallas_call | solution.py:467
  86.7 2.0 %collective-permute-done.22.refs_1_ = bf16[512,128]{1,0:T(8,128)(2,1)S(1)} collective-permute-done((bf16[512,128]{1,0:T(8,128)(2,1)S(1)}, bf16[512,128]{1,0:T(8,128)(2,1)S(1)}, u32[]{:S(2)}, u32[]{:S(2)}) %collective-permute-start.22) | collective-permute-done | bytes 131104 | tf_op jit(solution)/shard_map/ppermute | solution.py:411
  88.7 5.0 %collective-permute-done.23.refs_2_ = bf16[512,128]{1,0:T(8,128)(2,1)S(1)} collective-permute-done((bf16[512,128]{1,0:T(8,128)(2,1)S(1)}, bf16[512,128]{1,0:T(8,128)(2,1)S(1)}, u32[]{:S(2)}, u32[]{:S(2)}) %collective-permute-start.23) | collective-permute-done | bytes 131104 | tf_op jit(solution)/shard_map/ppermute | solution.py:411
  94.2 2.1 %collective-permute-start.27 = (bf16[512,128]{1,0:T(8,128)(2,1)S(1)}, bf16[512,128]{1,0:T(8,128)(2,1)S(1)}, u32[]{:S(2)}, u32[]{:S(2)}) collective-permute-start(bf16[512,128]{1,0:T(8,128)(2,1)S(1)} %get-tuple-element.179), channel_id=1, source_target_pairs={{0,12},{1,13},{2,14},{3,15},{4,8},{5,9},{6,10},{7,11},{8,4},{9,5},... | collective-permute-start | bytes 393224 | tf_op jit(solution)/shard_map/ppermute | solution.py:411
  96.3 2.4 %collective-permute-start.29 = (bf16[512,128]{1,0:T(8,128)(2,1)S(1)}, bf16[512,128]{1,0:T(8,128)(2,1)S(1)}, u32[]{:S(2)}, u32[]{:S(2)}) collective-permute-start(bf16[512,128]{1,0:T(8,128)(2,1)S(1)} %get-tuple-element.181), channel_id=1, source_target_pairs={{0,4},{1,5},{2,6},{3,7},{4,0},{5,1},{6,2},{7,3},{8,12},{9,13},{10,... | collective-permute-start | bytes 393224 | tf_op jit(solution)/shard_map/ppermute | solution.py:411
  98.6 1.8 %shard_map.80 = (bf16[512,128]{1,0:T(8,128)(2,1)S(1)}, bf16[512,128]{1,0:T(8,128)(2,1)S(1)}, bf16[512,128]{1,0:T(8,128)(2,1)S(1)}, bf16[512,128]{1,0:T(8,128)(2,1)S(1)}) custom-call(s32[3]{0:T(128)S(1)} %pad_add_fusion.place_ref, bf16[4,512,128]{2,1,0:T(8,128)(2,1)S(1)} %get-tuple-element.198.own, bf16[4,512,128]{2,1,0:T(8,128)(2,1)S(1)} %collective-permute-done.26.over_x, ...), custom_call_target="tpu_custom_call" | custom-call | flops 1000 | bytes 1000 | tf_op jit(solution)/shard_map/pallas_call | solution.py:467
  100.5 2.0 %collective-permute-done.27.refs_5_ = bf16[512,128]{1,0:T(8,128)(2,1)S(1)} collective-permute-done((bf16[512,128]{1,0:T(8,128)(2,1)S(1)}, bf16[512,128]{1,0:T(8,128)(2,1)S(1)}, u32[]{:S(2)}, u32[]{:S(2)}) %collective-permute-start.27) | collective-permute-done | bytes 131104 | tf_op jit(solution)/shard_map/ppermute | solution.py:411
  102.5 5.1 %collective-permute-done.28.refs_6_ = bf16[512,128]{1,0:T(8,128)(2,1)S(1)} collective-permute-done((bf16[512,128]{1,0:T(8,128)(2,1)S(1)}, bf16[512,128]{1,0:T(8,128)(2,1)S(1)}, u32[]{:S(2)}, u32[]{:S(2)}) %collective-permute-start.28) | collective-permute-done | bytes 131104 | tf_op jit(solution)/shard_map/ppermute | solution.py:411
  108.9 2.0 %collective-permute-start.32 = (bf16[512,128]{1,0:T(8,128)(2,1)S(1)}, bf16[512,128]{1,0:T(8,128)(2,1)S(1)}, u32[]{:S(2)}, u32[]{:S(2)}) collective-permute-start(bf16[512,128]{1,0:T(8,128)(2,1)S(1)} %get-tuple-element.194), channel_id=1, source_target_pairs={{0,12},{1,13},{2,14},{3,15},{4,8},{5,9},{6,10},{7,11},{8,4},{9,5},... | collective-permute-start | bytes 393224 | tf_op jit(solution)/shard_map/ppermute | solution.py:411
  110.9 2.4 %collective-permute-start.34 = (bf16[512,128]{1,0:T(8,128)(2,1)S(1)}, bf16[512,128]{1,0:T(8,128)(2,1)S(1)}, u32[]{:S(2)}, u32[]{:S(2)}) collective-permute-start(bf16[512,128]{1,0:T(8,128)(2,1)S(1)} %get-tuple-element.196), channel_id=1, source_target_pairs={{0,4},{1,5},{2,6},{3,7},{4,0},{5,1},{6,2},{7,3},{8,12},{9,13},{10,... | collective-permute-start | bytes 393224 | tf_op jit(solution)/shard_map/ppermute | solution.py:411
  113.3 2.9 %shard_map.81 = (bf16[128,8192]{1,0:T(8,128)(2,1)}, f32[2,128,128]{2,1,0:T(8,128)S(1)}) custom-call(s32[3]{0:T(128)S(1)} %pad_add_fusion.place_ref, s32[64]{0:T(128)S(1)} %copy-done.3, bf16[512,128]{1,0:T(8,128)(2,1)S(1)} %get-tuple-element.174.refs_0_, bf16[512,128]{1,0:T(8,128)(2,1)S(1)} %collective-permute-done.22.refs_1_, ...), custom_call_target="tpu_custom_call" | custom-call | flops 1000 | bytes 1000 | tf_op jit(solution)/shard_map/pallas_call | solution.py:530
  117.2 4.1 %collective-permute-done.33.refs_2_ = bf16[512,128]{1,0:T(8,128)(2,1)S(1)} collective-permute-done((bf16[512,128]{1,0:T(8,128)(2,1)S(1)}, bf16[512,128]{1,0:T(8,128)(2,1)S(1)}, u32[]{:S(2)}, u32[]{:S(2)}) %collective-permute-start.33) | collective-permute-done | bytes 131104 | tf_op jit(solution)/shard_map/ppermute | solution.py:411
  121.5 2.3 %shard_map.82 = bf16[128,8192]{1,0:T(8,128)(2,1)} custom-call(s32[3]{0:T(128)S(1)} %pad_add_fusion.place_ref, s32[64]{0:T(128)S(1)} %copy-done.3, bf16[128,8192]{1,0:T(8,128)(2,1)} %get-tuple-element.191.done_hbm, f32[2,128,128]{2,1,0:T(8,128)S(1)} %get-tuple-element.192.seam_ref, ...), custom_call_target="tpu_custom_call", output_to_operand_aliasing={{}: (2, {})} | custom-call | flops 1000 | bytes 1000 | tf_op jit(solution)/shard_map/pallas_call | solution.py:542
  (80 shorter events, 27.3 us)
Async XLA Ops:
  4.5 7.5 %collective-permute-start.2 = (bf16[128,512]{1,0:T(8,128)(2,1)S(1)}, bf16[128,512]{1,0:T(8,128)(2,1)S(1)}, u32[]{:S(2)}, u32[]{:S(2)}) collective-permute-start(bf16[128,512]{1,0:T(8,128)(2,1)S(1)} %get-tuple-element.111), channel_id=1, source_target_pairs={{0,1},{1,0},{2,3},{3,2},{4,5},{5,4},{6,7},{7,6},{8,9},{9,8},{10,11... | collective-permute-start | bytes 393224 | tf_op jit(solution)/shard_map/ppermute | solution.py:411
  5.0 7.0 %collective-permute-start.3 = (bf16[128,512]{1,0:T(8,128)(2,1)S(1)}, bf16[128,512]{1,0:T(8,128)(2,1)S(1)}, u32[]{:S(2)}, u32[]{:S(2)}) collective-permute-start(bf16[128,512]{1,0:T(8,128)(2,1)S(1)} %get-tuple-element.112), channel_id=1, source_target_pairs={{0,2},{1,3},{2,0},{3,1},{4,6},{5,7},{6,4},{7,5},{8,10},{9,11},{10,... | collective-permute-start | bytes 393224 | tf_op jit(solution)/shard_map/ppermute | solution.py:411
  7.5 6.6 %collective-permute-start.4 = (bf16[128,512]{1,0:T(8,128)(2,1)S(1)}, bf16[128,512]{1,0:T(8,128)(2,1)S(1)}, u32[]{:S(2)}, u32[]{:S(2)}) collective-permute-start(bf16[128,512]{1,0:T(8,128)(2,1)S(1)} %get-tuple-element.113), channel_id=1, source_target_pairs={{0,3},{1,2},{2,1},{3,0},{4,7},{5,6},{6,5},{7,4},{8,11},{9,10},{10,... | collective-permute-start | bytes 393224 | tf_op jit(solution)/shard_map/ppermute | solution.py:411
  14.3 14.7 %collective-permute-start.5 = (bf16[512,256]{1,0:T(8,128)(2,1)S(1)}, bf16[512,256]{1,0:T(8,128)(2,1)S(1)}, u32[]{:S(2)}, u32[]{:S(2)}) collective-permute-start(bf16[512,256]{1,0:T(8,128)(2,1)S(1)} %slice.21), channel_id=1, source_target_pairs={{0,4},{1,5},{2,6},{3,7},{4,0},{5,1},{6,2},{7,3},{8,12},{9,13},{10,... | collective-permute-start | bytes 786440 | tf_op jit(solution)/shard_map/ppermute | solution.py:411
  16.0 14.8 %collective-permute-start.6 = (bf16[512,256]{1,0:T(8,128)(2,1)S(1)}, bf16[512,256]{1,0:T(8,128)(2,1)S(1)}, u32[]{:S(2)}, u32[]{:S(2)}) collective-permute-start(bf16[512,256]{1,0:T(8,128)(2,1)S(1)} %slice.21), channel_id=1, source_target_pairs={{0,8},{1,9},{2,10},{3,11},{4,12},{5,13},{6,14},{7,15},{8,0},{9,1},... | collective-permute-start | bytes 786440 | tf_op jit(solution)/shard_map/ppermute | solution.py:411
  23.1 5.9 %collective-permute-start.1 = (bf16[2,128,128]{2,1,0:T(8,128)(2,1)S(1)}, bf16[2,128,128]{2,1,0:T(8,128)(2,1)S(1)}, u32[]{:S(2)}, u32[]{:S(2)}) collective-permute-start(bf16[2,128,128]{2,1,0:T(8,128)(2,1)S(1)} %get-tuple-element.105), channel_id=1, source_target_pairs={{0,16},{16,0},{1,17},{17,1},{2,18},{18,2},{3,19},{19,3},{4,20},{20... | collective-permute-start | bytes 196616 | tf_op jit(solution)/shard_map/ppermute | solution.py:417
  30.8 14.3 %collective-permute-start.10 = (bf16[2048,128]{1,0:T(8,128)(2,1)S(1)}, bf16[2048,128]{1,0:T(8,128)(2,1)S(1)}, u32[]{:S(2)}, u32[]{:S(2)}) collective-permute-start(bf16[2048,128]{1,0:T(8,128)(2,1)S(1)} %get-tuple-element.124), channel_id=1, source_target_pairs={{0,16},{16,0},{1,17},{17,1},{2,18},{18,2},{3,19},{19,3},{4,20},{20... | collective-permute-start | bytes 1572872 | tf_op jit(solution)/shard_map/ppermute | solution.py:417
  32.4 15.5 %collective-permute-start.9 = (bf16[1536,128]{1,0:T(8,128)(2,1)S(1)}, bf16[1536,128]{1,0:T(8,128)(2,1)S(1)}, u32[]{:S(2)}, u32[]{:S(2)}) collective-permute-start(bf16[1536,128]{1,0:T(8,128)(2,1)S(1)} %pad_maximum_fusion.8), channel_id=1, source_target_pairs={{0,4},{1,5},{2,6},{3,7},{4,0},{5,1},{6,2},{7,3},{8,12},{9,13},{10,... | collective-permute-start | bytes 1179656 | tf_op jit(solution)/shard_map/ppermute | solution.py:411
  32.9 15.0 %collective-permute-start.11 = (bf16[512,256]{1,0:T(8,128)(2,1)S(1)}, bf16[512,256]{1,0:T(8,128)(2,1)S(1)}, u32[]{:S(2)}, u32[]{:S(2)}) collective-permute-start(bf16[512,256]{1,0:T(8,128)(2,1)S(1)} %collective-permute-done.5.near), channel_id=1, source_target_pairs={{0,16},{16,0},{1,17},{17,1},{2,18},{18,2},{3,19},{19,3},{4,20},{20... | collective-permute-start | bytes 786440 | tf_op jit(solution)/shard_map/ppermute | solution.py:417
  33.4 13.9 %collective-permute-start.7 = (bf16[512,128]{1,0:T(8,128)(2,1)S(1)}, bf16[512,128]{1,0:T(8,128)(2,1)S(1)}, u32[]{:S(2)}, u32[]{:S(2)}) collective-permute-start(bf16[512,128]{1,0:T(8,128)(2,1)S(1)} %get-tuple-element.119), channel_id=1, source_target_pairs={{0,12},{1,13},{2,14},{3,15},{4,8},{5,9},{6,10},{7,11},{8,4},{9,5},... | collective-permute-start | bytes 393224 | tf_op jit(solution)/shard_map/ppermute | solution.py:411
  35.5 11.8 %collective-permute-start.8 = (bf16[512,128]{1,0:T(8,128)(2,1)S(1)}, bf16[512,128]{1,0:T(8,128)(2,1)S(1)}, u32[]{:S(2)}, u32[]{:S(2)}) collective-permute-start(bf16[512,128]{1,0:T(8,128)(2,1)S(1)} %get-tuple-element.120), channel_id=1, source_target_pairs={{0,8},{1,9},{2,10},{3,11},{4,12},{5,13},{6,14},{7,15},{8,0},{9,1},... | collective-permute-start | bytes 393224 | tf_op jit(solution)/shard_map/ppermute | solution.py:411
  48.1 16.6 %collective-permute-start.15 = (bf16[4,512,128]{2,1,0:T(8,128)(2,1)S(1)}, bf16[4,512,128]{2,1,0:T(8,128)(2,1)S(1)}, u32[]{:S(2)}, u32[]{:S(2)}) collective-permute-start(bf16[4,512,128]{2,1,0:T(8,128)(2,1)S(1)} %get-tuple-element.202.own), channel_id=1, source_target_pairs={{0,2},{1,3},{2,0},{3,1},{4,6},{5,7},{6,4},{7,5},{8,10},{9,11},{10,... | collective-permute-start | bytes 1572872 | tf_op jit(solution)/shard_map/ppermute | solution.py:411
  49.7 14.9 %collective-permute-start.16 = (bf16[2048,128]{1,0:T(8,128)(2,1)S(1)}, bf16[2048,128]{1,0:T(8,128)(2,1)S(1)}, u32[]{:S(2)}, u32[]{:S(2)}) collective-permute-start(bf16[2048,128]{1,0:T(8,128)(2,1)S(1)} %pad_maximum_fusion.4), channel_id=1, source_target_pairs={{0,16},{16,0},{1,17},{17,1},{2,18},{18,2},{3,19},{19,3},{4,20},{20... | collective-permute-start | bytes 1572872 | tf_op jit(solution)/shard_map/ppermute | solution.py:417
  51.3 7.8 %collective-permute-start.12 = (bf16[512,128]{1,0:T(8,128)(2,1)S(1)}, bf16[512,128]{1,0:T(8,128)(2,1)S(1)}, u32[]{:S(2)}, u32[]{:S(2)}) collective-permute-start(bf16[512,128]{1,0:T(8,128)(2,1)S(1)} %get-tuple-element.132), channel_id=1, source_target_pairs={{0,12},{1,13},{2,14},{3,15},{4,8},{5,9},{6,10},{7,11},{8,4},{9,5},... | collective-permute-start | bytes 393224 | tf_op jit(solution)/shard_map/ppermute | solution.py:411
  55.2 9.4 %collective-permute-start.13 = (bf16[512,128]{1,0:T(8,128)(2,1)S(1)}, bf16[512,128]{1,0:T(8,128)(2,1)S(1)}, u32[]{:S(2)}, u32[]{:S(2)}) collective-permute-start(bf16[512,128]{1,0:T(8,128)(2,1)S(1)} %get-tuple-element.133), channel_id=1, source_target_pairs={{0,8},{1,9},{2,10},{3,11},{4,12},{5,13},{6,14},{7,15},{8,0},{9,1},... | collective-permute-start | bytes 393224 | tf_op jit(solution)/shard_map/ppermute | solution.py:411
  55.2 9.4 %collective-permute-start.14 = (bf16[512,128]{1,0:T(8,128)(2,1)S(1)}, bf16[512,128]{1,0:T(8,128)(2,1)S(1)}, u32[]{:S(2)}, u32[]{:S(2)}) collective-permute-start(bf16[512,128]{1,0:T(8,128)(2,1)S(1)} %get-tuple-element.134), channel_id=1, source_target_pairs={{0,4},{1,5},{2,6},{3,7},{4,0},{5,1},{6,2},{7,3},{8,12},{9,13},{10,... | collective-permute-start | bytes 393224 | tf_op jit(solution)/shard_map/ppermute | solution.py:411
  65.0 14.4 %collective-permute-start.21 = (bf16[4,512,128]{2,1,0:T(8,128)(2,1)S(1)}, bf16[4,512,128]{2,1,0:T(8,128)(2,1)S(1)}, u32[]{:S(2)}, u32[]{:S(2)}) collective-permute-start(bf16[4,512,128]{2,1,0:T(8,128)(2,1)S(1)} %get-tuple-element.200.own), channel_id=1, source_target_pairs={{0,2},{1,3},{2,0},{3,1},{4,6},{5,7},{6,4},{7,5},{8,10},{9,11},{10,... | collective-permute-start | bytes 1572872 | tf_op jit(solution)/shard_map/ppermute | solution.py:411
  65.6 8.3 %collective-permute-start.17 = (bf16[512,128]{1,0:T(8,128)(2,1)S(1)}, bf16[512,128]{1,0:T(8,128)(2,1)S(1)}, u32[]{:S(2)}, u32[]{:S(2)}) collective-permute-start(bf16[512,128]{1,0:T(8,128)(2,1)S(1)} %get-tuple-element.147), channel_id=1, source_target_pairs={{0,12},{1,13},{2,14},{3,15},{4,8},{5,9},{6,10},{7,11},{8,4},{9,5},... | collective-permute-start | bytes 393224 | tf_op jit(solution)/shard_map/ppermute | solution.py:411
  67.1 11.5 %collective-permute-start.18 = (bf16[512,128]{1,0:T(8,128)(2,1)S(1)}, bf16[512,128]{1,0:T(8,128)(2,1)S(1)}, u32[]{:S(2)}, u32[]{:S(2)}) collective-permute-start(bf16[512,128]{1,0:T(8,128)(2,1)S(1)} %get-tuple-element.148), channel_id=1, source_target_pairs={{0,8},{1,9},{2,10},{3,11},{4,12},{5,13},{6,14},{7,15},{8,0},{9,1},... | collective-permute-start | bytes 393224 | tf_op jit(solution)/shard_map/ppermute | solution.py:411
  67.1 11.5 %collective-permute-start.19 = (bf16[512,128]{1,0:T(8,128)(2,1)S(1)}, bf16[512,128]{1,0:T(8,128)(2,1)S(1)}, u32[]{:S(2)}, u32[]{:S(2)}) collective-permute-start(bf16[512,128]{1,0:T(8,128)(2,1)S(1)} %get-tuple-element.149), channel_id=1, source_target_pairs={{0,4},{1,5},{2,6},{3,7},{4,0},{5,1},{6,2},{7,3},{8,12},{9,13},{10,... | collective-permute-start | bytes 393224 | tf_op jit(solution)/shard_map/ppermute | solution.py:411
  79.4 5.4 %collective-permute-start.25 = (bf16[2,4,512,128]{3,2,1,0:T(8,128)(2,1)S(1)}, bf16[2,4,512,128]{3,2,1,0:T(8,128)(2,1)S(1)}, u32[]{:S(2)}, u32[]{:S(2)}) collective-permute-start(bf16[2,4,512,128]{3,2,1,0:T(8,128)(2,1)S(1)} %pad_maximum_fusion.1), channel_id=1, source_target_pairs={{0,1},{1,0},{2,3},{3,2},{4,5},{5,4},{6,7},{7,6},{8,9},{9,8},{10,11... | collective-permute-start | bytes 3145736 | tf_op jit(solution)/shard_map/ppermute | solution.py:411
  79.6 14.4 %collective-permute-start.26 = (bf16[4,512,128]{2,1,0:T(8,128)(2,1)S(1)}, bf16[4,512,128]{2,1,0:T(8,128)(2,1)S(1)}, u32[]{:S(2)}, u32[]{:S(2)}) collective-permute-start(bf16[4,512,128]{2,1,0:T(8,128)(2,1)S(1)} %get-tuple-element.198.own), channel_id=1, source_target_pairs={{0,2},{1,3},{2,0},{3,1},{4,6},{5,7},{6,4},{7,5},{8,10},{9,11},{10,... | collective-permute-start | bytes 1572872 | tf_op jit(solution)/shard_map/ppermute | solution.py:411
  80.5 8.3 %collective-permute-start.22 = (bf16[512,128]{1,0:T(8,128)(2,1)S(1)}, bf16[512,128]{1,0:T(8,128)(2,1)S(1)}, u32[]{:S(2)}, u32[]{:S(2)}) collective-permute-start(bf16[512,128]{1,0:T(8,128)(2,1)S(1)} %get-tuple-element.162), channel_id=1, source_target_pairs={{0,12},{1,13},{2,14},{3,15},{4,8},{5,9},{6,10},{7,11},{8,4},{9,5},... | collective-permute-start | bytes 393224 | tf_op jit(solution)/shard_map/ppermute | solution.py:411
  82.1 11.7 %collective-permute-start.23 = (bf16[512,128]{1,0:T(8,128)(2,1)S(1)}, bf16[512,128]{1,0:T(8,128)(2,1)S(1)}, u32[]{:S(2)}, u32[]{:S(2)}) collective-permute-start(bf16[512,128]{1,0:T(8,128)(2,1)S(1)} %get-tuple-element.163), channel_id=1, source_target_pairs={{0,8},{1,9},{2,10},{3,11},{4,12},{5,13},{6,14},{7,15},{8,0},{9,1},... | collective-permute-start | bytes 393224 | tf_op jit(solution)/shard_map/ppermute | solution.py:411
  82.1 11.7 %collective-permute-start.24 = (bf16[512,128]{1,0:T(8,128)(2,1)S(1)}, bf16[512,128]{1,0:T(8,128)(2,1)S(1)}, u32[]{:S(2)}, u32[]{:S(2)}) collective-permute-start(bf16[512,128]{1,0:T(8,128)(2,1)S(1)} %get-tuple-element.164), channel_id=1, source_target_pairs={{0,4},{1,5},{2,6},{3,7},{4,0},{5,1},{6,2},{7,3},{8,12},{9,13},{10,... | collective-permute-start | bytes 393224 | tf_op jit(solution)/shard_map/ppermute | solution.py:411
  94.2 8.3 %collective-permute-start.27 = (bf16[512,128]{1,0:T(8,128)(2,1)S(1)}, bf16[512,128]{1,0:T(8,128)(2,1)S(1)}, u32[]{:S(2)}, u32[]{:S(2)}) collective-permute-start(bf16[512,128]{1,0:T(8,128)(2,1)S(1)} %get-tuple-element.179), channel_id=1, source_target_pairs={{0,12},{1,13},{2,14},{3,15},{4,8},{5,9},{6,10},{7,11},{8,4},{9,5},... | collective-permute-start | bytes 393224 | tf_op jit(solution)/shard_map/ppermute | solution.py:411
  96.3 11.3 %collective-permute-start.28 = (bf16[512,128]{1,0:T(8,128)(2,1)S(1)}, bf16[512,128]{1,0:T(8,128)(2,1)S(1)}, u32[]{:S(2)}, u32[]{:S(2)}) collective-permute-start(bf16[512,128]{1,0:T(8,128)(2,1)S(1)} %get-tuple-element.180), channel_id=1, source_target_pairs={{0,8},{1,9},{2,10},{3,11},{4,12},{5,13},{6,14},{7,15},{8,0},{9,1},... | collective-permute-start | bytes 393224 | tf_op jit(solution)/shard_map/ppermute | solution.py:411
  96.3 11.3 %collective-permute-start.29 = (bf16[512,128]{1,0:T(8,128)(2,1)S(1)}, bf16[512,128]{1,0:T(8,128)(2,1)S(1)}, u32[]{:S(2)}, u32[]{:S(2)}) collective-permute-start(bf16[512,128]{1,0:T(8,128)(2,1)S(1)} %get-tuple-element.181), channel_id=1, source_target_pairs={{0,4},{1,5},{2,6},{3,7},{4,0},{5,1},{6,2},{7,3},{8,12},{9,13},{10,... | collective-permute-start | bytes 393224 | tf_op jit(solution)/shard_map/ppermute | solution.py:411
  107.6 13.9 %collective-permute-start.31 = (bf16[2048,128]{1,0:T(8,128)(2,1)S(1)}, bf16[2048,128]{1,0:T(8,128)(2,1)S(1)}, u32[]{:S(2)}, u32[]{:S(2)}) collective-permute-start(bf16[2048,128]{1,0:T(8,128)(2,1)S(1)} %pad_maximum_fusion.7), channel_id=1, source_target_pairs={{0,16},{16,0},{1,17},{17,1},{2,18},{18,2},{3,19},{19,3},{4,20},{20... | collective-permute-start | bytes 1572872 | tf_op jit(solution)/shard_map/ppermute | solution.py:417
  108.9 8.3 %collective-permute-start.32 = (bf16[512,128]{1,0:T(8,128)(2,1)S(1)}, bf16[512,128]{1,0:T(8,128)(2,1)S(1)}, u32[]{:S(2)}, u32[]{:S(2)}) collective-permute-start(bf16[512,128]{1,0:T(8,128)(2,1)S(1)} %get-tuple-element.194), channel_id=1, source_target_pairs={{0,12},{1,13},{2,14},{3,15},{4,8},{5,9},{6,10},{7,11},{8,4},{9,5},... | collective-permute-start | bytes 393224 | tf_op jit(solution)/shard_map/ppermute | solution.py:411
  110.9 10.4 %collective-permute-start.33 = (bf16[512,128]{1,0:T(8,128)(2,1)S(1)}, bf16[512,128]{1,0:T(8,128)(2,1)S(1)}, u32[]{:S(2)}, u32[]{:S(2)}) collective-permute-start(bf16[512,128]{1,0:T(8,128)(2,1)S(1)} %get-tuple-element.195), channel_id=1, source_target_pairs={{0,8},{1,9},{2,10},{3,11},{4,12},{5,13},{6,14},{7,15},{8,0},{9,1},... | collective-permute-start | bytes 393224 | tf_op jit(solution)/shard_map/ppermute | solution.py:411
  110.9 10.4 %collective-permute-start.34 = (bf16[512,128]{1,0:T(8,128)(2,1)S(1)}, bf16[512,128]{1,0:T(8,128)(2,1)S(1)}, u32[]{:S(2)}, u32[]{:S(2)}) collective-permute-start(bf16[512,128]{1,0:T(8,128)(2,1)S(1)} %get-tuple-element.196), channel_id=1, source_target_pairs={{0,4},{1,5},{2,6},{3,7},{4,0},{5,1},{6,2},{7,3},{8,12},{9,13},{10,... | collective-permute-start | bytes 393224 | tf_op jit(solution)/shard_map/ppermute | solution.py:411
  (10 other events, 96.0 us)

commit v4 on v3

--- a/solution.py
+++ b/solution.py
@@ -119,7 +119,7 @@
         acc_ref[r] = product(tiles_ref[r], source_ref[r]) - more(r)
         return 0
 
-    loop(0, blocks, diagonal, 16)
+    loop(0, blocks, diagonal, 32)
     listed = tiles_ref.shape[0]
 
     def extra(k, _):
@@ -127,7 +127,7 @@
         extra_ref[k - blocks] = product(tiles_ref[k], source_ref[col])
         return 0
 
-    loop(blocks, listed, extra, 16)
+    loop(blocks, listed, extra, 24)
 
     def gather(k, _):
         inside = (cols_ref[k] >= 0) & (cols_ref[k] < blocks)

time: 124 us -> 124 us (level)
    ppermute x29, waiting for transfers between devices: 39.7 us -> 41.2 us  [swap(): return lax.ppermute(value, 'orb', [(i, i ^ bits) for i in range(orbs)])]
    ppermute x6, waiting for transfers between devices: 12.2 us -> 10.8 us  [other_slab(): return lax.ppermute(value, 'slab', [(0, 1), (1, 0)])]
  transfers between devices with their start and end apart: 35 -> 35, of which waited for: 19 -> 18; matrix products, arithmetic and copies ran while one was open for 0% -> 0% of each run, Pallas kernels for 16% -> 15%
where the time goes in v4:
time: 124 us
  waiting for transfers between devices  52 us (42%)
  starting transfers between devices  45.3 us (37%)
  Pallas kernels  23.1 us (19%)
  local copies, waits for them, and re-layouts  2.76 us (2%)
    ppermute x29, waiting for transfers between devices, swap(): return lax.ppermute(value, 'orb', [(i, i ^ bits) for i in range(orbs)])  41.2 us
    ppermute x29, starting transfers between devices, swap(): return lax.ppermute(value, 'orb', [(i, i ^ bits) for i in range(orbs)])  36.4 us
    ppermute x6, waiting for transfers between devices, other_slab(): return lax.ppermute(value, 'slab', [(0, 1), (1, 0)])  10.8 us
    ppermute x6, starting transfers between devices, other_slab(): return lax.ppermute(value, 'slab', [(0, 1), (1, 0)])  8.86 us
    pallas_call x3, Pallas kernels, rotate(): call(functools.partial(rotate_kernel, groups), 12, part_outs, [SMEM] + [V...  5.53 us
    pallas_call x1, Pallas kernels, paired(): call(functools.partial(first_kernel, blocks), 16, [shaped(block_shape), s...  4.03 us
    pallas_call x1, Pallas kernels, paired(): call(functools.partial(second_kernel, blocks, groups), 18, part_outs + [s...  3.98 us
    pallas_call x1, Pallas kernels, paired(): call(functools.partial(spread_kernel, blocks, groups), 12, [out, shaped((...  2.91 us
  transfers between devices with their start and end apart: 35, of which 18 were waited for; matrix products, arithmetic and copies ran while one was open for 0% of the time, Pallas kernels for 15%

profile of v4, /device:TPU:0, one launch (start us, length us, event | category | flops | bytes accessed | tf_op | source)
XLA Modules:
  0.0 124.1 jit_solution(16922643943479486756)
XLA Ops:
  5.0 2.6 %collective-permute-start.3 = (bf16[128,512]{1,0:T(8,128)(2,1)S(1)}, bf16[128,512]{1,0:T(8,128)(2,1)S(1)}, u32[]{:S(2)}, u32[]{:S(2)}) collective-permute-start(bf16[128,512]{1,0:T(8,128)(2,1)S(1)} %get-tuple-element.112), channel_id=1, source_target_pairs={{0,2},{1,3},{2,0},{3,1},{4,6},{5,7},{6,4},{7,5},{8,10},{9,11},{10,... | collective-permute-start | bytes 393224 | tf_op jit(solution)/shard_map/ppermute | solution.py:411
  7.6 1.8 %collective-permute-start = (bf16[128,256]{1,0:T(8,128)(2,1)S(1)}, bf16[128,256]{1,0:T(8,128)(2,1)S(1)}, u32[]{:S(2)}, u32[]{:S(2)}) collective-permute-start(bf16[128,256]{1,0:T(8,128)(2,1)S(1)} %get-tuple-element.102), channel_id=1, source_target_pairs={{0,16},{16,0},{1,17},{17,1},{2,18},{18,2},{3,19},{19,3},{4,20},{20... | collective-permute-start | bytes 196616 | tf_op jit(solution)/shard_map/ppermute | solution.py:417
  9.4 2.6 %collective-permute-done.halo_ref = bf16[128,256]{1,0:T(8,128)(2,1)S(1)} collective-permute-done((bf16[128,256]{1,0:T(8,128)(2,1)S(1)}, bf16[128,256]{1,0:T(8,128)(2,1)S(1)}, u32[]{:S(2)}, u32[]{:S(2)}) %collective-permute-start) | collective-permute-done | bytes 65568 | tf_op jit(solution)/shard_map/ppermute | solution.py:417
  12.0 2.2 %collective-permute-done.4 = bf16[128,512]{1,0:T(8,128)(2,1)S(1)} collective-permute-done((bf16[128,512]{1,0:T(8,128)(2,1)S(1)}, bf16[128,512]{1,0:T(8,128)(2,1)S(1)}, u32[]{:S(2)}, u32[]{:S(2)}) %collective-permute-start.4) | collective-permute-done | bytes 131104 | tf_op jit(solution)/shard_map/ppermute | solution.py:411
  16.0 2.6 %collective-permute-start.6 = (bf16[512,256]{1,0:T(8,128)(2,1)S(1)}, bf16[512,256]{1,0:T(8,128)(2,1)S(1)}, u32[]{:S(2)}, u32[]{:S(2)}) collective-permute-start(bf16[512,256]{1,0:T(8,128)(2,1)S(1)} %slice.21), channel_id=1, source_target_pairs={{0,8},{1,9},{2,10},{3,11},{4,12},{5,13},{6,14},{7,15},{8,0},{9,1},... | collective-permute-start | bytes 786440 | tf_op jit(solution)/shard_map/ppermute | solution.py:411
  18.6 4.0 %shard_map.74 = (bf16[64,128,128]{2,1,0:T(8,128)(2,1)S(1)}, bf16[2,128,128]{2,1,0:T(8,128)(2,1)S(1)}) custom-call(s32[3]{0:T(128)S(1)} %pad_add_fusion.place_ref, s32[112]{0:T(128)S(1)} %copy-done.4, s32[112]{0:T(128)S(1)} %copy-done.5, s32[64]{0:T(128)S(1)} %copy-done.3, f32[3]{0:T(128)S(1)} %copy-done.6, ...), custom_call_target="tpu_custom_call" | custom-call | flops 1000 | bytes 1000 | tf_op jit(solution)/shard_map/pallas_call | solution.py:434
  24.2 4.0 %shard_map.75 = (bf16[512,128]{1,0:T(8,128)(2,1)S(1)}, bf16[512,128]{1,0:T(8,128)(2,1)S(1)}, bf16[512,128]{1,0:T(8,128)(2,1)S(1)}, bf16[512,128]{1,0:T(8,128)(2,...) custom-call(s32[3]{0:T(128)S(1)} %pad_add_fusion.place_ref, ...), custom_call_target="tpu_custom_call" | custom-call | flops 1000 | bytes 1000 | tf_op jit(solution)/shard_map/pallas_call | solution.py:447
  28.2 2.5 %collective-permute-done.6.far_two = bf16[512,256]{1,0:T(8,128)(2,1)S(1)} collective-permute-done((bf16[512,256]{1,0:T(8,128)(2,1)S(1)}, bf16[512,256]{1,0:T(8,128)(2,1)S(1)}, u32[]{:S(2)}, u32[]{:S(2)}) %collective-permute-start.6) | collective-permute-done | bytes 262176 | tf_op jit(solution)/shard_map/ppermute | solution.py:411
  33.4 2.1 %collective-permute-start.7 = (bf16[512,128]{1,0:T(8,128)(2,1)S(1)}, bf16[512,128]{1,0:T(8,128)(2,1)S(1)}, u32[]{:S(2)}, u32[]{:S(2)}) collective-permute-start(bf16[512,128]{1,0:T(8,128)(2,1)S(1)} %get-tuple-element.119), channel_id=1, source_target_pairs={{0,12},{1,13},{2,14},{3,15},{4,8},{5,9},{6,10},{7,11},{8,4},{9,5},... | collective-permute-start | bytes 393224 | tf_op jit(solution)/shard_map/ppermute | solution.py:411
  36.5 7.9 %collective-permute-done.10.excess_ref = bf16[2048,128]{1,0:T(8,128)(2,1)S(1)} collective-permute-done((bf16[2048,128]{1,0:T(8,128)(2,1)S(1)}, bf16[2048,128]{1,0:T(8,128)(2,1)S(1)}, u32[]{:S(2)}, u32[]{:S(2)}) %collective-permute-start.10) | collective-permute-done | bytes 524320 | tf_op jit(solution)/shard_map/ppermute | solution.py:417
  45.1 2.2 %collective-permute-done.7 = bf16[512,128]{1,0:T(8,128)(2,1)S(1)} collective-permute-done((bf16[512,128]{1,0:T(8,128)(2,1)S(1)}, bf16[512,128]{1,0:T(8,128)(2,1)S(1)}, u32[]{:S(2)}, u32[]{:S(2)}) %collective-permute-start.7) | collective-permute-done | bytes 131104 | tf_op jit(solution)/shard_map/ppermute | solution.py:411
  49.1 2.2 %collective-permute-start.16 = (bf16[2048,128]{1,0:T(8,128)(2,1)S(1)}, bf16[2048,128]{1,0:T(8,128)(2,1)S(1)}, u32[]{:S(2)}, u32[]{:S(2)}) collective-permute-start(bf16[2048,128]{1,0:T(8,128)(2,1)S(1)} %pad_maximum_fusion.4), channel_id=1, source_target_pairs={{0,16},{16,0},{1,17},{17,1},{2,18},{18,2},{3,19},{19,3},{4,20},{20... | collective-permute-start | bytes 1572872 | tf_op jit(solution)/shard_map/ppermute | solution.py:417
  51.3 3.9 %collective-permute-start.12 = (bf16[512,128]{1,0:T(8,128)(2,1)S(1)}, bf16[512,128]{1,0:T(8,128)(2,1)S(1)}, u32[]{:S(2)}, u32[]{:S(2)}) collective-permute-start(bf16[512,128]{1,0:T(8,128)(2,1)S(1)} %get-tuple-element.132), channel_id=1, source_target_pairs={{0,12},{1,13},{2,14},{3,15},{4,8},{5,9},{6,10},{7,11},{8,4},{9,5},... | collective-permute-start | bytes 393224 | tf_op jit(solution)/shard_map/ppermute | solution.py:411
  59.1 5.5 %collective-permute-done.13 = bf16[512,128]{1,0:T(8,128)(2,1)S(1)} collective-permute-done((bf16[512,128]{1,0:T(8,128)(2,1)S(1)}, bf16[512,128]{1,0:T(8,128)(2,1)S(1)}, u32[]{:S(2)}, u32[]{:S(2)}) %collective-permute-start.13) | collective-permute-done | bytes 131104 | tf_op jit(solution)/shard_map/ppermute | solution.py:411
  67.1 2.8 %collective-permute-start.19 = (bf16[512,128]{1,0:T(8,128)(2,1)S(1)}, bf16[512,128]{1,0:T(8,128)(2,1)S(1)}, u32[]{:S(2)}, u32[]{:S(2)}) collective-permute-start(bf16[512,128]{1,0:T(8,128)(2,1)S(1)} %get-tuple-element.149), channel_id=1, source_target_pairs={{0,4},{1,5},{2,6},{3,7},{4,0},{5,1},{6,2},{7,3},{8,12},{9,13},{10,... | collective-permute-start | bytes 393224 | tf_op jit(solution)/shard_map/ppermute | solution.py:411
  69.9 1.8 %shard_map.78 = (bf16[512,128]{1,0:T(8,128)(2,1)S(1)}, bf16[512,128]{1,0:T(8,128)(2,1)S(1)}, bf16[512,128]{1,0:T(8,128)(2,1)S(1)}, bf16[512,128]{1,0:T(8,128)(2,1)S(1)}) custom-call(s32[3]{0:T(128)S(1)} %pad_add_fusion.place_ref, bf16[4,512,128]{2,1,0:T(8,128)(2,1)S(1)} %get-tuple-element.202.own, bf16[4,512,128]{2,1,0:T(8,128)(2,1)S(1)} %collective-permute-done.15.over_x, ...), custom_call_target="tpu_custom_call" | custom-call | flops 1000 | bytes 1000 | tf_op jit(solution)/shard_map/pallas_call | solution.py:467
  71.8 2.0 %collective-permute-done.17 = bf16[512,128]{1,0:T(8,128)(2,1)S(1)} collective-permute-done((bf16[512,128]{1,0:T(8,128)(2,1)S(1)}, bf16[512,128]{1,0:T(8,128)(2,1)S(1)}, u32[]{:S(2)}, u32[]{:S(2)}) %collective-permute-start.17) | collective-permute-done | bytes 131104 | tf_op jit(solution)/shard_map/ppermute | solution.py:411
  73.8 4.8 %collective-permute-done.18 = bf16[512,128]{1,0:T(8,128)(2,1)S(1)} collective-permute-done((bf16[512,128]{1,0:T(8,128)(2,1)S(1)}, bf16[512,128]{1,0:T(8,128)(2,1)S(1)}, u32[]{:S(2)}, u32[]{:S(2)}) %collective-permute-start.18) | collective-permute-done | bytes 131104 | tf_op jit(solution)/shard_map/ppermute | solution.py:411
  82.1 2.8 %collective-permute-start.24 = (bf16[512,128]{1,0:T(8,128)(2,1)S(1)}, bf16[512,128]{1,0:T(8,128)(2,1)S(1)}, u32[]{:S(2)}, u32[]{:S(2)}) collective-permute-start(bf16[512,128]{1,0:T(8,128)(2,1)S(1)} %get-tuple-element.164), channel_id=1, source_target_pairs={{0,4},{1,5},{2,6},{3,7},{4,0},{5,1},{6,2},{7,3},{8,12},{9,13},{10,... | collective-permute-start | bytes 393224 | tf_op jit(solution)/shard_map/ppermute | solution.py:411
  84.9 1.9 %shard_map.79 = (bf16[512,128]{1,0:T(8,128)(2,1)S(1)}, bf16[512,128]{1,0:T(8,128)(2,1)S(1)}, bf16[512,128]{1,0:T(8,128)(2,1)S(1)}, bf16[512,128]{1,0:T(8,128)(2,1)S(1)}) custom-call(s32[3]{0:T(128)S(1)} %pad_add_fusion.place_ref, bf16[4,512,128]{2,1,0:T(8,128)(2,1)S(1)} %get-tuple-element.200.own, bf16[4,512,128]{2,1,0:T(8,128)(2,1)S(1)} %collective-permute-done.21.over_x, ...), custom_call_target="tpu_custom_call" | custom-call | flops 1000 | bytes 1000 | tf_op jit(solution)/shard_map/pallas_call | solution.py:467
  86.7 2.0 %collective-permute-done.22.refs_1_ = bf16[512,128]{1,0:T(8,128)(2,1)S(1)} collective-permute-done((bf16[512,128]{1,0:T(8,128)(2,1)S(1)}, bf16[512,128]{1,0:T(8,128)(2,1)S(1)}, u32[]{:S(2)}, u32[]{:S(2)}) %collective-permute-start.22) | collective-permute-done | bytes 131104 | tf_op jit(solution)/shard_map/ppermute | solution.py:411
  88.7 5.0 %collective-permute-done.23.refs_2_ = bf16[512,128]{1,0:T(8,128)(2,1)S(1)} collective-permute-done((bf16[512,128]{1,0:T(8,128)(2,1)S(1)}, bf16[512,128]{1,0:T(8,128)(2,1)S(1)}, u32[]{:S(2)}, u32[]{:S(2)}) %collective-permute-start.23) | collective-permute-done | bytes 131104 | tf_op jit(solution)/shard_map/ppermute | solution.py:411
  94.2 2.1 %collective-permute-start.27 = (bf16[512,128]{1,0:T(8,128)(2,1)S(1)}, bf16[512,128]{1,0:T(8,128)(2,1)S(1)}, u32[]{:S(2)}, u32[]{:S(2)}) collective-permute-start(bf16[512,128]{1,0:T(8,128)(2,1)S(1)} %get-tuple-element.179), channel_id=1, source_target_pairs={{0,12},{1,13},{2,14},{3,15},{4,8},{5,9},{6,10},{7,11},{8,4},{9,5},... | collective-permute-start | bytes 393224 | tf_op jit(solution)/shard_map/ppermute | solution.py:411
  96.3 2.4 %collective-permute-start.29 = (bf16[512,128]{1,0:T(8,128)(2,1)S(1)}, bf16[512,128]{1,0:T(8,128)(2,1)S(1)}, u32[]{:S(2)}, u32[]{:S(2)}) collective-permute-start(bf16[512,128]{1,0:T(8,128)(2,1)S(1)} %get-tuple-element.181), channel_id=1, source_target_pairs={{0,4},{1,5},{2,6},{3,7},{4,0},{5,1},{6,2},{7,3},{8,12},{9,13},{10,... | collective-permute-start | bytes 393224 | tf_op jit(solution)/shard_map/ppermute | solution.py:411
  98.6 1.8 %shard_map.80 = (bf16[512,128]{1,0:T(8,128)(2,1)S(1)}, bf16[512,128]{1,0:T(8,128)(2,1)S(1)}, bf16[512,128]{1,0:T(8,128)(2,1)S(1)}, bf16[512,128]{1,0:T(8,128)(2,1)S(1)}) custom-call(s32[3]{0:T(128)S(1)} %pad_add_fusion.place_ref, bf16[4,512,128]{2,1,0:T(8,128)(2,1)S(1)} %get-tuple-element.198.own, bf16[4,512,128]{2,1,0:T(8,128)(2,1)S(1)} %collective-permute-done.26.over_x, ...), custom_call_target="tpu_custom_call" | custom-call | flops 1000 | bytes 1000 | tf_op jit(solution)/shard_map/pallas_call | solution.py:467
  100.5 2.0 %collective-permute-done.27.refs_5_ = bf16[512,128]{1,0:T(8,128)(2,1)S(1)} collective-permute-done((bf16[512,128]{1,0:T(8,128)(2,1)S(1)}, bf16[512,128]{1,0:T(8,128)(2,1)S(1)}, u32[]{:S(2)}, u32[]{:S(2)}) %collective-permute-start.27) | collective-permute-done | bytes 131104 | tf_op jit(solution)/shard_map/ppermute | solution.py:411
  102.5 5.1 %collective-permute-done.28.refs_6_ = bf16[512,128]{1,0:T(8,128)(2,1)S(1)} collective-permute-done((bf16[512,128]{1,0:T(8,128)(2,1)S(1)}, bf16[512,128]{1,0:T(8,128)(2,1)S(1)}, u32[]{:S(2)}, u32[]{:S(2)}) %collective-permute-start.28) | collective-permute-done | bytes 131104 | tf_op jit(solution)/shard_map/ppermute | solution.py:411
  108.9 2.0 %collective-permute-start.32 = (bf16[512,128]{1,0:T(8,128)(2,1)S(1)}, bf16[512,128]{1,0:T(8,128)(2,1)S(1)}, u32[]{:S(2)}, u32[]{:S(2)}) collective-permute-start(bf16[512,128]{1,0:T(8,128)(2,1)S(1)} %get-tuple-element.194), channel_id=1, source_target_pairs={{0,12},{1,13},{2,14},{3,15},{4,8},{5,9},{6,10},{7,11},{8,4},{9,5},... | collective-permute-start | bytes 393224 | tf_op jit(solution)/shard_map/ppermute | solution.py:411
  110.9 2.4 %collective-permute-start.34 = (bf16[512,128]{1,0:T(8,128)(2,1)S(1)}, bf16[512,128]{1,0:T(8,128)(2,1)S(1)}, u32[]{:S(2)}, u32[]{:S(2)}) collective-permute-start(bf16[512,128]{1,0:T(8,128)(2,1)S(1)} %get-tuple-element.196), channel_id=1, source_target_pairs={{0,4},{1,5},{2,6},{3,7},{4,0},{5,1},{6,2},{7,3},{8,12},{9,13},{10,... | collective-permute-start | bytes 393224 | tf_op jit(solution)/shard_map/ppermute | solution.py:411
  113.3 2.9 %shard_map.81 = (bf16[128,8192]{1,0:T(8,128)(2,1)}, f32[2,128,128]{2,1,0:T(8,128)S(1)}) custom-call(s32[3]{0:T(128)S(1)} %pad_add_fusion.place_ref, s32[64]{0:T(128)S(1)} %copy-done.3, bf16[512,128]{1,0:T(8,128)(2,1)S(1)} %get-tuple-element.174.refs_0_, bf16[512,128]{1,0:T(8,128)(2,1)S(1)} %collective-permute-done.22.refs_1_, ...), custom_call_target="tpu_custom_call" | custom-call | flops 1000 | bytes 1000 | tf_op jit(solution)/shard_map/pallas_call | solution.py:530
  117.2 4.1 %collective-permute-done.33.refs_2_ = bf16[512,128]{1,0:T(8,128)(2,1)S(1)} collective-permute-done((bf16[512,128]{1,0:T(8,128)(2,1)S(1)}, bf16[512,128]{1,0:T(8,128)(2,1)S(1)}, u32[]{:S(2)}, u32[]{:S(2)}) %collective-permute-start.33) | collective-permute-done | bytes 131104 | tf_op jit(solution)/shard_map/ppermute | solution.py:411
  121.5 2.6 %shard_map.82 = bf16[128,8192]{1,0:T(8,128)(2,1)} custom-call(s32[3]{0:T(128)S(1)} %pad_add_fusion.place_ref, s32[64]{0:T(128)S(1)} %copy-done.3, bf16[128,8192]{1,0:T(8,128)(2,1)} %get-tuple-element.191.done_hbm, f32[2,128,128]{2,1,0:T(8,128)S(1)} %get-tuple-element.192.seam_ref, ...), custom_call_target="tpu_custom_call", output_to_operand_aliasing={{}: (2, {})} | custom-call | flops 1000 | bytes 1000 | tf_op jit(solution)/shard_map/pallas_call | solution.py:542
  (80 shorter events, 27.3 us)
Async XLA Ops:
  4.5 7.5 %collective-permute-start.2 = (bf16[128,512]{1,0:T(8,128)(2,1)S(1)}, bf16[128,512]{1,0:T(8,128)(2,1)S(1)}, u32[]{:S(2)}, u32[]{:S(2)}) collective-permute-start(bf16[128,512]{1,0:T(8,128)(2,1)S(1)} %get-tuple-element.111), channel_id=1, source_target_pairs={{0,1},{1,0},{2,3},{3,2},{4,5},{5,4},{6,7},{7,6},{8,9},{9,8},{10,11... | collective-permute-start | bytes 393224 | tf_op jit(solution)/shard_map/ppermute | solution.py:411
  5.0 7.0 %collective-permute-start.3 = (bf16[128,512]{1,0:T(8,128)(2,1)S(1)}, bf16[128,512]{1,0:T(8,128)(2,1)S(1)}, u32[]{:S(2)}, u32[]{:S(2)}) collective-permute-start(bf16[128,512]{1,0:T(8,128)(2,1)S(1)} %get-tuple-element.112), channel_id=1, source_target_pairs={{0,2},{1,3},{2,0},{3,1},{4,6},{5,7},{6,4},{7,5},{8,10},{9,11},{10,... | collective-permute-start | bytes 393224 | tf_op jit(solution)/shard_map/ppermute | solution.py:411
  7.5 6.6 %collective-permute-start.4 = (bf16[128,512]{1,0:T(8,128)(2,1)S(1)}, bf16[128,512]{1,0:T(8,128)(2,1)S(1)}, u32[]{:S(2)}, u32[]{:S(2)}) collective-permute-start(bf16[128,512]{1,0:T(8,128)(2,1)S(1)} %get-tuple-element.113), channel_id=1, source_target_pairs={{0,3},{1,2},{2,1},{3,0},{4,7},{5,6},{6,5},{7,4},{8,11},{9,10},{10,... | collective-permute-start | bytes 393224 | tf_op jit(solution)/shard_map/ppermute | solution.py:411
  14.3 14.0 %collective-permute-start.5 = (bf16[512,256]{1,0:T(8,128)(2,1)S(1)}, bf16[512,256]{1,0:T(8,128)(2,1)S(1)}, u32[]{:S(2)}, u32[]{:S(2)}) collective-permute-start(bf16[512,256]{1,0:T(8,128)(2,1)S(1)} %slice.21), channel_id=1, source_target_pairs={{0,4},{1,5},{2,6},{3,7},{4,0},{5,1},{6,2},{7,3},{8,12},{9,13},{10,... | collective-permute-start | bytes 786440 | tf_op jit(solution)/shard_map/ppermute | solution.py:411
  16.0 14.8 %collective-permute-start.6 = (bf16[512,256]{1,0:T(8,128)(2,1)S(1)}, bf16[512,256]{1,0:T(8,128)(2,1)S(1)}, u32[]{:S(2)}, u32[]{:S(2)}) collective-permute-start(bf16[512,256]{1,0:T(8,128)(2,1)S(1)} %slice.21), channel_id=1, source_target_pairs={{0,8},{1,9},{2,10},{3,11},{4,12},{5,13},{6,14},{7,15},{8,0},{9,1},... | collective-permute-start | bytes 786440 | tf_op jit(solution)/shard_map/ppermute | solution.py:411
  22.6 5.5 %collective-permute-start.1 = (bf16[2,128,128]{2,1,0:T(8,128)(2,1)S(1)}, bf16[2,128,128]{2,1,0:T(8,128)(2,1)S(1)}, u32[]{:S(2)}, u32[]{:S(2)}) collective-permute-start(bf16[2,128,128]{2,1,0:T(8,128)(2,1)S(1)} %get-tuple-element.105), channel_id=1, source_target_pairs={{0,16},{16,0},{1,17},{17,1},{2,18},{18,2},{3,19},{19,3},{4,20},{20... | collective-permute-start | bytes 196616 | tf_op jit(solution)/shard_map/ppermute | solution.py:417
  30.8 13.6 %collective-permute-start.10 = (bf16[2048,128]{1,0:T(8,128)(2,1)S(1)}, bf16[2048,128]{1,0:T(8,128)(2,1)S(1)}, u32[]{:S(2)}, u32[]{:S(2)}) collective-permute-start(bf16[2048,128]{1,0:T(8,128)(2,1)S(1)} %get-tuple-element.124), channel_id=1, source_target_pairs={{0,16},{16,0},{1,17},{17,1},{2,18},{18,2},{3,19},{19,3},{4,20},{20... | collective-permute-start | bytes 1572872 | tf_op jit(solution)/shard_map/ppermute | solution.py:417
  32.4 14.9 %collective-permute-start.9 = (bf16[1536,128]{1,0:T(8,128)(2,1)S(1)}, bf16[1536,128]{1,0:T(8,128)(2,1)S(1)}, u32[]{:S(2)}, u32[]{:S(2)}) collective-permute-start(bf16[1536,128]{1,0:T(8,128)(2,1)S(1)} %pad_maximum_fusion.8), channel_id=1, source_target_pairs={{0,4},{1,5},{2,6},{3,7},{4,0},{5,1},{6,2},{7,3},{8,12},{9,13},{10,... | collective-permute-start | bytes 1179656 | tf_op jit(solution)/shard_map/ppermute | solution.py:411
  32.9 14.4 %collective-permute-start.11 = (bf16[512,256]{1,0:T(8,128)(2,1)S(1)}, bf16[512,256]{1,0:T(8,128)(2,1)S(1)}, u32[]{:S(2)}, u32[]{:S(2)}) collective-permute-start(bf16[512,256]{1,0:T(8,128)(2,1)S(1)} %collective-permute-done.5.near), channel_id=1, source_target_pairs={{0,16},{16,0},{1,17},{17,1},{2,18},{18,2},{3,19},{19,3},{4,20},{20... | collective-permute-start | bytes 786440 | tf_op jit(solution)/shard_map/ppermute | solution.py:417
  33.4 13.9 %collective-permute-start.7 = (bf16[512,128]{1,0:T(8,128)(2,1)S(1)}, bf16[512,128]{1,0:T(8,128)(2,1)S(1)}, u32[]{:S(2)}, u32[]{:S(2)}) collective-permute-start(bf16[512,128]{1,0:T(8,128)(2,1)S(1)} %get-tuple-element.119), channel_id=1, source_target_pairs={{0,12},{1,13},{2,14},{3,15},{4,8},{5,9},{6,10},{7,11},{8,4},{9,5},... | collective-permute-start | bytes 393224 | tf_op jit(solution)/shard_map/ppermute | solution.py:411
  35.5 11.8 %collective-permute-start.8 = (bf16[512,128]{1,0:T(8,128)(2,1)S(1)}, bf16[512,128]{1,0:T(8,128)(2,1)S(1)}, u32[]{:S(2)}, u32[]{:S(2)}) collective-permute-start(bf16[512,128]{1,0:T(8,128)(2,1)S(1)} %get-tuple-element.120), channel_id=1, source_target_pairs={{0,8},{1,9},{2,10},{3,11},{4,12},{5,13},{6,14},{7,15},{8,0},{9,1},... | collective-permute-start | bytes 393224 | tf_op jit(solution)/shard_map/ppermute | solution.py:411
  47.5 17.2 %collective-permute-start.15 = (bf16[4,512,128]{2,1,0:T(8,128)(2,1)S(1)}, bf16[4,512,128]{2,1,0:T(8,128)(2,1)S(1)}, u32[]{:S(2)}, u32[]{:S(2)}) collective-permute-start(bf16[4,512,128]{2,1,0:T(8,128)(2,1)S(1)} %get-tuple-element.202.own), channel_id=1, source_target_pairs={{0,2},{1,3},{2,0},{3,1},{4,6},{5,7},{6,4},{7,5},{8,10},{9,11},{10,... | collective-permute-start | bytes 1572872 | tf_op jit(solution)/shard_map/ppermute | solution.py:411
  49.1 15.5 %collective-permute-start.16 = (bf16[2048,128]{1,0:T(8,128)(2,1)S(1)}, bf16[2048,128]{1,0:T(8,128)(2,1)S(1)}, u32[]{:S(2)}, u32[]{:S(2)}) collective-permute-start(bf16[2048,128]{1,0:T(8,128)(2,1)S(1)} %pad_maximum_fusion.4), channel_id=1, source_target_pairs={{0,16},{16,0},{1,17},{17,1},{2,18},{18,2},{3,19},{19,3},{4,20},{20... | collective-permute-start | bytes 1572872 | tf_op jit(solution)/shard_map/ppermute | solution.py:417
  51.3 7.8 %collective-permute-start.12 = (bf16[512,128]{1,0:T(8,128)(2,1)S(1)}, bf16[512,128]{1,0:T(8,128)(2,1)S(1)}, u32[]{:S(2)}, u32[]{:S(2)}) collective-permute-start(bf16[512,128]{1,0:T(8,128)(2,1)S(1)} %get-tuple-element.132), channel_id=1, source_target_pairs={{0,12},{1,13},{2,14},{3,15},{4,8},{5,9},{6,10},{7,11},{8,4},{9,5},... | collective-permute-start | bytes 393224 | tf_op jit(solution)/shard_map/ppermute | solution.py:411
  55.2 9.4 %collective-permute-start.13 = (bf16[512,128]{1,0:T(8,128)(2,1)S(1)}, bf16[512,128]{1,0:T(8,128)(2,1)S(1)}, u32[]{:S(2)}, u32[]{:S(2)}) collective-permute-start(bf16[512,128]{1,0:T(8,128)(2,1)S(1)} %get-tuple-element.133), channel_id=1, source_target_pairs={{0,8},{1,9},{2,10},{3,11},{4,12},{5,13},{6,14},{7,15},{8,0},{9,1},... | collective-permute-start | bytes 393224 | tf_op jit(solution)/shard_map/ppermute | solution.py:411
  55.2 9.4 %collective-permute-start.14 = (bf16[512,128]{1,0:T(8,128)(2,1)S(1)}, bf16[512,128]{1,0:T(8,128)(2,1)S(1)}, u32[]{:S(2)}, u32[]{:S(2)}) collective-permute-start(bf16[512,128]{1,0:T(8,128)(2,1)S(1)} %get-tuple-element.134), channel_id=1, source_target_pairs={{0,4},{1,5},{2,6},{3,7},{4,0},{5,1},{6,2},{7,3},{8,12},{9,13},{10,... | collective-permute-start | bytes 393224 | tf_op jit(solution)/shard_map/ppermute | solution.py:411
  65.0 14.4 %collective-permute-start.21 = (bf16[4,512,128]{2,1,0:T(8,128)(2,1)S(1)}, bf16[4,512,128]{2,1,0:T(8,128)(2,1)S(1)}, u32[]{:S(2)}, u32[]{:S(2)}) collective-permute-start(bf16[4,512,128]{2,1,0:T(8,128)(2,1)S(1)} %get-tuple-element.200.own), channel_id=1, source_target_pairs={{0,2},{1,3},{2,0},{3,1},{4,6},{5,7},{6,4},{7,5},{8,10},{9,11},{10,... | collective-permute-start | bytes 1572872 | tf_op jit(solution)/shard_map/ppermute | solution.py:411
  65.6 8.3 %collective-permute-start.17 = (bf16[512,128]{1,0:T(8,128)(2,1)S(1)}, bf16[512,128]{1,0:T(8,128)(2,1)S(1)}, u32[]{:S(2)}, u32[]{:S(2)}) collective-permute-start(bf16[512,128]{1,0:T(8,128)(2,1)S(1)} %get-tuple-element.147), channel_id=1, source_target_pairs={{0,12},{1,13},{2,14},{3,15},{4,8},{5,9},{6,10},{7,11},{8,4},{9,5},... | collective-permute-start | bytes 393224 | tf_op jit(solution)/shard_map/ppermute | solution.py:411
  67.1 11.5 %collective-permute-start.18 = (bf16[512,128]{1,0:T(8,128)(2,1)S(1)}, bf16[512,128]{1,0:T(8,128)(2,1)S(1)}, u32[]{:S(2)}, u32[]{:S(2)}) collective-permute-start(bf16[512,128]{1,0:T(8,128)(2,1)S(1)} %get-tuple-element.148), channel_id=1, source_target_pairs={{0,8},{1,9},{2,10},{3,11},{4,12},{5,13},{6,14},{7,15},{8,0},{9,1},... | collective-permute-start | bytes 393224 | tf_op jit(solution)/shard_map/ppermute | solution.py:411
  67.1 11.5 %collective-permute-start.19 = (bf16[512,128]{1,0:T(8,128)(2,1)S(1)}, bf16[512,128]{1,0:T(8,128)(2,1)S(1)}, u32[]{:S(2)}, u32[]{:S(2)}) collective-permute-start(bf16[512,128]{1,0:T(8,128)(2,1)S(1)} %get-tuple-element.149), channel_id=1, source_target_pairs={{0,4},{1,5},{2,6},{3,7},{4,0},{5,1},{6,2},{7,3},{8,12},{9,13},{10,... | collective-permute-start | bytes 393224 | tf_op jit(solution)/shard_map/ppermute | solution.py:411
  79.4 5.4 %collective-permute-start.25 = (bf16[2,4,512,128]{3,2,1,0:T(8,128)(2,1)S(1)}, bf16[2,4,512,128]{3,2,1,0:T(8,128)(2,1)S(1)}, u32[]{:S(2)}, u32[]{:S(2)}) collective-permute-start(bf16[2,4,512,128]{3,2,1,0:T(8,128)(2,1)S(1)} %pad_maximum_fusion.1), channel_id=1, source_target_pairs={{0,1},{1,0},{2,3},{3,2},{4,5},{5,4},{6,7},{7,6},{8,9},{9,8},{10,11... | collective-permute-start | bytes 3145736 | tf_op jit(solution)/shard_map/ppermute | solution.py:411
  79.6 14.4 %collective-permute-start.26 = (bf16[4,512,128]{2,1,0:T(8,128)(2,1)S(1)}, bf16[4,512,128]{2,1,0:T(8,128)(2,1)S(1)}, u32[]{:S(2)}, u32[]{:S(2)}) collective-permute-start(bf16[4,512,128]{2,1,0:T(8,128)(2,1)S(1)} %get-tuple-element.198.own), channel_id=1, source_target_pairs={{0,2},{1,3},{2,0},{3,1},{4,6},{5,7},{6,4},{7,5},{8,10},{9,11},{10,... | collective-permute-start | bytes 1572872 | tf_op jit(solution)/shard_map/ppermute | solution.py:411
  80.5 8.3 %collective-permute-start.22 = (bf16[512,128]{1,0:T(8,128)(2,1)S(1)}, bf16[512,128]{1,0:T(8,128)(2,1)S(1)}, u32[]{:S(2)}, u32[]{:S(2)}) collective-permute-start(bf16[512,128]{1,0:T(8,128)(2,1)S(1)} %get-tuple-element.162), channel_id=1, source_target_pairs={{0,12},{1,13},{2,14},{3,15},{4,8},{5,9},{6,10},{7,11},{8,4},{9,5},... | collective-permute-start | bytes 393224 | tf_op jit(solution)/shard_map/ppermute | solution.py:411
  82.1 11.7 %collective-permute-start.23 = (bf16[512,128]{1,0:T(8,128)(2,1)S(1)}, bf16[512,128]{1,0:T(8,128)(2,1)S(1)}, u32[]{:S(2)}, u32[]{:S(2)}) collective-permute-start(bf16[512,128]{1,0:T(8,128)(2,1)S(1)} %get-tuple-element.163), channel_id=1, source_target_pairs={{0,8},{1,9},{2,10},{3,11},{4,12},{5,13},{6,14},{7,15},{8,0},{9,1},... | collective-permute-start | bytes 393224 | tf_op jit(solution)/shard_map/ppermute | solution.py:411
  82.1 11.7 %collective-permute-start.24 = (bf16[512,128]{1,0:T(8,128)(2,1)S(1)}, bf16[512,128]{1,0:T(8,128)(2,1)S(1)}, u32[]{:S(2)}, u32[]{:S(2)}) collective-permute-start(bf16[512,128]{1,0:T(8,128)(2,1)S(1)} %get-tuple-element.164), channel_id=1, source_target_pairs={{0,4},{1,5},{2,6},{3,7},{4,0},{5,1},{6,2},{7,3},{8,12},{9,13},{10,... | collective-permute-start | bytes 393224 | tf_op jit(solution)/shard_map/ppermute | solution.py:411
  94.2 8.3 %collective-permute-start.27 = (bf16[512,128]{1,0:T(8,128)(2,1)S(1)}, bf16[512,128]{1,0:T(8,128)(2,1)S(1)}, u32[]{:S(2)}, u32[]{:S(2)}) collective-permute-start(bf16[512,128]{1,0:T(8,128)(2,1)S(1)} %get-tuple-element.179), channel_id=1, source_target_pairs={{0,12},{1,13},{2,14},{3,15},{4,8},{5,9},{6,10},{7,11},{8,4},{9,5},... | collective-permute-start | bytes 393224 | tf_op jit(solution)/shard_map/ppermute | solution.py:411
  96.3 11.3 %collective-permute-start.28 = (bf16[512,128]{1,0:T(8,128)(2,1)S(1)}, bf16[512,128]{1,0:T(8,128)(2,1)S(1)}, u32[]{:S(2)}, u32[]{:S(2)}) collective-permute-start(bf16[512,128]{1,0:T(8,128)(2,1)S(1)} %get-tuple-element.180), channel_id=1, source_target_pairs={{0,8},{1,9},{2,10},{3,11},{4,12},{5,13},{6,14},{7,15},{8,0},{9,1},... | collective-permute-start | bytes 393224 | tf_op jit(solution)/shard_map/ppermute | solution.py:411
  96.3 11.3 %collective-permute-start.29 = (bf16[512,128]{1,0:T(8,128)(2,1)S(1)}, bf16[512,128]{1,0:T(8,128)(2,1)S(1)}, u32[]{:S(2)}, u32[]{:S(2)}) collective-permute-start(bf16[512,128]{1,0:T(8,128)(2,1)S(1)} %get-tuple-element.181), channel_id=1, source_target_pairs={{0,4},{1,5},{2,6},{3,7},{4,0},{5,1},{6,2},{7,3},{8,12},{9,13},{10,... | collective-permute-start | bytes 393224 | tf_op jit(solution)/shard_map/ppermute | solution.py:411
  107.6 13.9 %collective-permute-start.31 = (bf16[2048,128]{1,0:T(8,128)(2,1)S(1)}, bf16[2048,128]{1,0:T(8,128)(2,1)S(1)}, u32[]{:S(2)}, u32[]{:S(2)}) collective-permute-start(bf16[2048,128]{1,0:T(8,128)(2,1)S(1)} %pad_maximum_fusion.7), channel_id=1, source_target_pairs={{0,16},{16,0},{1,17},{17,1},{2,18},{18,2},{3,19},{19,3},{4,20},{20... | collective-permute-start | bytes 1572872 | tf_op jit(solution)/shard_map/ppermute | solution.py:417
  108.9 8.3 %collective-permute-start.32 = (bf16[512,128]{1,0:T(8,128)(2,1)S(1)}, bf16[512,128]{1,0:T(8,128)(2,1)S(1)}, u32[]{:S(2)}, u32[]{:S(2)}) collective-permute-start(bf16[512,128]{1,0:T(8,128)(2,1)S(1)} %get-tuple-element.194), channel_id=1, source_target_pairs={{0,12},{1,13},{2,14},{3,15},{4,8},{5,9},{6,10},{7,11},{8,4},{9,5},... | collective-permute-start | bytes 393224 | tf_op jit(solution)/shard_map/ppermute | solution.py:411
  110.9 10.4 %collective-permute-start.33 = (bf16[512,128]{1,0:T(8,128)(2,1)S(1)}, bf16[512,128]{1,0:T(8,128)(2,1)S(1)}, u32[]{:S(2)}, u32[]{:S(2)}) collective-permute-start(bf16[512,128]{1,0:T(8,128)(2,1)S(1)} %get-tuple-element.195), channel_id=1, source_target_pairs={{0,8},{1,9},{2,10},{3,11},{4,12},{5,13},{6,14},{7,15},{8,0},{9,1},... | collective-permute-start | bytes 393224 | tf_op jit(solution)/shard_map/ppermute | solution.py:411
  110.9 10.4 %collective-permute-start.34 = (bf16[512,128]{1,0:T(8,128)(2,1)S(1)}, bf16[512,128]{1,0:T(8,128)(2,1)S(1)}, u32[]{:S(2)}, u32[]{:S(2)}) collective-permute-start(bf16[512,128]{1,0:T(8,128)(2,1)S(1)} %get-tuple-element.196), channel_id=1, source_target_pairs={{0,4},{1,5},{2,6},{3,7},{4,0},{5,1},{6,2},{7,3},{8,12},{9,13},{10,... | collective-permute-start | bytes 393224 | tf_op jit(solution)/shard_map/ppermute | solution.py:411
  (10 other events, 96.0 us)

commit v5 on v4

--- a/solution.py
+++ b/solution.py
@@ -9,7 +9,7 @@
 
 HB = 2
 EDGE = 2 * HB
-GROUP = 8
+GROUP = 4
 PLANE = 4
 ORDER = (0, 3, 2, 1)
 VMEM = pl.BlockSpec(memory_space=pltpu.VMEM)

time: 124 us -> 124 us (level)
  transfers between devices with their start and end apart: 35 -> 35, of which waited for: 18 -> 19; matrix products, arithmetic and copies ran while one was open for 0% -> 0% of each run, Pallas kernels for 15% -> 15%
where the time goes in v5:
time: 124 us
  waiting for transfers between devices  51.9 us (42%)
  starting transfers between devices  45.3 us (37%)
  Pallas kernels  23 us (19%)
  local copies, waits for them, and re-layouts  2.76 us (2%)
    ppermute x29, waiting for transfers between devices, swap(): return lax.ppermute(value, 'orb', [(i, i ^ bits) for i in range(orbs)])  41.1 us
    ppermute x29, starting transfers between devices, swap(): return lax.ppermute(value, 'orb', [(i, i ^ bits) for i in range(orbs)])  36.4 us
    ppermute x6, waiting for transfers between devices, other_slab(): return lax.ppermute(value, 'slab', [(0, 1), (1, 0)])  10.8 us
    ppermute x6, starting transfers between devices, other_slab(): return lax.ppermute(value, 'slab', [(0, 1), (1, 0)])  8.9 us
    pallas_call x3, Pallas kernels, rotate(): call(functools.partial(rotate_kernel, groups), 12, part_outs, [SMEM] + [V...  5.53 us
    pallas_call x1, Pallas kernels, paired(): call(functools.partial(second_kernel, blocks, groups), 18, part_outs + [s...  3.97 us
    pallas_call x1, Pallas kernels, paired(): call(functools.partial(first_kernel, blocks), 16, [shaped(block_shape), s...  3.95 us
    pallas_call x1, Pallas kernels, paired(): call(functools.partial(spread_kernel, blocks, groups), 12, [out, shaped((...  3.18 us
  transfers between devices with their start and end apart: 35, of which 19 were waited for; matrix products, arithmetic and copies ran while one was open for 0% of the time, Pallas kernels for 15%

profile of v5, /device:TPU:0, one launch (start us, length us, event | category | flops | bytes accessed | tf_op | source)
XLA Modules:
  0.0 124.0 jit_solution(6632326745948469829)
XLA Ops:
  5.0 2.6 %collective-permute-start.3 = (bf16[128,512]{1,0:T(8,128)(2,1)S(1)}, bf16[128,512]{1,0:T(8,128)(2,1)S(1)}, u32[]{:S(2)}, u32[]{:S(2)}) collective-permute-start(bf16[128,512]{1,0:T(8,128)(2,1)S(1)} %get-tuple-element.112), channel_id=1, source_target_pairs={{0,2},{1,3},{2,0},{3,1},{4,6},{5,7},{6,4},{7,5},{8,10},{9,11},{10,... | collective-permute-start | bytes 393224 | tf_op jit(solution)/shard_map/ppermute | solution.py:411
  9.4 2.6 %collective-permute-done.halo_ref = bf16[128,256]{1,0:T(8,128)(2,1)S(1)} collective-permute-done((bf16[128,256]{1,0:T(8,128)(2,1)S(1)}, bf16[128,256]{1,0:T(8,128)(2,1)S(1)}, u32[]{:S(2)}, u32[]{:S(2)}) %collective-permute-start) | collective-permute-done | bytes 65568 | tf_op jit(solution)/shard_map/ppermute | solution.py:417
  12.0 2.2 %collective-permute-done.4 = bf16[128,512]{1,0:T(8,128)(2,1)S(1)} collective-permute-done((bf16[128,512]{1,0:T(8,128)(2,1)S(1)}, bf16[128,512]{1,0:T(8,128)(2,1)S(1)}, u32[]{:S(2)}, u32[]{:S(2)}) %collective-permute-start.4) | collective-permute-done | bytes 131104 | tf_op jit(solution)/shard_map/ppermute | solution.py:411
  16.0 2.6 %collective-permute-start.6 = (bf16[512,256]{1,0:T(8,128)(2,1)S(1)}, bf16[512,256]{1,0:T(8,128)(2,1)S(1)}, u32[]{:S(2)}, u32[]{:S(2)}) collective-permute-start(bf16[512,256]{1,0:T(8,128)(2,1)S(1)} %slice.21), channel_id=1, source_target_pairs={{0,8},{1,9},{2,10},{3,11},{4,12},{5,13},{6,14},{7,15},{8,0},{9,1},... | collective-permute-start | bytes 786440 | tf_op jit(solution)/shard_map/ppermute | solution.py:411
  18.6 4.0 %shard_map.74 = (bf16[64,128,128]{2,1,0:T(8,128)(2,1)S(1)}, bf16[2,128,128]{2,1,0:T(8,128)(2,1)S(1)}) custom-call(s32[3]{0:T(128)S(1)} %pad_add_fusion.place_ref, s32[112]{0:T(128)S(1)} %copy-done.4, s32[112]{0:T(128)S(1)} %copy-done.5, s32[64]{0:T(128)S(1)} %copy-done.3, f32[3]{0:T(128)S(1)} %copy-done.6, ...), custom_call_target="tpu_custom_call" | custom-call | flops 1000 | bytes 1000 | tf_op jit(solution)/shard_map/pallas_call | solution.py:434
  24.1 4.0 %shard_map.75 = (bf16[512,128]{1,0:T(8,128)(2,1)S(1)}, bf16[512,128]{1,0:T(8,128)(2,1)S(1)}, bf16[512,128]{1,0:T(8,128)(2,1)S(1)}, bf16[512,128]{1,0:T(8,128)(2,...) custom-call(s32[3]{0:T(128)S(1)} %pad_add_fusion.place_ref, ...), custom_call_target="tpu_custom_call" | custom-call | flops 1000 | bytes 1000 | tf_op jit(solution)/shard_map/pallas_call | solution.py:447
  28.2 2.5 %collective-permute-done.6.far_two = bf16[512,256]{1,0:T(8,128)(2,1)S(1)} collective-permute-done((bf16[512,256]{1,0:T(8,128)(2,1)S(1)}, bf16[512,256]{1,0:T(8,128)(2,1)S(1)}, u32[]{:S(2)}, u32[]{:S(2)}) %collective-permute-start.6) | collective-permute-done | bytes 262176 | tf_op jit(solution)/shard_map/ppermute | solution.py:411
  33.4 2.1 %collective-permute-start.7 = (bf16[512,128]{1,0:T(8,128)(2,1)S(1)}, bf16[512,128]{1,0:T(8,128)(2,1)S(1)}, u32[]{:S(2)}, u32[]{:S(2)}) collective-permute-start(bf16[512,128]{1,0:T(8,128)(2,1)S(1)} %get-tuple-element.119), channel_id=1, source_target_pairs={{0,12},{1,13},{2,14},{3,15},{4,8},{5,9},{6,10},{7,11},{8,4},{9,5},... | collective-permute-start | bytes 393224 | tf_op jit(solution)/shard_map/ppermute | solution.py:411
  36.5 7.9 %collective-permute-done.10.excess_ref = bf16[2048,128]{1,0:T(8,128)(2,1)S(1)} collective-permute-done((bf16[2048,128]{1,0:T(8,128)(2,1)S(1)}, bf16[2048,128]{1,0:T(8,128)(2,1)S(1)}, u32[]{:S(2)}, u32[]{:S(2)}) %collective-permute-start.10) | collective-permute-done | bytes 524320 | tf_op jit(solution)/shard_map/ppermute | solution.py:417
  45.1 2.2 %collective-permute-done.7 = bf16[512,128]{1,0:T(8,128)(2,1)S(1)} collective-permute-done((bf16[512,128]{1,0:T(8,128)(2,1)S(1)}, bf16[512,128]{1,0:T(8,128)(2,1)S(1)}, u32[]{:S(2)}, u32[]{:S(2)}) %collective-permute-start.7) | collective-permute-done | bytes 131104 | tf_op jit(solution)/shard_map/ppermute | solution.py:411
  49.1 2.2 %collective-permute-start.16 = (bf16[2048,128]{1,0:T(8,128)(2,1)S(1)}, bf16[2048,128]{1,0:T(8,128)(2,1)S(1)}, u32[]{:S(2)}, u32[]{:S(2)}) collective-permute-start(bf16[2048,128]{1,0:T(8,128)(2,1)S(1)} %pad_maximum_fusion.4), channel_id=1, source_target_pairs={{0,16},{16,0},{1,17},{17,1},{2,18},{18,2},{3,19},{19,3},{4,20},{20... | collective-permute-start | bytes 1572872 | tf_op jit(solution)/shard_map/ppermute | solution.py:417
  51.3 3.9 %collective-permute-start.12 = (bf16[512,128]{1,0:T(8,128)(2,1)S(1)}, bf16[512,128]{1,0:T(8,128)(2,1)S(1)}, u32[]{:S(2)}, u32[]{:S(2)}) collective-permute-start(bf16[512,128]{1,0:T(8,128)(2,1)S(1)} %get-tuple-element.132), channel_id=1, source_target_pairs={{0,12},{1,13},{2,14},{3,15},{4,8},{5,9},{6,10},{7,11},{8,4},{9,5},... | collective-permute-start | bytes 393224 | tf_op jit(solution)/shard_map/ppermute | solution.py:411
  57.3 1.8 %collective-permute-done.12 = bf16[512,128]{1,0:T(8,128)(2,1)S(1)} collective-permute-done((bf16[512,128]{1,0:T(8,128)(2,1)S(1)}, bf16[512,128]{1,0:T(8,128)(2,1)S(1)}, u32[]{:S(2)}, u32[]{:S(2)}) %collective-permute-start.12) | collective-permute-done | bytes 131104 | tf_op jit(solution)/shard_map/ppermute | solution.py:411
  59.1 5.5 %collective-permute-done.13 = bf16[512,128]{1,0:T(8,128)(2,1)S(1)} collective-permute-done((bf16[512,128]{1,0:T(8,128)(2,1)S(1)}, bf16[512,128]{1,0:T(8,128)(2,1)S(1)}, u32[]{:S(2)}, u32[]{:S(2)}) %collective-permute-start.13) | collective-permute-done | bytes 131104 | tf_op jit(solution)/shard_map/ppermute | solution.py:411
  67.1 2.8 %collective-permute-start.19 = (bf16[512,128]{1,0:T(8,128)(2,1)S(1)}, bf16[512,128]{1,0:T(8,128)(2,1)S(1)}, u32[]{:S(2)}, u32[]{:S(2)}) collective-permute-start(bf16[512,128]{1,0:T(8,128)(2,1)S(1)} %get-tuple-element.149), channel_id=1, source_target_pairs={{0,4},{1,5},{2,6},{3,7},{4,0},{5,1},{6,2},{7,3},{8,12},{9,13},{10,... | collective-permute-start | bytes 393224 | tf_op jit(solution)/shard_map/ppermute | solution.py:411
  69.9 1.8 %shard_map.78 = (bf16[512,128]{1,0:T(8,128)(2,1)S(1)}, bf16[512,128]{1,0:T(8,128)(2,1)S(1)}, bf16[512,128]{1,0:T(8,128)(2,1)S(1)}, bf16[512,128]{1,0:T(8,128)(2,1)S(1)}) custom-call(s32[3]{0:T(128)S(1)} %pad_add_fusion.place_ref, bf16[4,512,128]{2,1,0:T(8,128)(2,1)S(1)} %get-tuple-element.202.own, bf16[4,512,128]{2,1,0:T(8,128)(2,1)S(1)} %collective-permute-done.15.over_x, ...), custom_call_target="tpu_custom_call" | custom-call | flops 1000 | bytes 1000 | tf_op jit(solution)/shard_map/pallas_call | solution.py:467
  71.8 2.0 %collective-permute-done.17 = bf16[512,128]{1,0:T(8,128)(2,1)S(1)} collective-permute-done((bf16[512,128]{1,0:T(8,128)(2,1)S(1)}, bf16[512,128]{1,0:T(8,128)(2,1)S(1)}, u32[]{:S(2)}, u32[]{:S(2)}) %collective-permute-start.17) | collective-permute-done | bytes 131104 | tf_op jit(solution)/shard_map/ppermute | solution.py:411
  73.8 4.8 %collective-permute-done.18 = bf16[512,128]{1,0:T(8,128)(2,1)S(1)} collective-permute-done((bf16[512,128]{1,0:T(8,128)(2,1)S(1)}, bf16[512,128]{1,0:T(8,128)(2,1)S(1)}, u32[]{:S(2)}, u32[]{:S(2)}) %collective-permute-start.18) | collective-permute-done | bytes 131104 | tf_op jit(solution)/shard_map/ppermute | solution.py:411
  82.1 2.8 %collective-permute-start.24 = (bf16[512,128]{1,0:T(8,128)(2,1)S(1)}, bf16[512,128]{1,0:T(8,128)(2,1)S(1)}, u32[]{:S(2)}, u32[]{:S(2)}) collective-permute-start(bf16[512,128]{1,0:T(8,128)(2,1)S(1)} %get-tuple-element.164), channel_id=1, source_target_pairs={{0,4},{1,5},{2,6},{3,7},{4,0},{5,1},{6,2},{7,3},{8,12},{9,13},{10,... | collective-permute-start | bytes 393224 | tf_op jit(solution)/shard_map/ppermute | solution.py:411
  84.9 1.9 %shard_map.79 = (bf16[512,128]{1,0:T(8,128)(2,1)S(1)}, bf16[512,128]{1,0:T(8,128)(2,1)S(1)}, bf16[512,128]{1,0:T(8,128)(2,1)S(1)}, bf16[512,128]{1,0:T(8,128)(2,1)S(1)}) custom-call(s32[3]{0:T(128)S(1)} %pad_add_fusion.place_ref, bf16[4,512,128]{2,1,0:T(8,128)(2,1)S(1)} %get-tuple-element.200.own, bf16[4,512,128]{2,1,0:T(8,128)(2,1)S(1)} %collective-permute-done.21.over_x, ...), custom_call_target="tpu_custom_call" | custom-call | flops 1000 | bytes 1000 | tf_op jit(solution)/shard_map/pallas_call | solution.py:467
  86.7 2.0 %collective-permute-done.22.refs_1_ = bf16[512,128]{1,0:T(8,128)(2,1)S(1)} collective-permute-done((bf16[512,128]{1,0:T(8,128)(2,1)S(1)}, bf16[512,128]{1,0:T(8,128)(2,1)S(1)}, u32[]{:S(2)}, u32[]{:S(2)}) %collective-permute-start.22) | collective-permute-done | bytes 131104 | tf_op jit(solution)/shard_map/ppermute | solution.py:411
  88.7 5.0 %collective-permute-done.23.refs_2_ = bf16[512,128]{1,0:T(8,128)(2,1)S(1)} collective-permute-done((bf16[512,128]{1,0:T(8,128)(2,1)S(1)}, bf16[512,128]{1,0:T(8,128)(2,1)S(1)}, u32[]{:S(2)}, u32[]{:S(2)}) %collective-permute-start.23) | collective-permute-done | bytes 131104 | tf_op jit(solution)/shard_map/ppermute | solution.py:411
  94.2 2.1 %collective-permute-start.27 = (bf16[512,128]{1,0:T(8,128)(2,1)S(1)}, bf16[512,128]{1,0:T(8,128)(2,1)S(1)}, u32[]{:S(2)}, u32[]{:S(2)}) collective-permute-start(bf16[512,128]{1,0:T(8,128)(2,1)S(1)} %get-tuple-element.179), channel_id=1, source_target_pairs={{0,12},{1,13},{2,14},{3,15},{4,8},{5,9},{6,10},{7,11},{8,4},{9,5},... | collective-permute-start | bytes 393224 | tf_op jit(solution)/shard_map/ppermute | solution.py:411
  96.3 2.4 %collective-permute-start.29 = (bf16[512,128]{1,0:T(8,128)(2,1)S(1)}, bf16[512,128]{1,0:T(8,128)(2,1)S(1)}, u32[]{:S(2)}, u32[]{:S(2)}) collective-permute-start(bf16[512,128]{1,0:T(8,128)(2,1)S(1)} %get-tuple-element.181), channel_id=1, source_target_pairs={{0,4},{1,5},{2,6},{3,7},{4,0},{5,1},{6,2},{7,3},{8,12},{9,13},{10,... | collective-permute-start | bytes 393224 | tf_op jit(solution)/shard_map/ppermute | solution.py:411
  98.6 1.8 %shard_map.80 = (bf16[512,128]{1,0:T(8,128)(2,1)S(1)}, bf16[512,128]{1,0:T(8,128)(2,1)S(1)}, bf16[512,128]{1,0:T(8,128)(2,1)S(1)}, bf16[512,128]{1,0:T(8,128)(2,1)S(1)}) custom-call(s32[3]{0:T(128)S(1)} %pad_add_fusion.place_ref, bf16[4,512,128]{2,1,0:T(8,128)(2,1)S(1)} %get-tuple-element.198.own, bf16[4,512,128]{2,1,0:T(8,128)(2,1)S(1)} %collective-permute-done.26.over_x, ...), custom_call_target="tpu_custom_call" | custom-call | flops 1000 | bytes 1000 | tf_op jit(solution)/shard_map/pallas_call | solution.py:467
  100.5 2.0 %collective-permute-done.27.refs_5_ = bf16[512,128]{1,0:T(8,128)(2,1)S(1)} collective-permute-done((bf16[512,128]{1,0:T(8,128)(2,1)S(1)}, bf16[512,128]{1,0:T(8,128)(2,1)S(1)}, u32[]{:S(2)}, u32[]{:S(2)}) %collective-permute-start.27) | collective-permute-done | bytes 131104 | tf_op jit(solution)/shard_map/ppermute | solution.py:411
  102.5 5.1 %collective-permute-done.28.refs_6_ = bf16[512,128]{1,0:T(8,128)(2,1)S(1)} collective-permute-done((bf16[512,128]{1,0:T(8,128)(2,1)S(1)}, bf16[512,128]{1,0:T(8,128)(2,1)S(1)}, u32[]{:S(2)}, u32[]{:S(2)}) %collective-permute-start.28) | collective-permute-done | bytes 131104 | tf_op jit(solution)/shard_map/ppermute | solution.py:411
  108.9 2.0 %collective-permute-start.32 = (bf16[512,128]{1,0:T(8,128)(2,1)S(1)}, bf16[512,128]{1,0:T(8,128)(2,1)S(1)}, u32[]{:S(2)}, u32[]{:S(2)}) collective-permute-start(bf16[512,128]{1,0:T(8,128)(2,1)S(1)} %get-tuple-element.194), channel_id=1, source_target_pairs={{0,12},{1,13},{2,14},{3,15},{4,8},{5,9},{6,10},{7,11},{8,4},{9,5},... | collective-permute-start | bytes 393224 | tf_op jit(solution)/shard_map/ppermute | solution.py:411
  110.9 2.4 %collective-permute-start.34 = (bf16[512,128]{1,0:T(8,128)(2,1)S(1)}, bf16[512,128]{1,0:T(8,128)(2,1)S(1)}, u32[]{:S(2)}, u32[]{:S(2)}) collective-permute-start(bf16[512,128]{1,0:T(8,128)(2,1)S(1)} %get-tuple-element.196), channel_id=1, source_target_pairs={{0,4},{1,5},{2,6},{3,7},{4,0},{5,1},{6,2},{7,3},{8,12},{9,13},{10,... | collective-permute-start | bytes 393224 | tf_op jit(solution)/shard_map/ppermute | solution.py:411
  113.3 3.2 %shard_map.81 = (bf16[128,8192]{1,0:T(8,128)(2,1)}, f32[2,128,128]{2,1,0:T(8,128)S(1)}) custom-call(s32[3]{0:T(128)S(1)} %pad_add_fusion.place_ref, s32[64]{0:T(128)S(1)} %copy-done.3, bf16[512,128]{1,0:T(8,128)(2,1)S(1)} %get-tuple-element.174.refs_0_, bf16[512,128]{1,0:T(8,128)(2,1)S(1)} %collective-permute-done.22.refs_1_, ...), custom_call_target="tpu_custom_call" | custom-call | flops 1000 | bytes 1000 | tf_op jit(solution)/shard_map/pallas_call | solution.py:530
  117.2 4.1 %collective-permute-done.33.refs_2_ = bf16[512,128]{1,0:T(8,128)(2,1)S(1)} collective-permute-done((bf16[512,128]{1,0:T(8,128)(2,1)S(1)}, bf16[512,128]{1,0:T(8,128)(2,1)S(1)}, u32[]{:S(2)}, u32[]{:S(2)}) %collective-permute-start.33) | collective-permute-done | bytes 131104 | tf_op jit(solution)/shard_map/ppermute | solution.py:411
  121.5 2.5 %shard_map.82 = bf16[128,8192]{1,0:T(8,128)(2,1)} custom-call(s32[3]{0:T(128)S(1)} %pad_add_fusion.place_ref, s32[64]{0:T(128)S(1)} %copy-done.3, bf16[128,8192]{1,0:T(8,128)(2,1)} %get-tuple-element.191.done_hbm, f32[2,128,128]{2,1,0:T(8,128)S(1)} %get-tuple-element.192.seam_ref, ...), custom_call_target="tpu_custom_call", output_to_operand_aliasing={{}: (2, {})} | custom-call | flops 1000 | bytes 1000 | tf_op jit(solution)/shard_map/pallas_call | solution.py:542
  (80 shorter events, 27.0 us)
Async XLA Ops:
  4.5 7.5 %collective-permute-start.2 = (bf16[128,512]{1,0:T(8,128)(2,1)S(1)}, bf16[128,512]{1,0:T(8,128)(2,1)S(1)}, u32[]{:S(2)}, u32[]{:S(2)}) collective-permute-start(bf16[128,512]{1,0:T(8,128)(2,1)S(1)} %get-tuple-element.111), channel_id=1, source_target_pairs={{0,1},{1,0},{2,3},{3,2},{4,5},{5,4},{6,7},{7,6},{8,9},{9,8},{10,11... | collective-permute-start | bytes 393224 | tf_op jit(solution)/shard_map/ppermute | solution.py:411
  5.0 7.0 %collective-permute-start.3 = (bf16[128,512]{1,0:T(8,128)(2,1)S(1)}, bf16[128,512]{1,0:T(8,128)(2,1)S(1)}, u32[]{:S(2)}, u32[]{:S(2)}) collective-permute-start(bf16[128,512]{1,0:T(8,128)(2,1)S(1)} %get-tuple-element.112), channel_id=1, source_target_pairs={{0,2},{1,3},{2,0},{3,1},{4,6},{5,7},{6,4},{7,5},{8,10},{9,11},{10,... | collective-permute-start | bytes 393224 | tf_op jit(solution)/shard_map/ppermute | solution.py:411
  7.5 6.6 %collective-permute-start.4 = (bf16[128,512]{1,0:T(8,128)(2,1)S(1)}, bf16[128,512]{1,0:T(8,128)(2,1)S(1)}, u32[]{:S(2)}, u32[]{:S(2)}) collective-permute-start(bf16[128,512]{1,0:T(8,128)(2,1)S(1)} %get-tuple-element.113), channel_id=1, source_target_pairs={{0,3},{1,2},{2,1},{3,0},{4,7},{5,6},{6,5},{7,4},{8,11},{9,10},{10,... | collective-permute-start | bytes 393224 | tf_op jit(solution)/shard_map/ppermute | solution.py:411
  14.3 14.0 %collective-permute-start.5 = (bf16[512,256]{1,0:T(8,128)(2,1)S(1)}, bf16[512,256]{1,0:T(8,128)(2,1)S(1)}, u32[]{:S(2)}, u32[]{:S(2)}) collective-permute-start(bf16[512,256]{1,0:T(8,128)(2,1)S(1)} %slice.21), channel_id=1, source_target_pairs={{0,4},{1,5},{2,6},{3,7},{4,0},{5,1},{6,2},{7,3},{8,12},{9,13},{10,... | collective-permute-start | bytes 786440 | tf_op jit(solution)/shard_map/ppermute | solution.py:411
  16.0 14.8 %collective-permute-start.6 = (bf16[512,256]{1,0:T(8,128)(2,1)S(1)}, bf16[512,256]{1,0:T(8,128)(2,1)S(1)}, u32[]{:S(2)}, u32[]{:S(2)}) collective-permute-start(bf16[512,256]{1,0:T(8,128)(2,1)S(1)} %slice.21), channel_id=1, source_target_pairs={{0,8},{1,9},{2,10},{3,11},{4,12},{5,13},{6,14},{7,15},{8,0},{9,1},... | collective-permute-start | bytes 786440 | tf_op jit(solution)/shard_map/ppermute | solution.py:411
  22.6 5.6 %collective-permute-start.1 = (bf16[2,128,128]{2,1,0:T(8,128)(2,1)S(1)}, bf16[2,128,128]{2,1,0:T(8,128)(2,1)S(1)}, u32[]{:S(2)}, u32[]{:S(2)}) collective-permute-start(bf16[2,128,128]{2,1,0:T(8,128)(2,1)S(1)} %get-tuple-element.105), channel_id=1, source_target_pairs={{0,16},{16,0},{1,17},{17,1},{2,18},{18,2},{3,19},{19,3},{4,20},{20... | collective-permute-start | bytes 196616 | tf_op jit(solution)/shard_map/ppermute | solution.py:417
  30.8 13.6 %collective-permute-start.10 = (bf16[2048,128]{1,0:T(8,128)(2,1)S(1)}, bf16[2048,128]{1,0:T(8,128)(2,1)S(1)}, u32[]{:S(2)}, u32[]{:S(2)}) collective-permute-start(bf16[2048,128]{1,0:T(8,128)(2,1)S(1)} %get-tuple-element.124), channel_id=1, source_target_pairs={{0,16},{16,0},{1,17},{17,1},{2,18},{18,2},{3,19},{19,3},{4,20},{20... | collective-permute-start | bytes 1572872 | tf_op jit(solution)/shard_map/ppermute | solution.py:417
  32.4 14.9 %collective-permute-start.9 = (bf16[1536,128]{1,0:T(8,128)(2,1)S(1)}, bf16[1536,128]{1,0:T(8,128)(2,1)S(1)}, u32[]{:S(2)}, u32[]{:S(2)}) collective-permute-start(bf16[1536,128]{1,0:T(8,128)(2,1)S(1)} %pad_maximum_fusion.8), channel_id=1, source_target_pairs={{0,4},{1,5},{2,6},{3,7},{4,0},{5,1},{6,2},{7,3},{8,12},{9,13},{10,... | collective-permute-start | bytes 1179656 | tf_op jit(solution)/shard_map/ppermute | solution.py:411
  32.9 14.4 %collective-permute-start.11 = (bf16[512,256]{1,0:T(8,128)(2,1)S(1)}, bf16[512,256]{1,0:T(8,128)(2,1)S(1)}, u32[]{:S(2)}, u32[]{:S(2)}) collective-permute-start(bf16[512,256]{1,0:T(8,128)(2,1)S(1)} %collective-permute-done.5.near), channel_id=1, source_target_pairs={{0,16},{16,0},{1,17},{17,1},{2,18},{18,2},{3,19},{19,3},{4,20},{20... | collective-permute-start | bytes 786440 | tf_op jit(solution)/shard_map/ppermute | solution.py:417
  33.4 13.9 %collective-permute-start.7 = (bf16[512,128]{1,0:T(8,128)(2,1)S(1)}, bf16[512,128]{1,0:T(8,128)(2,1)S(1)}, u32[]{:S(2)}, u32[]{:S(2)}) collective-permute-start(bf16[512,128]{1,0:T(8,128)(2,1)S(1)} %get-tuple-element.119), channel_id=1, source_target_pairs={{0,12},{1,13},{2,14},{3,15},{4,8},{5,9},{6,10},{7,11},{8,4},{9,5},... | collective-permute-start | bytes 393224 | tf_op jit(solution)/shard_map/ppermute | solution.py:411
  35.5 11.8 %collective-permute-start.8 = (bf16[512,128]{1,0:T(8,128)(2,1)S(1)}, bf16[512,128]{1,0:T(8,128)(2,1)S(1)}, u32[]{:S(2)}, u32[]{:S(2)}) collective-permute-start(bf16[512,128]{1,0:T(8,128)(2,1)S(1)} %get-tuple-element.120), channel_id=1, source_target_pairs={{0,8},{1,9},{2,10},{3,11},{4,12},{5,13},{6,14},{7,15},{8,0},{9,1},... | collective-permute-start | bytes 393224 | tf_op jit(solution)/shard_map/ppermute | solution.py:411
  47.5 17.2 %collective-permute-start.15 = (bf16[4,512,128]{2,1,0:T(8,128)(2,1)S(1)}, bf16[4,512,128]{2,1,0:T(8,128)(2,1)S(1)}, u32[]{:S(2)}, u32[]{:S(2)}) collective-permute-start(bf16[4,512,128]{2,1,0:T(8,128)(2,1)S(1)} %get-tuple-element.202.own), channel_id=1, source_target_pairs={{0,2},{1,3},{2,0},{3,1},{4,6},{5,7},{6,4},{7,5},{8,10},{9,11},{10,... | collective-permute-start | bytes 1572872 | tf_op jit(solution)/shard_map/ppermute | solution.py:411
  49.1 15.5 %collective-permute-start.16 = (bf16[2048,128]{1,0:T(8,128)(2,1)S(1)}, bf16[2048,128]{1,0:T(8,128)(2,1)S(1)}, u32[]{:S(2)}, u32[]{:S(2)}) collective-permute-start(bf16[2048,128]{1,0:T(8,128)(2,1)S(1)} %pad_maximum_fusion.4), channel_id=1, source_target_pairs={{0,16},{16,0},{1,17},{17,1},{2,18},{18,2},{3,19},{19,3},{4,20},{20... | collective-permute-start | bytes 1572872 | tf_op jit(solution)/shard_map/ppermute | solution.py:417
  51.3 7.8 %collective-permute-start.12 = (bf16[512,128]{1,0:T(8,128)(2,1)S(1)}, bf16[512,128]{1,0:T(8,128)(2,1)S(1)}, u32[]{:S(2)}, u32[]{:S(2)}) collective-permute-start(bf16[512,128]{1,0:T(8,128)(2,1)S(1)} %get-tuple-element.132), channel_id=1, source_target_pairs={{0,12},{1,13},{2,14},{3,15},{4,8},{5,9},{6,10},{7,11},{8,4},{9,5},... | collective-permute-start | bytes 393224 | tf_op jit(solution)/shard_map/ppermute | solution.py:411
  55.2 9.4 %collective-permute-start.13 = (bf16[512,128]{1,0:T(8,128)(2,1)S(1)}, bf16[512,128]{1,0:T(8,128)(2,1)S(1)}, u32[]{:S(2)}, u32[]{:S(2)}) collective-permute-start(bf16[512,128]{1,0:T(8,128)(2,1)S(1)} %get-tuple-element.133), channel_id=1, source_target_pairs={{0,8},{1,9},{2,10},{3,11},{4,12},{5,13},{6,14},{7,15},{8,0},{9,1},... | collective-permute-start | bytes 393224 | tf_op jit(solution)/shard_map/ppermute | solution.py:411
  55.2 9.4 %collective-permute-start.14 = (bf16[512,128]{1,0:T(8,128)(2,1)S(1)}, bf16[512,128]{1,0:T(8,128)(2,1)S(1)}, u32[]{:S(2)}, u32[]{:S(2)}) collective-permute-start(bf16[512,128]{1,0:T(8,128)(2,1)S(1)} %get-tuple-element.134), channel_id=1, source_target_pairs={{0,4},{1,5},{2,6},{3,7},{4,0},{5,1},{6,2},{7,3},{8,12},{9,13},{10,... | collective-permute-start | bytes 393224 | tf_op jit(solution)/shard_map/ppermute | solution.py:411
  65.0 14.4 %collective-permute-start.21 = (bf16[4,512,128]{2,1,0:T(8,128)(2,1)S(1)}, bf16[4,512,128]{2,1,0:T(8,128)(2,1)S(1)}, u32[]{:S(2)}, u32[]{:S(2)}) collective-permute-start(bf16[4,512,128]{2,1,0:T(8,128)(2,1)S(1)} %get-tuple-element.200.own), channel_id=1, source_target_pairs={{0,2},{1,3},{2,0},{3,1},{4,6},{5,7},{6,4},{7,5},{8,10},{9,11},{10,... | collective-permute-start | bytes 1572872 | tf_op jit(solution)/shard_map/ppermute | solution.py:411
  65.6 8.3 %collective-permute-start.17 = (bf16[512,128]{1,0:T(8,128)(2,1)S(1)}, bf16[512,128]{1,0:T(8,128)(2,1)S(1)}, u32[]{:S(2)}, u32[]{:S(2)}) collective-permute-start(bf16[512,128]{1,0:T(8,128)(2,1)S(1)} %get-tuple-element.147), channel_id=1, source_target_pairs={{0,12},{1,13},{2,14},{3,15},{4,8},{5,9},{6,10},{7,11},{8,4},{9,5},... | collective-permute-start | bytes 393224 | tf_op jit(solution)/shard_map/ppermute | solution.py:411
  67.1 11.5 %collective-permute-start.18 = (bf16[512,128]{1,0:T(8,128)(2,1)S(1)}, bf16[512,128]{1,0:T(8,128)(2,1)S(1)}, u32[]{:S(2)}, u32[]{:S(2)}) collective-permute-start(bf16[512,128]{1,0:T(8,128)(2,1)S(1)} %get-tuple-element.148), channel_id=1, source_target_pairs={{0,8},{1,9},{2,10},{3,11},{4,12},{5,13},{6,14},{7,15},{8,0},{9,1},... | collective-permute-start | bytes 393224 | tf_op jit(solution)/shard_map/ppermute | solution.py:411
  67.1 11.5 %collective-permute-start.19 = (bf16[512,128]{1,0:T(8,128)(2,1)S(1)}, bf16[512,128]{1,0:T(8,128)(2,1)S(1)}, u32[]{:S(2)}, u32[]{:S(2)}) collective-permute-start(bf16[512,128]{1,0:T(8,128)(2,1)S(1)} %get-tuple-element.149), channel_id=1, source_target_pairs={{0,4},{1,5},{2,6},{3,7},{4,0},{5,1},{6,2},{7,3},{8,12},{9,13},{10,... | collective-permute-start | bytes 393224 | tf_op jit(solution)/shard_map/ppermute | solution.py:411
  79.4 5.4 %collective-permute-start.25 = (bf16[2,4,512,128]{3,2,1,0:T(8,128)(2,1)S(1)}, bf16[2,4,512,128]{3,2,1,0:T(8,128)(2,1)S(1)}, u32[]{:S(2)}, u32[]{:S(2)}) collective-permute-start(bf16[2,4,512,128]{3,2,1,0:T(8,128)(2,1)S(1)} %pad_maximum_fusion.1), channel_id=1, source_target_pairs={{0,1},{1,0},{2,3},{3,2},{4,5},{5,4},{6,7},{7,6},{8,9},{9,8},{10,11... | collective-permute-start | bytes 3145736 | tf_op jit(solution)/shard_map/ppermute | solution.py:411
  79.6 14.4 %collective-permute-start.26 = (bf16[4,512,128]{2,1,0:T(8,128)(2,1)S(1)}, bf16[4,512,128]{2,1,0:T(8,128)(2,1)S(1)}, u32[]{:S(2)}, u32[]{:S(2)}) collective-permute-start(bf16[4,512,128]{2,1,0:T(8,128)(2,1)S(1)} %get-tuple-element.198.own), channel_id=1, source_target_pairs={{0,2},{1,3},{2,0},{3,1},{4,6},{5,7},{6,4},{7,5},{8,10},{9,11},{10,... | collective-permute-start | bytes 1572872 | tf_op jit(solution)/shard_map/ppermute | solution.py:411
  80.5 8.3 %collective-permute-start.22 = (bf16[512,128]{1,0:T(8,128)(2,1)S(1)}, bf16[512,128]{1,0:T(8,128)(2,1)S(1)}, u32[]{:S(2)}, u32[]{:S(2)}) collective-permute-start(bf16[512,128]{1,0:T(8,128)(2,1)S(1)} %get-tuple-element.162), channel_id=1, source_target_pairs={{0,12},{1,13},{2,14},{3,15},{4,8},{5,9},{6,10},{7,11},{8,4},{9,5},... | collective-permute-start | bytes 393224 | tf_op jit(solution)/shard_map/ppermute | solution.py:411
  82.1 11.7 %collective-permute-start.23 = (bf16[512,128]{1,0:T(8,128)(2,1)S(1)}, bf16[512,128]{1,0:T(8,128)(2,1)S(1)}, u32[]{:S(2)}, u32[]{:S(2)}) collective-permute-start(bf16[512,128]{1,0:T(8,128)(2,1)S(1)} %get-tuple-element.163), channel_id=1, source_target_pairs={{0,8},{1,9},{2,10},{3,11},{4,12},{5,13},{6,14},{7,15},{8,0},{9,1},... | collective-permute-start | bytes 393224 | tf_op jit(solution)/shard_map/ppermute | solution.py:411
  82.1 11.7 %collective-permute-start.24 = (bf16[512,128]{1,0:T(8,128)(2,1)S(1)}, bf16[512,128]{1,0:T(8,128)(2,1)S(1)}, u32[]{:S(2)}, u32[]{:S(2)}) collective-permute-start(bf16[512,128]{1,0:T(8,128)(2,1)S(1)} %get-tuple-element.164), channel_id=1, source_target_pairs={{0,4},{1,5},{2,6},{3,7},{4,0},{5,1},{6,2},{7,3},{8,12},{9,13},{10,... | collective-permute-start | bytes 393224 | tf_op jit(solution)/shard_map/ppermute | solution.py:411
  94.2 8.3 %collective-permute-start.27 = (bf16[512,128]{1,0:T(8,128)(2,1)S(1)}, bf16[512,128]{1,0:T(8,128)(2,1)S(1)}, u32[]{:S(2)}, u32[]{:S(2)}) collective-permute-start(bf16[512,128]{1,0:T(8,128)(2,1)S(1)} %get-tuple-element.179), channel_id=1, source_target_pairs={{0,12},{1,13},{2,14},{3,15},{4,8},{5,9},{6,10},{7,11},{8,4},{9,5},... | collective-permute-start | bytes 393224 | tf_op jit(solution)/shard_map/ppermute | solution.py:411
  96.3 11.3 %collective-permute-start.28 = (bf16[512,128]{1,0:T(8,128)(2,1)S(1)}, bf16[512,128]{1,0:T(8,128)(2,1)S(1)}, u32[]{:S(2)}, u32[]{:S(2)}) collective-permute-start(bf16[512,128]{1,0:T(8,128)(2,1)S(1)} %get-tuple-element.180), channel_id=1, source_target_pairs={{0,8},{1,9},{2,10},{3,11},{4,12},{5,13},{6,14},{7,15},{8,0},{9,1},... | collective-permute-start | bytes 393224 | tf_op jit(solution)/shard_map/ppermute | solution.py:411
  96.3 11.3 %collective-permute-start.29 = (bf16[512,128]{1,0:T(8,128)(2,1)S(1)}, bf16[512,128]{1,0:T(8,128)(2,1)S(1)}, u32[]{:S(2)}, u32[]{:S(2)}) collective-permute-start(bf16[512,128]{1,0:T(8,128)(2,1)S(1)} %get-tuple-element.181), channel_id=1, source_target_pairs={{0,4},{1,5},{2,6},{3,7},{4,0},{5,1},{6,2},{7,3},{8,12},{9,13},{10,... | collective-permute-start | bytes 393224 | tf_op jit(solution)/shard_map/ppermute | solution.py:411
  107.6 13.9 %collective-permute-start.31 = (bf16[2048,128]{1,0:T(8,128)(2,1)S(1)}, bf16[2048,128]{1,0:T(8,128)(2,1)S(1)}, u32[]{:S(2)}, u32[]{:S(2)}) collective-permute-start(bf16[2048,128]{1,0:T(8,128)(2,1)S(1)} %pad_maximum_fusion.7), channel_id=1, source_target_pairs={{0,16},{16,0},{1,17},{17,1},{2,18},{18,2},{3,19},{19,3},{4,20},{20... | collective-permute-start | bytes 1572872 | tf_op jit(solution)/shard_map/ppermute | solution.py:417
  108.9 8.3 %collective-permute-start.32 = (bf16[512,128]{1,0:T(8,128)(2,1)S(1)}, bf16[512,128]{1,0:T(8,128)(2,1)S(1)}, u32[]{:S(2)}, u32[]{:S(2)}) collective-permute-start(bf16[512,128]{1,0:T(8,128)(2,1)S(1)} %get-tuple-element.194), channel_id=1, source_target_pairs={{0,12},{1,13},{2,14},{3,15},{4,8},{5,9},{6,10},{7,11},{8,4},{9,5},... | collective-permute-start | bytes 393224 | tf_op jit(solution)/shard_map/ppermute | solution.py:411
  110.9 10.4 %collective-permute-start.33 = (bf16[512,128]{1,0:T(8,128)(2,1)S(1)}, bf16[512,128]{1,0:T(8,128)(2,1)S(1)}, u32[]{:S(2)}, u32[]{:S(2)}) collective-permute-start(bf16[512,128]{1,0:T(8,128)(2,1)S(1)} %get-tuple-element.195), channel_id=1, source_target_pairs={{0,8},{1,9},{2,10},{3,11},{4,12},{5,13},{6,14},{7,15},{8,0},{9,1},... | collective-permute-start | bytes 393224 | tf_op jit(solution)/shard_map/ppermute | solution.py:411
  110.9 10.4 %collective-permute-start.34 = (bf16[512,128]{1,0:T(8,128)(2,1)S(1)}, bf16[512,128]{1,0:T(8,128)(2,1)S(1)}, u32[]{:S(2)}, u32[]{:S(2)}) collective-permute-start(bf16[512,128]{1,0:T(8,128)(2,1)S(1)} %get-tuple-element.196), channel_id=1, source_target_pairs={{0,4},{1,5},{2,6},{3,7},{4,0},{5,1},{6,2},{7,3},{8,12},{9,13},{10,... | collective-permute-start | bytes 393224 | tf_op jit(solution)/shard_map/ppermute | solution.py:411
  (10 other events, 96.0 us)
